TPU v7x, 128 devices: a whole 4x4x4 slice. The times are simulated.
128 devices in a mesh: tile: 64 (over y, x_hi, z, core), comp: 2 (over x_lo).
Axes of the slice: x: 4 (x_hi: 2, x_lo: 2; x = x_hi * 2 + x_lo), y: 4, z: 4, core: 2. Of those that a mesh axis runs over, the one named last changes fastest.
Arguments:
- atm_state: bfloat16 [256, 1024, 256], P('comp', 'tile')
- ocean_state: bfloat16 [256, 32768], P('comp', 'tile')
- ocean_count: int32 [64], P('tile'), may hold values from 1 to 4, as said below
- regrid_src: int32 [2048, 2], P('tile'), may hold values from 0 to 255, as said below
- regrid_w: bfloat16 [2048, 2, 128, 128], P('tile'), may hold values from -0.375 to 0.375
- dw_kernel: float32 [9, 256], P(None, 'comp'), may hold values from -2.5 to 2.5
- atm_gain: bfloat16 [256], P('comp'), may hold values from 0.099609375 to 1.8984375
- atm_up: bfloat16 [256, 1024], P(None, 'comp'), may hold values from -0.375 to 0.375
- atm_down: bfloat16 [1024, 256], P('comp'), may hold values from -0.1875 to 0.1875
- ocean_gain: bfloat16 [256], P('comp'), may hold values from 0.099609375 to 1.8984375
- ocean_up: bfloat16 [256, 1024], P(None, 'comp'), may hold values from -0.375 to 0.375
- ocean_down: bfloat16 [1024, 256], P('comp'), may hold values from -0.1875 to 0.1875
Outputs:
- atm_out: bfloat16 [256, 1024, 256], P('comp', 'tile')
- ocean_result: bfloat16 [256, 32768], P('comp', 'tile')
Inputs may be any that keep to these rules, and one draw needn't show every extreme that they name: Tile slots s < ocean_count[t] of tile index t hold ocean, the rest land; some entry equals 4. `regrid_src`: every entry names a live ocean slot g, whose tile index g // 4 differs by at most 2 from the tile index r // 32 of its block r.
All inputs are finite; a program needn't handle non-finite values.
Results may differ from a plain program's by a relative error of at most 0.012.
Values may be sent and summed in bfloat16 or wider, within the bound.
No kernel may reach another device: no remote copies, remote signals or barrier semaphores. Data moves between devices by JAX's collectives and lax.ppermute only.
A program may use at most 64 MiB of HBM per device.

v0:
```python
import jax
import jax.numpy as jnp
from jax import lax
from jax.sharding import PartitionSpec as P

CHANNEL_COUNT = 256
CELLS_PER_TILE = 128
REACH = 2


def padded_2(shard, sides, width):
    for axis, dim in sides:
        size, length = (lax.axis_size(axis), shard.shape[dim])
        up = [(i, (i + 1) % size) for i in range(size - 1)]
        down = [(j, i) for i, j in up]
        last = lax.slice_in_dim(shard, length - width, length, axis=dim)
        first = lax.slice_in_dim(shard, 0, width, axis=dim)
        before = lax.ppermute(last, axis, up)
        after = lax.ppermute(first, axis, down)
        shard = jnp.concatenate([before, shard, after], axis=dim)
    return shard


def shifted(block, axis, distance):
    devices = range(lax.axis_size(axis))
    route = [(i - distance, i) for i in devices if i - distance in devices]
    return lax.ppermute(block, axis, route)


def expand(weight, values):
    return jnp.dot(weight.T, values, preferred_element_type=jnp.float32)


def normalize(values, total, squares, gain):
    center = total / CHANNEL_COUNT
    spread = squares / CHANNEL_COUNT - center * center
    scaled = (values - center) * lax.rsqrt(spread + 1e-06) * gain.astype(jnp.float32)[:, None]
    return scaled.astype(jnp.bfloat16)


def on_device(
    atm_state,
    ocean_state,
    ocean_count,
    regrid_src,
    regrid_w,
    dw_kernel,
    atm_gain,
    atm_up,
    atm_down,
    ocean_gain,
    ocean_up,
    ocean_down,
):
    channels, height, breadth = atm_state.shape
    padded = padded_2(atm_state, (("tile", 1),), 1).astype(jnp.float32)
    conv = jnp.zeros((channels, height, breadth), jnp.float32)
    for lift in range(3):
        for turn in (-1, 0, 1):
            conv = conv + dw_kernel[lift * 3 + turn + 1][:, None, None] * jnp.roll(
                padded[:, lift : lift + height, :], -turn, axis=2
            )
    atm_conv = conv.reshape(channels, height * breadth)
    atm_cells = atm_conv.shape[1]
    ocean_cells = ocean_state.shape[1]
    ocean_input = ocean_state.astype(jnp.float32)
    totals = lax.psum(
        (
            jnp.sum(atm_conv, 0),
            jnp.sum(atm_conv * atm_conv, 0),
            jnp.sum(ocean_input, 0),
            jnp.sum(ocean_input * ocean_input, 0),
        ),
        "comp",
    )
    normed_atm = normalize(atm_conv, totals[0], totals[1], atm_gain)
    normed_ocean = normalize(ocean_input, totals[2], totals[3], ocean_gain)
    before_atm = expand(atm_up, lax.all_gather(normed_atm, "comp", axis=0, tiled=True))
    before_ocean = expand(ocean_up, lax.all_gather(normed_ocean, "comp", axis=0, tiled=True))
    hidden_atm = jax.nn.gelu(before_atm).astype(jnp.bfloat16)
    hidden_ocean = jax.nn.gelu(before_ocean).astype(jnp.bfloat16)
    summed = lax.psum_scatter(
        jnp.concatenate(
            [expand(atm_down, hidden_atm), expand(ocean_down, hidden_ocean)], axis=1
        ).astype(jnp.bfloat16),
        "comp",
        scatter_dimension=0,
        tiled=True,
    ).astype(jnp.float32)
    delta_atm = summed[:, :atm_cells]
    delta_ocean = summed[:, atm_cells:]
    live = jnp.arange(ocean_cells, dtype=jnp.int32) // CELLS_PER_TILE < ocean_count[0]
    ocean_result = jnp.where(live[None, :], ocean_input + delta_ocean, 0.0).astype(jnp.bfloat16)
    blocks = regrid_src.shape[0]
    members = regrid_src.shape[1]
    wanted = (
        regrid_src[:, :, None] * CELLS_PER_TILE
        + jnp.arange(CELLS_PER_TILE, dtype=jnp.int32)[None, None, :]
    )

    def collect(carry, piece, start):
        length = piece.shape[1]
        local = wanted - start
        inside = (local >= 0) & (local < length)
        taken = jnp.take(piece, jnp.clip(local, 0, length - 1).reshape(-1), axis=1).reshape(
            channels, blocks, members, CELLS_PER_TILE
        )
        return jnp.where(inside[None], taken, carry)

    empty = jnp.zeros((channels, blocks, members, CELLS_PER_TILE), jnp.bfloat16)
    position = lax.axis_index("tile")
    extent = ocean_result.shape[1]
    slabs = collect(empty, ocean_result, position * extent)
    for offset in range(-REACH, REACH + 1):
        if offset != 0:
            nearby = shifted(ocean_result, "tile", offset)
            slabs = collect(slabs, nearby, (position - offset) * extent)
    regrid = jnp.einsum(
        "bkpq,cbkq->cbp", regrid_w, slabs, preferred_element_type=jnp.float32
    ).reshape(channels, height, breadth)
    atm_out = (
        atm_state.astype(jnp.float32) + delta_atm.reshape(channels, height, breadth) + regrid
    ).astype(jnp.bfloat16)
    return (atm_out, ocean_result)


def solution(mesh):
    return jax.shard_map(
        on_device,
        mesh=mesh,
        in_specs=(
            P("comp", "tile", None),
            P("comp", "tile"),
            P("tile"),
            P("tile", None),
            P("tile", None, None, None),
            P(None, "comp"),
            P("comp"),
            P(None, "comp"),
            P("comp", None),
            P("comp"),
            P(None, "comp"),
            P("comp", None),
        ),
        out_specs=(P("comp", "tile", None), P("comp", "tile")),
        check_vma=False,
    )
```

profile of v0, /device:TPU:24, one launch (start us, length us, event | category | flops | bytes accessed | tf_op | source)
XLA Modules:
  0.0 399.3 jit_solution(13746351651867649240)
XLA Ops:
  7.2 1.5 fusion.80
  8.8 1.9 collective-permute-start
  10.7 8.2 %collective-permute-start.1 = (bf16[128,1,256]{2,1,0:T(2,128)(2,1)S(1)}, bf16[128,1,256]{2,1,0:T(2,128)(2,1)S(1)}, u32[]{:S(2)}, u32[]{:S(2)}) collective-permute-start(bf16[128,1,256]{2,1,0:T(2,128)(2,1)S(1)} %get-tuple-element.29), channel_id=1, source_target_pairs={{2,0},{4,2},{6,4},{8,6},{10,8},{12,10},{14,12},{16,14},{18,16},{20... | collective-permute-start | bytes 196616 | tf_op jit(solution)/shard_map/ppermute | solution.py:19
  18.9 1.0 slice_bitcast_fusion.8
  19.9 1.0 copy.24
  20.9 0.7 convert_element_type.39
  21.7 3.7 maximum_convert_fusion
  25.4 12.4 %fusion.79 = (f32[128,16,255]{2,1,0:T(8,128)}, f32[128,16,255]{2,1,0:T(8,128)}, f32[128,16,255]{2,1,0:T(8,128)}, f32[128,16,255]{2,1,0:T(8,128)}, f32[128,16,255]{2,1,0:T(8,128)}, /*index=5*/f32[128,16,255]{2,1,0:T(8,128)}) fusion(f32[128,18,256]{2,1,0:T(8,128)} %maximum_convert_fusion), kind=kLoop, calls=%fused_computation.145 | loop fusion | bytes 25067520 | tf_op jit(solution)/shard_map/jit(_roll_static)/slice | solution.py:60
  37.9 4.8 %fusion.78 = (f32[128,16,1]{2,1,0:T(8,128)S(1)}, f32[128,16,1]{2,1,0:T(8,128)S(1)}, f32[128,16,1]{2,1,0:T(8,128)S(1)}, f32[128,16,1]{2,1,0:T(8,128)S(1)}, f32[12...) fusion(f32[128,18,256]{2,1,0:T(8,128)} %maximum_convert_fusion), kind=kLoop, calls=%fused_computation.144 | loop fusion | bytes 98304 | tf_op jit(solution)/shard_map/jit(_roll_static)/slice | solution.py:60
  43.0 0.6 copy-done.5
  44.8 6.2 %fusion.76 = (f32[16,256]{1,0:T(8,128)S(1)}, f32[16,256]{1,0:T(8,128)S(1)}, f32[128,16,256]{2,1,0:T(8,128)S(1)}) fusion(f32[128,16,1]{2,1,0:T(8,128)S(1)} %get-tuple-element.19, f32[128,16,255]{2,1,0:T(8,128)} %get-tuple-element.27, f32[128]{0:T(128)S(1)} %get-tuple-element.49, f32[128,18,256]{2,1,0:T(8,128)S(1)} %copy-done.1, ...), kind=kLoop, calls=%fused_computation.143 | loop fusion | flops 13623296 | bytes 21008896 | tf_op jit(solution)/shard_map/reduce_sum | solution.py:69
  51.0 3.0 copy.37
  54.0 8.5 %all-reduce = (f32[512]{0:T(512)S(1)}, f32[512]{0:T(512)S(1)}, f32[4096]{0:T(1024)S(1)}, f32[4096]{0:T(1024)S(1)}) all-reduce(f32[512]{0:T(512)S(1)} %get-tuple-element.10, f32[512]{0:T(512)S(1)} %get-tuple-element.9, f32[4096]{0:T(1024)S(1)} %bitcast.99, f32[4096]{0:T(1024)S(1)} %bitcast.98), channel_id=1, replica_groups=mesh['tile'=64,'comp'=2] {'comp'}, use_global_device_ids=true, to_apply=%region_7.8 | all-reduce | flops 9216 | bytes 73728 | tf_op jit(solution)/shard_map/psum | solution.py:67
  62.5 2.9 multiply_convert_fusion
  65.8 5.8 %all_gather.7 = bf16[256,512]{0,1:T(8,128)(2,1)S(1)} all-gather(bf16[128,512]{0,1:T(8,128)(2,1)S(1)} %fusion.44), channel_id=1, replica_groups=mesh['tile'=64,'comp'=2] {'comp'}, dimensions={0}, use_global_device_ids=true | all-gather | bytes 393216 | tf_op jit(solution)/shard_map/all_gather | solution.py:79
  72.2 29.1 %all-gather.2.cloned.1.call-done = bf16[256,4096]{1,0:T(8,128)(2,1)} async-done(((bf16[128,4096]{1,0:T(8,128)(2,1)}), bf16[256,4096]{1,0:T(8,128)(2,1)}) %all-gather.2.cloned.1.call-update) | async-done | bytes 2097168 | tf_op jit(solution)/shard_map/all_gather | solution.py:78
  101.3 6.2 %fusion.8 = bf16[256,4096]{0,1:T(8,128)(2,1)} fusion(bf16[512,256]{1,0:T(8,128)(2,1)} %param.22, bf16[256,4096]{1,0:T(8,128)(2,1)} %all-gather.2.cloned.1.call-done, bf16[256,512]{1,0:T(8,128)(2,1)} %param.21), kind=kOutput, calls=%fused_computation.15 | convolution fusion | flops 2167406592 | bytes 4718592 | tf_op jit(solution)/shard_map/dot_general | solution.py:31
  107.5 3.2 pad_maximum_fusion
  110.7 4.3 %copy.35 = bf16[256,4608]{1,0:T(8,128)(2,1)} copy(bf16[256,4608]{0,1:T(8,128)(2,1)} %pad_maximum_fusion) | data formatting | bytes 4718592
  119.2 0.9 compare_and_fusion.4
  120.0 33.4 %reduce-scatter.4.cloned.1.call-done = bf16[128,4608]{1,0:T(8,128)(2,1)} async-done(((bf16[256,4608]{1,0:T(8,128)(2,1)}), bf16[128,4608]{1,0:T(8,128)(2,1)}) %reduce-scatter.4.cloned.1.call-update) | async-done | bytes 1179664
  153.4 1.7 copy.36
  155.1 1.0 copy-done.2
  157.0 7.2 %collective-permute-start.5 = (bf16[128,512]{0,1:T(8,128)(2,1)S(1)}, bf16[128,512]{0,1:T(8,128)(2,1)S(1)}, u32[]{:S(2)}, u32[]{:S(2)}) collective-permute-start(bf16[128,512]{0,1:T(8,128)(2,1)S(1)} %fusion.47), channel_id=1, source_target_pairs={{4,0},{6,2},{8,4},{10,6},{12,8},{14,10},{16,12},{18,14},{20,16},{2... | collective-permute-start | bytes 393224 | tf_op jit(solution)/shard_map/ppermute | solution.py:27
  164.2 1.9 collective-permute-start.4
  166.1 2.4 collective-permute-start.3
  168.6 2.8 collective-permute-start.2
  171.4 31.9 %gather_fusion.4 = bf16[8192,128]{1,0:T(8,128)(2,1)} fusion(bf16[128,512]{0,1:T(8,128)(2,1)S(1)} %fusion.47, s32[8192]{0:T(1024)} %fusion.62), kind=kCustom, calls=%fused_computation.4.clone | custom fusion | bytes 4227072 | tf_op jit(solution)/shard_map/jit(_take)/gather | solution.py:105
  203.3 6.7 %broadcast_select_fusion = bf16[8192,128]{1,0:T(8,128)(2,1)} fusion(bf16[8192,128]{1,0:T(8,128)(2,1)} %gather_fusion.4, pred[8192]{0:T(1024)(128)(4,1)S(1)} %copy-done.11), kind=kLoop, calls=%fused_computation.43 | loop fusion | flops 1048576 | bytes 4202496 | tf_op jit(solution)/shard_map/jit(_take)/select_n | solution.py:105
  209.9 1.5 slice.159
  211.4 0.8 copy.33
  212.2 4.1 %copy.27 = bf16[128,32,2,128]{3,0,2,1:T(8,128)(2,1)} copy(bf16[128,32,2,128]{0,3,2,1:T(8,128)(2,1)} %bitcast.82) | data formatting | bytes 4194304 | tf_op jit(solution)/shard_map/reshape | solution.py:105
  216.3 3.1 copy.25
  219.4 29.2 %gather_fusion.3 = bf16[8192,128]{1,0:T(8,128)(2,1)} fusion(bf16[128,512]{0,1:T(8,128)(2,1)S(1)} %collective-permute-done.5, s32[8192]{0:T(1024)S(1)} %fusion.61), kind=kCustom, calls=%fused_computation.3.clone | custom fusion | bytes 4227072 | tf_op jit(solution)/shard_map/jit(_take)/gather | solution.py:105
  248.6 6.6 %broadcast_select_fusion.1 = bf16[8192,128]{1,0:T(8,128)(2,1)} fusion(bf16[8192,128]{1,0:T(8,128)(2,1)} %gather_fusion.3, pred[8192]{0:T(1024)(128)(4,1)S(1)} %copy-done.10), kind=kLoop, calls=%fused_computation.44 | loop fusion | flops 1048576 | bytes 4202496 | tf_op jit(solution)/shard_map/jit(_take)/select_n | solution.py:105
  255.2 29.2 %gather_fusion.2 = bf16[8192,128]{1,0:T(8,128)(2,1)} fusion(bf16[128,512]{0,1:T(8,128)(2,1)S(1)} %collective-permute-done.4, s32[8192]{0:T(1024)S(1)} %fusion.60), kind=kCustom, calls=%fused_computation.2.clone | custom fusion | bytes 4227072 | tf_op jit(solution)/shard_map/jit(_take)/gather | solution.py:105
  284.5 6.6 %broadcast_select_fusion.2 = bf16[8192,128]{1,0:T(8,128)(2,1)} fusion(bf16[8192,128]{1,0:T(8,128)(2,1)} %gather_fusion.2, pred[8192]{0:T(1024)(128)(4,1)S(1)} %copy-done.9), kind=kLoop, calls=%fused_computation.45 | loop fusion | flops 1048576 | bytes 4202496 | tf_op jit(solution)/shard_map/jit(_take)/select_n | solution.py:105
  291.0 29.2 %gather_fusion.1 = bf16[8192,128]{1,0:T(8,128)(2,1)} fusion(bf16[128,512]{0,1:T(8,128)(2,1)S(1)} %collective-permute-done.3, s32[8192]{0:T(1024)S(1)} %fusion.59), kind=kCustom, calls=%fused_computation.1.clone | custom fusion | bytes 4227072 | tf_op jit(solution)/shard_map/jit(_take)/gather | solution.py:105
  320.3 6.6 %broadcast_select_fusion.3 = bf16[8192,128]{1,0:T(8,128)(2,1)} fusion(bf16[8192,128]{1,0:T(8,128)(2,1)} %gather_fusion.1, pred[8192]{0:T(1024)(128)(4,1)S(1)} %compare_and_fusion.8), kind=kLoop, calls=%fused_computation.46 | loop fusion | flops 1048576 | bytes 4202496 | tf_op jit(solution)/shard_map/jit(_take)/select_n | solution.py:105
  326.8 4.1 %copy.28 = bf16[128,32,2,128]{3,0,2,1:T(8,128)(2,1)} copy(bf16[128,32,2,128]{0,3,2,1:T(8,128)(2,1)} %bitcast.78) | data formatting | bytes 4194304 | tf_op jit(solution)/shard_map/reshape | solution.py:105
  330.9 4.1 %copy.29 = bf16[128,32,2,128]{3,0,2,1:T(8,128)(2,1)} copy(bf16[128,32,2,128]{0,3,2,1:T(8,128)(2,1)} %bitcast.80) | data formatting | bytes 4194304 | tf_op jit(solution)/shard_map/reshape | solution.py:105
  335.0 4.1 %copy.30 = bf16[128,32,2,128]{3,0,2,1:T(8,128)(2,1)} copy(bf16[128,32,2,128]{0,3,2,1:T(8,128)(2,1)} %bitcast.81) | data formatting | bytes 4194304 | tf_op jit(solution)/shard_map/reshape | solution.py:105
  339.1 29.2 %gather_fusion = bf16[8192,128]{1,0:T(8,128)(2,1)} fusion(bf16[128,512]{0,1:T(8,128)(2,1)S(1)} %collective-permute-done.2, s32[8192]{0:T(1024)S(1)} %fusion.58), kind=kCustom, calls=%fused_computation.clone | custom fusion | bytes 4227072 | tf_op jit(solution)/shard_map/jit(_take)/gather | solution.py:105
  368.3 6.6 %broadcast_select_fusion.4 = bf16[8192,128]{1,0:T(8,128)(2,1)} fusion(bf16[8192,128]{1,0:T(8,128)(2,1)} %gather_fusion, pred[8192]{0:T(1024)(128)(4,1)S(1)} %compare_and_fusion.9), kind=kLoop, calls=%fused_computation.47 | loop fusion | flops 1048576 | bytes 4202496 | tf_op jit(solution)/shard_map/jit(_take)/select_n | solution.py:105
  374.9 4.1 %copy.31 = bf16[128,32,2,128]{3,0,2,1:T(8,128)(2,1)} copy(bf16[128,32,2,128]{0,3,2,1:T(8,128)(2,1)} %bitcast.84) | data formatting | bytes 4194304 | tf_op jit(solution)/shard_map/reshape | solution.py:105
  379.1 6.4 %fusion.17 = f32[32,128,128,1]{1,2,3,0:T(8,128)} fusion(bf16[32,2,128,128]{3,2,1,0:T(8,128)(2,1)S(1)} %copy-done, bf16[128,32,2,128]{3,0,2,1:T(8,128)(2,1)} %copy.31, bf16[128,32,2,128]{3,0,2,1:T(8,128)(2,1)} %copy.30, bf16[128,32,2,128]{3,0,2,1:T(8,128)(2,1)} %copy.29, bf16[128,32,2,128]{3,0,2,1:T(8,128)(2,1)} %copy.28, ...), kind=kOutput, calls=%fused_computation.35 | convolution fusion | flops 273678336 | bytes 14721024 | tf_op jit(solution)/shard_map/bkpq,cbkq->cbp/dot_general | solution.py:118
  385.5 3.2 copy.32
  388.6 3.8 add_convert_fusion
  (76 shorter events, 6.9 us)
Async XLA Ops:
  7.2 371.9 %copy-start = (bf16[32,2,128,128]{3,2,1,0:T(8,128)(2,1)S(1)}, bf16[32,2,128,128]{3,2,1,0:T(8,128)(2,1)}, u32[]{:S(2)}) copy-start(bf16[32,2,128,128]{3,2,1,0:T(8,128)(2,1)} %param.18) | copy-start | bytes 6291460
  7.2 94.2 %all-gather.2.cloned.1.call-start = ((), (), s32[]{:S(2)}) async-start(), calls=%async_computation.1 | async-start | bytes 3145728 | tf_op jit(solution)/shard_map/all_gather | solution.py:78
  8.8 13.0 %collective-permute-start = (bf16[128,1,256]{2,1,0:T(2,128)(2,1)S(1)}, bf16[128,1,256]{2,1,0:T(2,128)(2,1)S(1)}, u32[]{:S(2)}, u32[]{:S(2)}) collective-permute-start(bf16[128,1,256]{2,1,0:T(2,128)(2,1)S(1)} %get-tuple-element.28), channel_id=1, source_target_pairs={{0,2},{2,4},{4,6},{6,8},{8,10},{10,12},{12,14},{14,16},{16,18},{18... | collective-permute-start | bytes 196616 | tf_op jit(solution)/shard_map/ppermute | solution.py:18
  10.7 11.0 %collective-permute-start.1 = (bf16[128,1,256]{2,1,0:T(2,128)(2,1)S(1)}, bf16[128,1,256]{2,1,0:T(2,128)(2,1)S(1)}, u32[]{:S(2)}, u32[]{:S(2)}) collective-permute-start(bf16[128,1,256]{2,1,0:T(2,128)(2,1)S(1)} %get-tuple-element.29), channel_id=1, source_target_pairs={{2,0},{4,2},{6,4},{8,6},{10,8},{12,10},{14,12},{16,14},{18,16},{20... | collective-permute-start | bytes 196616 | tf_op jit(solution)/shard_map/ppermute | solution.py:19
  37.8 4.8 %copy-start.1 = (f32[128,18,256]{2,1,0:T(8,128)S(1)}, f32[128,18,256]{2,1,0:T(8,128)}, u32[]{:S(2)}) copy-start(f32[128,18,256]{2,1,0:T(8,128)} %maximum_convert_fusion) | copy-start | bytes 7077892
  37.9 5.1 %copy-start.4 = (f32[128,16,255]{2,1,0:T(8,128)S(1)}, f32[128,16,255]{2,1,0:T(8,128)}, u32[]{:S(2)}) copy-start(f32[128,16,255]{2,1,0:T(8,128)} %get-tuple-element.22) | copy-start | bytes 6266884
  37.9 5.7 %copy-start.5 = (f32[128,16,255]{2,1,0:T(8,128)S(1)}, f32[128,16,255]{2,1,0:T(8,128)}, u32[]{:S(2)}) copy-start(f32[128,16,255]{2,1,0:T(8,128)} %get-tuple-element.23) | copy-start | bytes 6266884
  37.9 6.3 %copy-start.6 = (f32[128,16,255]{2,1,0:T(8,128)S(1)}, f32[128,16,255]{2,1,0:T(8,128)}, u32[]{:S(2)}) copy-start(f32[128,16,255]{2,1,0:T(8,128)} %get-tuple-element.24) | copy-start | bytes 6266884
  37.9 6.9 %copy-start.7 = (f32[128,16,255]{2,1,0:T(8,128)S(1)}, f32[128,16,255]{2,1,0:T(8,128)}, u32[]{:S(2)}) copy-start(f32[128,16,255]{2,1,0:T(8,128)} %get-tuple-element.25) | copy-start | bytes 6266884
  62.5 3.0 copy-start.21
  62.5 9.1 %copy-start.19 = (bf16[512,256]{1,0:T(8,128)(2,1)S(1)}, bf16[512,256]{1,0:T(8,128)(2,1)}, u32[]{:S(2)}) copy-start(bf16[512,256]{1,0:T(8,128)(2,1)} %param.25) | copy-start | bytes 786436
  62.5 9.1 %copy-start.20 = (bf16[256,512]{1,0:T(8,128)(2,1)S(1)}, bf16[256,512]{1,0:T(8,128)(2,1)}, u32[]{:S(2)}) copy-start(bf16[256,512]{1,0:T(8,128)(2,1)} %param.24) | copy-start | bytes 786436
  65.5 87.9 %reduce-scatter.4.cloned.1.call-start = ((), (), s32[]{:S(2)}) async-start(), calls=%async_computation.2 | async-start | bytes 3538944
  115.0 0.7 copy-start.17
  155.1 1.0 copy-start.2
  156.1 0.7 copy-start.18
  157.0 46.3 %copy-start.11 = (pred[8192]{0:T(1024)(128)(4,1)S(1)}, pred[8192]{0:T(1024)(128)(4,1)}, u32[]{:S(2)}) copy-start(pred[8192]{0:T(1024)(128)(4,1)} %compare_and_fusion.5) | copy-start | bytes 24580
  157.0 62.4 %collective-permute-start.5 = (bf16[128,512]{0,1:T(8,128)(2,1)S(1)}, bf16[128,512]{0,1:T(8,128)(2,1)S(1)}, u32[]{:S(2)}, u32[]{:S(2)}) collective-permute-start(bf16[128,512]{0,1:T(8,128)(2,1)S(1)} %fusion.47), channel_id=1, source_target_pairs={{4,0},{6,2},{8,4},{10,6},{12,8},{14,10},{16,12},{18,14},{20,16},{2... | collective-permute-start | bytes 393224 | tf_op jit(solution)/shard_map/ppermute | solution.py:27
  164.2 91.0 %collective-permute-start.4 = (bf16[128,512]{0,1:T(8,128)(2,1)S(1)}, bf16[128,512]{0,1:T(8,128)(2,1)S(1)}, u32[]{:S(2)}, u32[]{:S(2)}) collective-permute-start(bf16[128,512]{0,1:T(8,128)(2,1)S(1)} %fusion.47), channel_id=1, source_target_pairs={{2,0},{4,2},{6,4},{8,6},{10,8},{12,10},{14,12},{16,14},{18,16},{20... | collective-permute-start | bytes 393224 | tf_op jit(solution)/shard_map/ppermute | solution.py:27
  166.1 124.9 %collective-permute-start.3 = (bf16[128,512]{0,1:T(8,128)(2,1)S(1)}, bf16[128,512]{0,1:T(8,128)(2,1)S(1)}, u32[]{:S(2)}, u32[]{:S(2)}) collective-permute-start(bf16[128,512]{0,1:T(8,128)(2,1)S(1)} %fusion.47), channel_id=1, source_target_pairs={{0,2},{2,4},{4,6},{6,8},{8,10},{10,12},{12,14},{14,16},{16,18},{18... | collective-permute-start | bytes 393224 | tf_op jit(solution)/shard_map/ppermute | solution.py:27
  168.6 170.6 %collective-permute-start.2 = (bf16[128,512]{0,1:T(8,128)(2,1)S(1)}, bf16[128,512]{0,1:T(8,128)(2,1)S(1)}, u32[]{:S(2)}, u32[]{:S(2)}) collective-permute-start(bf16[128,512]{0,1:T(8,128)(2,1)S(1)} %fusion.47), channel_id=1, source_target_pairs={{0,4},{2,6},{4,8},{6,10},{8,12},{10,14},{12,16},{14,18},{16,20},{1... | collective-permute-start | bytes 393224 | tf_op jit(solution)/shard_map/ppermute | solution.py:27
  203.3 6.7 %copy-start.3 = (bf16[128,4608]{0,1:T(8,128)(2,1)S(1)}, bf16[128,4608]{0,1:T(8,128)(2,1)}, u32[]{:S(2)}) copy-start(bf16[128,4608]{0,1:T(8,128)(2,1)} %copy-done.2) | copy-start | bytes 3538948
  219.4 29.2 %copy-start.10 = (pred[8192]{0:T(1024)(128)(4,1)S(1)}, pred[8192]{0:T(1024)(128)(4,1)}, u32[]{:S(2)}) copy-start(pred[8192]{0:T(1024)(128)(4,1)} %compare_and_fusion.6) | copy-start | bytes 24580
  255.2 29.2 %copy-start.9 = (pred[8192]{0:T(1024)(128)(4,1)S(1)}, pred[8192]{0:T(1024)(128)(4,1)}, u32[]{:S(2)}) copy-start(pred[8192]{0:T(1024)(128)(4,1)} %compare_and_fusion.7) | copy-start | bytes 24580
  374.9 4.2 %copy-start.12 = (pred[32,2,128]{2,1,0:T(4,128)(4,1)S(1)}, pred[32,2,128]{2,1,0:T(4,128)(4,1)}, u32[]{:S(2)}) copy-start(pred[32,2,128]{2,1,0:T(4,128)(4,1)} %get-tuple-element.30) | copy-start | bytes 24580
  374.9 4.2 %copy-start.13 = (pred[32,2,128]{2,1,0:T(4,128)(4,1)S(1)}, pred[32,2,128]{2,1,0:T(4,128)(4,1)}, u32[]{:S(2)}) copy-start(pred[32,2,128]{2,1,0:T(4,128)(4,1)} %get-tuple-element.31) | copy-start | bytes 24580
  374.9 4.2 %copy-start.14 = (pred[32,2,128]{2,1,0:T(4,128)(4,1)S(1)}, pred[32,2,128]{2,1,0:T(4,128)(4,1)}, u32[]{:S(2)}) copy-start(pred[32,2,128]{2,1,0:T(4,128)(4,1)} %get-tuple-element.32) | copy-start | bytes 24580
  374.9 4.2 %copy-start.15 = (pred[32,2,128]{2,1,0:T(4,128)(4,1)S(1)}, pred[32,2,128]{2,1,0:T(4,128)(4,1)}, u32[]{:S(2)}) copy-start(pred[32,2,128]{2,1,0:T(4,128)(4,1)} %get-tuple-element.33) | copy-start | bytes 24580
  374.9 4.2 %copy-start.16 = (pred[32,2,128]{2,1,0:T(4,128)(4,1)S(1)}, pred[32,2,128]{2,1,0:T(4,128)(4,1)}, u32[]{:S(2)}) copy-start(pred[32,2,128]{2,1,0:T(4,128)(4,1)} %get-tuple-element.34) | copy-start | bytes 24580
  385.5 3.2 copy-start.8
Sparse Core Ops, SparseCore 0:
  65.6 35.6 all-gather.1
  115.2 38.1 reduce-scatter.3
where the time goes:
time: 402 us; the launch traced here: 399 us
  local copies, waits for them, and re-layouts  211 us (52%)
  waiting for transfers between devices  62.5 us (16%)
  other arithmetic  58.3 us (15%)
  starting transfers between devices  24.5 us (6%)
  between operations  15.1 us (4%)
  blocking collectives  14.3 us (4%)
  matrix products  13.1 us (3%)
    gather x5, local copies, waits for them, and re-layouts, collect(): jnp.take(piece, jnp.clip(local, 0, length - 1).reshape(-1), axis=1)  149 us
    unnamed x3, waiting for transfers between devices  33.4 us
    select_n x5, other arithmetic, collect(): jnp.take(piece, jnp.clip(local, 0, length - 1).reshape(-1), axis=1)  33 us
    all_gather x1, waiting for transfers between devices, on_device(): lax.all_gather(normed_atm, 'comp', axis=0, tiled=True)  29.1 us
    reshape x5, local copies, waits for them, and re-layouts, collect(): jnp.take(piece, jnp.clip(local, 0, length - 1).reshape(-1), axis=1)  20.5 us
    slice x2, local copies, waits for them, and re-layouts, on_device(): jnp.roll(padded[:, lift:lift + height, :], -turn, axis=2)  17.2 us
    unnamed x51, local copies, waits for them, and re-layouts  14.6 us
    ppermute x4, starting transfers between devices, shifted(): return lax.ppermute(block, axis, route)  14.4 us
  transfers between devices with their start and end apart: 8, of which 2 were waited for; matrix products, arithmetic and copies ran while one was open for 44% of the time, Pallas kernels for 0%

commit v1 on v0

v1 whole, which is shorter than its diff:
```python
import functools

import jax
import jax.numpy as jnp
from jax import lax
from jax.experimental import pallas as pl
from jax.experimental.pallas import tpu as pltpu
from jax.sharding import PartitionSpec as P

CHANNELS = 256
HALF = 128
ROWS = 16
COLS = 256
LANES = 128
CELLS_PER_TILE = 128
SLOTS = 4
F32 = jnp.float32
BF16 = jnp.bfloat16
AXES = ("tile", "comp")
WHOLE = pl.BlockSpec()
SMEM = pl.BlockSpec(memory_space=pltpu.SMEM)
SENT = ((3, 9), (1, 3))
MIXED = ((4, 8), (0, 4))


def sds(shape, dtype=BF16):
    return jax.ShapeDtypeStruct(shape, dtype)


def call(kernel, out, ins, specs, scratch=(), flops=0, moved=1 << 20, name=None, **kw):
    return pl.pallas_call(
        kernel,
        out_shape=out,
        in_specs=specs,
        out_specs=kw.pop("out_specs", jax.tree.map(lambda _: WHOLE, out)),
        scratch_shapes=list(scratch),
        compiler_params=pltpu.CompilerParams(vmem_limit_bytes=60 << 20),
        cost_estimate=pl.CostEstimate(flops=flops, bytes_accessed=moved, transcendentals=0),
        name=name,
        **kw,
    )(*ins)


def side_of():
    return lax.axis_index("comp")


def row_at(j, side):
    return jnp.where(side == 0, j, ROWS - 1 - j)


def prep_kernel(state, taps, atm_gain, ocean_gain, *rest):
    sends, (head, keep, own_p, tall) = rest[: len(SENT)], rest[len(SENT) :]
    side = side_of()
    gains = [g[...].astype(F32).reshape(1, HALF) for g in (atm_gain, ocean_gain)]
    own_p[...] = jnp.concatenate([taps[...], *gains, jnp.zeros((5, HALF), F32)], 0)
    high = own_p[...].astype(BF16)
    low = (own_p[...] - high.astype(F32)).astype(BF16)
    head[HALF:, :LANES] = high
    head[HALF:, LANES:] = low
    for h in range(2):
        part = state[:, :, h * LANES : (h + 1) * LANES].astype(F32)
        tall[h] = part.reshape(HALF * ROWS, LANES)

    def row(r):
        parts = [tall.at[h][pl.ds(r, HALF, stride=ROWS), :] for h in range(2)]
        return jnp.concatenate(parts, 1).astype(BF16)

    for j in range(9):
        keep[j] = row(row_at(j, side))
        away = row(row_at(j, 1 - side))
        if j == 0:
            head[:HALF, :] = away
        for (first, last), sent in zip(SENT, sends):
            if first <= j < last:
                sent[j - first] = away


def params_of(head):
    return head[HALF:, :LANES].astype(F32) + head[HALF:, LANES:].astype(F32)


def gelu(x):
    inner = x * (0.7978845608028654 + 0.035677408136300125 * (x * x))
    return (x * (0.5 + 0.5 * jnp.tanh(inner))).astype(BF16)


def dot(a, b):
    return jnp.dot(a, b, preferred_element_type=F32)


def normed(values, gains):
    total = sum(jnp.sum(v, 0, keepdims=True) for v in values)
    squares = sum(jnp.sum(v * v, 0, keepdims=True) for v in values)
    center = total / CHANNELS
    spread = squares / CHANNELS - center * center
    scale = lax.rsqrt(spread + 1e-06)
    return [((v - center) * scale * g).astype(BF16) for v, g in zip(values, gains)]


def turned_up(up, j, side):
    halves = [up[pl.ds(pl.multiple_of(s * HALF, HALF), HALF), j * 256 : (j + 1) * 256] for s in (side, 1 - side)]
    return jnp.concatenate(halves, 0).T


def turned_down(down, j, side):
    halves = [down[j * 256 : (j + 1) * 256, pl.ds(pl.multiple_of(s * HALF, HALF), HALF)] for s in (side, 1 - side)]
    return jnp.concatenate(halves, 1).T


def ocean_kernel(mine, theirs, own_p, head, keep, up, down, kept, sent, pair, x):
    side = side_of()
    pair[0] = keep[0]
    pair[1] = head[:HALF, :]
    gains = [own_p[...].T[:, 10:11], params_of(head).T[:, 10:11]]
    own, other = normed([mine[...].astype(F32), theirs[...].astype(F32)], gains)
    x[:HALF, :] = own
    x[HALF:, :] = other
    total = None
    for j in range(2):
        hidden = gelu(dot(turned_up(up, j, side), x[...]))
        part = dot(turned_down(down, j, side), hidden)
        total = part if total is None else total + part
    kept[...] = total[:HALF]
    sent[...] = total[HALF:].astype(BF16)


def ocean_result_kernel(count, state, kept, got, result, slots):
    for s in range(SLOTS):
        cells = slice(s * CELLS_PER_TILE, (s + 1) * CELLS_PER_TILE)
        value = state[:, cells].astype(F32) + (kept[:, cells] + got[:, cells].astype(F32))
        value = jnp.where(s < count[0], value, 0.0).astype(BF16)
        result[:, cells] = value
        slots[s] = value


def mix(rows, where_own, where_other, ins, own_p, head, blocks, kept, sent, x):
    side = side_of()
    params = []
    for taps in (own_p[...], params_of(head)):
        flipped = jnp.concatenate([taps[6:9], taps[3:6], taps[0:3], taps[9:]], 0)
        params.append(jnp.where(side == 0, taps, flipped).T)

    def fetch(place):
        ref, index = place
        value = ins[ref][:HALF, :] if index is None else ins[ref][index]
        return value.astype(F32)

    def conv(places, p):
        lines = [fetch(place) for place in places]
        left, middle, right = [
            sum(p[:, 3 * a + b : 3 * a + b + 1] * lines[a] for a in range(3)) for b in range(3)
        ]
        return middle + pltpu.roll(left, 1, 1) + pltpu.roll(right, COLS - 1, 1)

    for i in range(rows):
        values = [conv(where_own[i : i + 3], params[0]), conv(where_other[i : i + 3], params[1])]
        own, other = normed(values, [p[:, 9:10] for p in params])
        x[:HALF, i * COLS : (i + 1) * COLS] = own
        x[HALF:, i * COLS : (i + 1) * COLS] = other
    for i in range(0, rows, 2):
        cells = slice(i * COLS, (i + 2) * COLS)
        delta = None
        for j in range(4):
            part = dot(blocks[4 + j], gelu(dot(blocks[j], x[:, cells])))
            delta = part if delta is None else delta + part
        for n in range(2):
            value = delta[:, n * COLS : (n + 1) * COLS].astype(BF16)
            kept[i + n] = value[:HALF]
            sent[i + n] = value[HALF:]


def mix_first_kernel(rows, where_own, where_other, n_in, own_p, head, up, down, got_up, got_down, *rest):
    ins, (kept, sent, blocks, x) = rest[:n_in], rest[n_in:]
    side = side_of()
    for n, (u, d) in enumerate(((up, down), (got_up, got_down))):
        for j in range(2):
            blocks[2 * n + j] = turned_up(u, j, side)
            blocks[4 + 2 * n + j] = turned_down(d, j, side)
    mix(rows, where_own, where_other, ins, own_p, head, blocks, kept, sent, x)


def mix_kernel(rows, where_own, where_other, n_in, own_p, head, blocks, *rest):
    ins, (kept, sent, x) = rest[:n_in], rest[n_in:]
    mix(rows, where_own, where_other, ins, own_p, head, blocks, kept, sent, x)


def regrid_kernel(source, table_own, table_swap, table_e1, table_e2, table_last, w, out, table):
    step = pl.program_id(0)
    tile = lax.axis_index("tile")
    core, odd = lax.rem(tile, 2), lax.rem(tile // 2, 2)

    @pl.when(step == 0)
    def _():
        for n, part in enumerate((table_own, table_swap, table_last, table_e1, table_e2)):
            table[n * SLOTS : (n + 1) * SLOTS] = part[...]

    def slab(b, k):
        slot = source[b, k]
        offset = slot // SLOTS - tile
        near = jnp.where((offset > 0) == (core == 0), 1, 2)
        far = jnp.where((offset > 0) == (odd == 1), 3, 4)
        part = jnp.where(offset == 0, 0, jnp.where(abs(offset) == 1, near, far))
        return table[part * SLOTS + lax.rem(slot, SLOTS)]

    per_step = w.shape[0]
    for n in range(per_step):
        b = step * per_step + n
        slabs = jnp.concatenate([slab(b, 0), slab(b, 1)], 1)
        weight = jnp.concatenate([w[n, 0], w[n, 1]], 1)
        value = lax.dot_general(slabs, weight, (((1,), (1,)), ((), ())), preferred_element_type=F32)
        out[n // 2, :, (n % 2) * 128 : (n % 2 + 1) * 128] = value


def final_kernel(n, state, regrid, *rest):
    kept, got, out, tall = rest[:n], rest[n : 2 * n], rest[2 * n], rest[2 * n + 1]
    side = side_of()
    depth = state.shape[0]
    for refs, which in ((kept, side), (got, 1 - side)):
        for (first, last), ref in zip(MIXED, refs):
            for j in range(first, last):
                r = row_at(j, which)
                value = regrid[r] + ref[j - first].astype(F32)
                for h in range(2):
                    tall.at[h][pl.ds(r, depth, stride=ROWS), :] = value[:, h * LANES : (h + 1) * LANES]
    for h in range(2):
        lanes = slice(h * LANES, (h + 1) * LANES)
        added = tall[h].reshape(depth, ROWS, LANES)
        out[:, :, lanes] = (state[:, :, lanes].astype(F32) + added).astype(BF16)


def on_device(
    atm_state, ocean_state, ocean_count, regrid_src, regrid_w, dw_kernel,
    atm_gain, atm_up, atm_down, ocean_gain, ocean_up, ocean_down,
):
    tiles = lax.axis_size("tile")
    tile = lax.axis_index("tile")

    def move(x, to):
        route = []
        for t in range(tiles):
            for c in range(2):
                u, d = to(t, c)
                if 0 <= u < tiles:
                    route.append((t * 2 + c, u * 2 + d))
        return lax.ppermute(x, AXES, route)

    def partner(x):
        return move(x, lambda t, c: (t, 1 - c))

    half_turn = 8 if tiles >= 16 else 0

    def across(x):
        return move(x, lambda t, c: (t ^ half_turn, 1 - c))

    ocean_theirs = partner(ocean_state)
    got_up, got_down = across(atm_up), across(atm_down)
    *sends, head_sent, keep, own_p = call(
        prep_kernel,
        [sds((b - a, HALF, COLS)) for a, b in SENT]
        + [sds((HALF + 16, COLS)), sds((9, HALF, COLS)), sds((16, HALF), F32)],
        (atm_state, dw_kernel, atm_gain, ocean_gain),
        [WHOLE] * 4,
        [pltpu.VMEM((2, HALF * ROWS, LANES), F32)],
        moved=3 << 20,
        name="prep",
    )
    head = partner(head_sent)
    got = [partner(s) for s in sends]

    cells = ocean_state.shape[1]
    ocean_kept, ocean_sent, pair = call(
        ocean_kernel,
        [sds((HALF, cells), F32), sds((HALF, cells)), sds((2, HALF, COLS))],
        (ocean_state, ocean_theirs, own_p, head, keep, ocean_up, ocean_down),
        [WHOLE] * 7,
        [pltpu.VMEM((256, cells), BF16)],
        flops=2 * 2 * 256 * 512 * cells,
        moved=2 << 20,
        name="ocean",
    )
    ocean_got = partner(ocean_sent)
    edges = move(pair, lambda t, c: (t - 1 + 2 * c, 1 - c))
    ocean_result, slots = call(
        ocean_result_kernel,
        [sds((HALF, cells)), sds((SLOTS, HALF, CELLS_PER_TILE))],
        (ocean_count, ocean_state, ocean_kept, ocean_got),
        [SMEM, WHOLE, WHOLE, WHOLE],
        moved=1 << 20,
        name="ocean_result",
    )
    swapped = move(slots, lambda t, c: (t ^ 1, c))
    e2 = move(slots, lambda t, c: (t ^ 2, c))
    e1 = move(slots, lambda t, c: (t + 2 if t // 2 % 2 else t - 2, c))
    passed = jnp.where(tile % 2 == tile // 2 % 2, e2, e1)
    last = move(passed, lambda t, c: (t ^ 1, c))

    kept_rows, got_rows, blocks = [], [], None
    for a, b in MIXED:
        ins, where_own, where_other = [keep], [], []
        for j in range(a - 1, b + 1):
            if j < 0:
                where_own.append((len(ins), 1))
                where_other.append((len(ins), 0))
                ins.append(edges)
                continue
            where_own.append((0, j))
            if j == 0:
                where_other.append((len(ins), None))
                ins.append(head)
                continue
            k = [n for n, (p, q) in enumerate(SENT) if p <= j < q][0]
            place = [n for n, x in enumerate(ins) if x is got[k]]
            if not place:
                place = [len(ins)]
                ins.append(got[k])
            where_other.append((place[0], j - SENT[k][0]))
        rows = b - a
        cost = dict(flops=rows * COLS * 256 * 1024 * 4, moved=3 << 20)
        out = [sds((rows, HALF, COLS))] * 2
        x_spec = pltpu.VMEM((CHANNELS, rows * COLS), BF16)
        if blocks is None:
            kept, sent, blocks = call(
                functools.partial(mix_first_kernel, rows, where_own, where_other, len(ins)),
                out + [sds((8, 256, 256))],
                (own_p, head, atm_up, atm_down, got_up, got_down, *ins),
                [WHOLE] * (6 + len(ins)),
                [x_spec],
                name="mix_first",
                **cost,
            )
        else:
            kept, sent = call(
                functools.partial(mix_kernel, rows, where_own, where_other, len(ins)),
                out,
                (own_p, head, blocks, *ins),
                [WHOLE] * (3 + len(ins)),
                [x_spec],
                name="mix",
                **cost,
            )
        kept_rows.append(kept)
        got_rows.append(partner(sent))

    steps = 4
    per_step = regrid_src.shape[0] // steps
    table = pl.BlockSpec((SLOTS, HALF, CELLS_PER_TILE), lambda i: (0, 0, 0))
    regrid = call(
        regrid_kernel,
        sds((ROWS, HALF, COLS), F32),
        (regrid_src, slots, swapped, e1, e2, last, regrid_w),
        [SMEM] + [table] * 5 + [pl.BlockSpec((per_step, 2, 128, 128), lambda i: (i, 0, 0, 0))],
        [pltpu.VMEM((5 * SLOTS, HALF, CELLS_PER_TILE), BF16)],
        grid=(steps,),
        out_specs=pl.BlockSpec((ROWS // steps, HALF, COLS), lambda i: (i, 0, 0)),
        flops=32 * 2 * 128 * 256 * 128,
        moved=5 << 20,
        name="regrid",
    )
    depth = HALF // 4
    rows_spec = [pl.BlockSpec((b - a, depth, COLS), lambda i: (0, i, 0)) for a, b in MIXED]
    state_spec = pl.BlockSpec((depth, ROWS, COLS), lambda i: (i, 0, 0))
    atm_out = call(
        functools.partial(final_kernel, len(MIXED)),
        sds((HALF, ROWS, COLS)),
        (atm_state, regrid, *kept_rows, *got_rows),
        [state_spec, pl.BlockSpec((ROWS, depth, COLS), lambda i: (0, i, 0))] + rows_spec * 2,
        [pltpu.VMEM((2, depth * ROWS, LANES), F32)],
        grid=(HALF // depth,),
        out_specs=state_spec,
        moved=5 << 20,
        name="final",
    )
    return (atm_out, ocean_result)


def solution(mesh):
    return jax.shard_map(
        on_device,
        mesh=mesh,
        in_specs=(
            P("comp", "tile", None),
            P("comp", "tile"),
            P("tile"),
            P("tile", None),
            P("tile", None, None, None),
            P(None, "comp"),
            P("comp"),
            P(None, "comp"),
            P("comp", None),
            P("comp"),
            P(None, "comp"),
            P("comp", None),
        ),
        out_specs=(P("comp", "tile", None), P("comp", "tile")),
        check_vma=False,
    )
```

time: 402 us -> 77.4 us (0.19)
  local copies, waits for them, and re-layouts: 211 us -> 3.51 us
  other arithmetic: 58.3 us -> 0.02 us
  waiting for transfers between devices: 62.5 us -> 20.2 us
  Pallas kernels: 0 us -> 30.3 us
  blocking collectives: 14.3 us -> 0 us
  between operations: 15.1 us -> 1.45 us
  matrix products: 13.1 us -> 0 us
    gather x5 -> x0, local copies, waits for them, and re-layouts: 149 us -> none  [collect(): jnp.take(piece, jnp.clip(local, 0, length - 1).reshape(-1), axis=1)]
    unnamed x3 -> x0, waiting for transfers between devices: 33.4 us -> none
    select_n x5 -> x1, other arithmetic: 33 us -> 0.02 us  [on_device(): passed = jnp.where(tile % 2 == tile // 2 % 2, e2, e1)]
    pallas_call x0 -> x7, Pallas kernels: none -> 30.3 us  [call(): pl.pallas_call(kernel, out_shape=out, in_specs=specs, out_specs=kw.pop('o...]
    all_gather x1 -> x0, waiting for transfers between devices: 29.1 us -> none  [on_device(): lax.all_gather(normed_atm, 'comp', axis=0, tiled=True)]
    reshape x7 -> x0, local copies, waits for them, and re-layouts: 26.8 us -> none  [the longest x5 20.5 us: collect(): jnp.take(piece, jnp.clip(local, 0, length - 1).reshape(-1), axis=1)]
    slice x4 -> x0, local copies, waits for them, and re-layouts: 20.2 us -> none  [the longest x2 17.2 us: on_device(): jnp.roll(padded[:, lift:lift + height, :], -turn, axis=2)]
    ppermute x6 -> x14, waiting for transfers between devices: 0.02 us -> 20.2 us  [move(): return lax.ppermute(x, AXES, route)]
  transfers between devices with their start and end apart: 8 -> 14, of which waited for: 2 -> 5; matrix products, arithmetic and copies ran while one was open for 44% -> 1% of each run, Pallas kernels for 0% -> 29%
where the time goes in v1:
time: 77.4 us; the launch traced here: 77 us
  Pallas kernels  30.3 us (39%)
  starting transfers between devices  21.5 us (28%)
  waiting for transfers between devices  20.2 us (26%)
  local copies, waits for them, and re-layouts  3.51 us (5%)
  between operations  1.45 us (2%)
    pallas_call x7, Pallas kernels, call(): pl.pallas_call(kernel, out_shape=out, in_specs=specs, out_specs=kw.pop('o...  30.3 us
    ppermute x14, starting transfers between devices, move(): return lax.ppermute(x, AXES, route)  21.5 us
    ppermute x14, waiting for transfers between devices, move(): return lax.ppermute(x, AXES, route)  20.2 us
    unnamed x33, local copies, waits for them, and re-layouts  3.51 us
  transfers between devices with their start and end apart: 14, of which 5 were waited for; matrix products, arithmetic and copies ran while one was open for 1% of the time, Pallas kernels for 29%

profile of v1, /device:TPU:24, one launch (start us, length us, event | category | flops | bytes accessed | tf_op | source)
XLA Modules:
  0.0 77.0 jit_solution(633852213864120058)
XLA Ops:
  0.6 3.4 %prep.1 = (bf16[6,128,256]{2,1,0:T(8,128)(2,1)}, bf16[2,128,256]{2,1,0:T(8,128)(2,1)}, bf16[144,256]{1,0:T(8,128)(2,1)}, bf16[9,128,256]{2,1,0:T(8,128)(2,1)}, f32[16,128]{1,0:T(8,128)}) custom-call(bf16[128,16,256]{2,1,0:T(8,128)(2,1)} %state.5, f32[9,128]{1,0:T(8,128)} %taps.1, bf16[128]{0:T(256)(128)(2,1)} %atm_gain.1, bf16[128]{0:T(256)(128)(2,1)} %ocean_gain.1), custom_call_target="tpu_custom_call" | custom-call | bytes 3145728 | tf_op jit(solution)/shard_map/prep/pallas_call | solution.py:31
  4.0 1.5 %collective-permute-start.9 = (bf16[6,128,256]{2,1,0:T(8,128)(2,1)}, bf16[6,128,256]{2,1,0:T(8,128)(2,1)S(1)}, u32[]{:S(2)}, u32[]{:S(2)}) collective-permute-start(bf16[6,128,256]{2,1,0:T(8,128)(2,1)} %get-tuple-element.23), channel_id=1, source_target_pairs={{0,1},{1,0},{2,3},{3,2},{4,5},{5,4},{6,7},{7,6},{8,9},{9,8},{10,11... | collective-permute-start | bytes 1179656 | tf_op jit(solution)/shard_map/ppermute | solution.py:246
  5.5 0.5 collective-permute-start
  6.0 2.8 %collective-permute-start.7 = (bf16[256,512]{1,0:T(8,128)(2,1)}, bf16[256,512]{1,0:T(8,128)(2,1)S(1)}, u32[]{:S(2)}, u32[]{:S(2)}) collective-permute-start(bf16[256,512]{1,0:T(8,128)(2,1)} %up.3), channel_id=1, source_target_pairs={{0,17},{1,16},{2,19},{3,18},{4,21},{5,20},{6,23},{7,22},{8,25},{9,... | collective-permute-start | bytes 786440 | tf_op jit(solution)/shard_map/ppermute | solution.py:246
  8.8 0.5 collective-permute-start.8
  9.3 0.3 collective-permute-start.1
  9.6 9.9 %collective-permute-done.1.head.rest_2_ = bf16[144,256]{1,0:T(8,128)(2,1)S(1)} collective-permute-done((bf16[144,256]{1,0:T(8,128)(2,1)}, bf16[144,256]{1,0:T(8,128)(2,1)S(1)}, u32[]{:S(2)}, u32[]{:S(2)}) %collective-permute-start.1) | collective-permute-done | bytes 73760 | tf_op jit(solution)/shard_map/ppermute | solution.py:246
  19.5 0.0 collective-permute-done.theirs
  19.5 0.6 copy-done.8
  20.1 0.1 copy-done.6
  20.2 3.1 %ocean.1 = (f32[128,512]{1,0:T(8,128)}, bf16[128,512]{1,0:T(8,128)(2,1)}, bf16[2,128,256]{2,1,0:T(8,128)(2,1)}) custom-call(bf16[128,512]{1,0:T(8,128)(2,1)} %state.4, bf16[128,512]{1,0:T(8,128)(2,1)} %copy-done.6, f32[16,128]{1,0:T(8,128)} %get-tuple-element.17.own_p, bf16[144,256]{1,0:T(8,128)(2,1)} %copy-done.8, ...), custom_call_target="tpu_custom_call" | custom-call | flops 268435456 | bytes 2097152 | tf_op jit(solution)/shard_map/ocean/pallas_call | solution.py:31
  23.3 1.5 %collective-permute-start.2 = (bf16[128,512]{1,0:T(8,128)(2,1)}, bf16[128,512]{1,0:T(8,128)(2,1)S(1)}, u32[]{:S(2)}, u32[]{:S(2)}) collective-permute-start(bf16[128,512]{1,0:T(8,128)(2,1)} %get-tuple-element.21), channel_id=1, source_target_pairs={{0,1},{1,0},{2,3},{3,2},{4,5},{5,4},{6,7},{7,6},{8,9},{9,8},{10,11... | collective-permute-start | bytes 393224 | tf_op jit(solution)/shard_map/ppermute | solution.py:246
  24.8 0.5 collective-permute-start.11
  25.3 4.0 %collective-permute-done.2.got = bf16[128,512]{1,0:T(8,128)(2,1)S(1)} collective-permute-done((bf16[128,512]{1,0:T(8,128)(2,1)}, bf16[128,512]{1,0:T(8,128)(2,1)S(1)}, u32[]{:S(2)}, u32[]{:S(2)}) %collective-permute-start.2) | collective-permute-done | bytes 131104 | tf_op jit(solution)/shard_map/ppermute | solution.py:246
  29.2 4.9 %collective-permute-start.10 = (bf16[2,128,256]{2,1,0:T(8,128)(2,1)}, bf16[2,128,256]{2,1,0:T(8,128)(2,1)S(1)}, u32[]{:S(2)}, u32[]{:S(2)}) collective-permute-start(bf16[2,128,256]{2,1,0:T(8,128)(2,1)} %get-tuple-element.26), channel_id=1, source_target_pairs={{1,2},{2,1},{3,4},{4,3},{5,6},{6,5},{7,8},{8,7},{9,10},{10,9},{11,... | collective-permute-start | bytes 393224 | tf_op jit(solution)/shard_map/ppermute | solution.py:246
  34.8 0.0 copy-done.4
  34.8 1.8 %ocean_result.1 = (bf16[128,512]{1,0:T(8,128)(2,1)}, bf16[4,128,128]{2,1,0:T(8,128)(2,1)}) custom-call(s32[1]{0:T(128)S(6)} %copy.15.count, bf16[128,512]{1,0:T(8,128)(2,1)} %state.4, f32[128,512]{1,0:T(8,128)} %get-tuple-element.20.kept, bf16[128,512]{1,0:T(8,128)(2,1)} %copy-done.4), custom_call_target="tpu_custom_call" | custom-call | bytes 1048576 | tf_op jit(solution)/shard_map/ocean_result/pallas_call | solution.py:31
  36.7 0.0 collective-permute-done.7.got_up
  36.7 0.1 collective-permute-start.5
  36.7 0.0 collective-permute-done.8.got_down
  36.7 0.0 copy-start.12
  36.7 6.0 %collective-permute-start.4 = (bf16[4,128,128]{2,1,0:T(8,128)(2,1)}, bf16[4,128,128]{2,1,0:T(8,128)(2,1)S(1)}, u32[]{:S(2)}, u32[]{:S(2)}) collective-permute-start(bf16[4,128,128]{2,1,0:T(8,128)(2,1)} %get-tuple-element.22.table_own), channel_id=1, source_target_pairs={{4,8},{5,9},{6,10},{7,11},{8,4},{9,5},{10,6},{11,7},{12,16},{13,17... | collective-permute-start | bytes 393224 | tf_op jit(solution)/shard_map/ppermute | solution.py:246
  42.7 0.0 collective-permute-done.9.rest_1_.rest_4_
  42.7 0.8 %collective-permute-start.3 = (bf16[4,128,128]{2,1,0:T(8,128)(2,1)}, bf16[4,128,128]{2,1,0:T(8,128)(2,1)S(1)}, u32[]{:S(2)}, u32[]{:S(2)}) collective-permute-start(bf16[4,128,128]{2,1,0:T(8,128)(2,1)} %get-tuple-element.22.table_own), channel_id=1, source_target_pairs={{0,2},{1,3},{2,0},{3,1},{4,6},{5,7},{6,4},{7,5},{8,10},{9,11},{10,... | collective-permute-start | bytes 393224 | tf_op jit(solution)/shard_map/ppermute | solution.py:246
  43.5 0.0 copy-done.12
  43.5 6.5 %mix_first.1 = (bf16[4,128,256]{2,1,0:T(8,128)(2,1)}, bf16[4,128,256]{2,1,0:T(8,128)(2,1)}, bf16[8,256,256]{2,1,0:T(8,128)(2,1)}) custom-call(f32[16,128]{1,0:T(8,128)} %get-tuple-element.17.own_p, bf16[144,256]{1,0:T(8,128)(2,1)} %copy-done.8, bf16[256,512]{1,0:T(8,128)(2,1)} %up.3, bf16[512,256]{1,0:T(8,128)(2,1)} %down.3, bf16[256,512]{1,0:T(8,128)(2,1)} %copy-done.11, ...), custom_call_target="tpu_custom_call" | custom-call | flops 1073741824 | bytes 3145728 | tf_op jit(solution)/shard_map/mix_first/pallas_call | solution.py:31
  50.1 0.0 collective-permute-done.11.rest_3_
  50.1 0.0 copy-start.14
  50.1 0.0 collective-permute-done.10.rest_1_
  50.1 0.6 copy-done.14
  50.7 0.1 copy-done.15
  50.8 6.3 %mix.1 = (bf16[4,128,256]{2,1,0:T(8,128)(2,1)}, bf16[4,128,256]{2,1,0:T(8,128)(2,1)}) custom-call(f32[16,128]{1,0:T(8,128)} %get-tuple-element.17.own_p, bf16[144,256]{1,0:T(8,128)(2,1)} %copy-done.8, bf16[8,256,256]{2,1,0:T(8,128)(2,1)} %get-tuple-element.25.blocks, bf16[9,128,256]{2,1,0:T(8,128)(2,1)} %get-tuple-element.19.keep.rest_0_, ...), custom_call_target="tpu_custom_call" | custom-call | flops 1073741824 | bytes 3145728 | tf_op jit(solution)/shard_map/mix/pallas_call | solution.py:31
  57.1 1.3 %collective-permute-start.13 = (bf16[4,128,256]{2,1,0:T(8,128)(2,1)}, bf16[4,128,256]{2,1,0:T(8,128)(2,1)S(1)}, u32[]{:S(2)}, u32[]{:S(2)}) collective-permute-start(bf16[4,128,256]{2,1,0:T(8,128)(2,1)} %get-tuple-element.30), channel_id=1, source_target_pairs={{0,1},{1,0},{2,3},{3,2},{4,5},{5,4},{6,7},{7,6},{8,9},{9,8},{10,11... | collective-permute-start | bytes 786440 | tf_op jit(solution)/shard_map/ppermute | solution.py:246
  58.4 0.7 collective-permute-start.12
  59.2 0.0 collective-permute-done.5.table_e2
  59.2 0.0 collective-permute-done.4.table_e1
  59.2 0.2 collective-permute-start.6
  59.4 0.7 copy.14.source
  60.1 0.0 collective-permute-done.3.table_swap
  60.1 0.6 collective-permute-done.6.table_last
  60.6 0.0 copy-done.1
  60.6 0.1 copy-done.5
  60.7 0.7 copy-done.7
  61.4 4.7 %regrid.1 = f32[16,128,256]{2,1,0:T(8,128)} custom-call(s32[32,2]{1,0:T(8,128)} %copy.14.source, bf16[4,128,128]{2,1,0:T(8,128)(2,1)} %get-tuple-element.22.table_own, bf16[4,128,128]{2,1,0:T(8,128)(2,1)} %copy-done.5, bf16[4,128,128]{2,1,0:T(8,128)(2,1)} %copy-done.1, bf16[4,128,128]{2,1,0:T(8,128)(2,1)} %copy-done, bf16[4,128,128]{2,1,0:T(8,128)(2,1)} %copy-done.7, ...), custom_call_target="tpu_custom_call" | custom-call | flops 268435456 | bytes 5242880 | tf_op jit(solution)/shard_map/regrid/pallas_call | solution.py:31
  66.1 0.4 collective-permute-done.13.rest_3_
  66.5 5.3 %collective-permute-done.12.rest_2_ = bf16[4,128,256]{2,1,0:T(8,128)(2,1)S(1)} collective-permute-done((bf16[4,128,256]{2,1,0:T(8,128)(2,1)S(1)}, bf16[4,128,256]{2,1,0:T(8,128)(2,1)S(1)}, u32[]{:S(2)}, u32[]{:S(2)}) %collective-permute-start.12) | collective-permute-done | bytes 262176 | tf_op jit(solution)/shard_map/ppermute | solution.py:246
  71.8 0.7 copy-done.3
  72.5 4.4 %final.1 = bf16[128,16,256]{2,1,0:T(8,128)(2,1)} custom-call(bf16[128,16,256]{2,1,0:T(8,128)(2,1)} %state.5, f32[16,128,256]{2,1,0:T(8,128)} %regrid.1, bf16[4,128,256]{2,1,0:T(8,128)(2,1)} %get-tuple-element.24.rest_0_, bf16[4,128,256]{2,1,0:T(8,128)(2,1)} %get-tuple-element.28.rest_1_, bf16[4,128,256]{2,1,0:T(8,128)(2,1)} %copy-done.3, ...), custom_call_target="tpu_custom_call" | custom-call | bytes 5242880 | tf_op jit(solution)/shard_map/final/pallas_call | solution.py:31
  (21 shorter events, 0.1 us)
Async XLA Ops:
  4.0 38.7 %collective-permute-start.9 = (bf16[6,128,256]{2,1,0:T(8,128)(2,1)}, bf16[6,128,256]{2,1,0:T(8,128)(2,1)S(1)}, u32[]{:S(2)}, u32[]{:S(2)}) collective-permute-start(bf16[6,128,256]{2,1,0:T(8,128)(2,1)} %get-tuple-element.23), channel_id=1, source_target_pairs={{0,1},{1,0},{2,3},{3,2},{4,5},{5,4},{6,7},{7,6},{8,9},{9,8},{10,11... | collective-permute-start | bytes 1179656 | tf_op jit(solution)/shard_map/ppermute | solution.py:246
  5.5 14.0 %collective-permute-start = (bf16[128,512]{1,0:T(8,128)(2,1)}, bf16[128,512]{1,0:T(8,128)(2,1)S(1)}, u32[]{:S(2)}, u32[]{:S(2)}) collective-permute-start(bf16[128,512]{1,0:T(8,128)(2,1)} %state.4), channel_id=1, source_target_pairs={{0,1},{1,0},{2,3},{3,2},{4,5},{5,4},{6,7},{7,6},{8,9},{9,8},{10,11... | collective-permute-start | bytes 393224 | tf_op jit(solution)/shard_map/ppermute | solution.py:246
  6.0 30.6 %collective-permute-start.7 = (bf16[256,512]{1,0:T(8,128)(2,1)}, bf16[256,512]{1,0:T(8,128)(2,1)S(1)}, u32[]{:S(2)}, u32[]{:S(2)}) collective-permute-start(bf16[256,512]{1,0:T(8,128)(2,1)} %up.3), channel_id=1, source_target_pairs={{0,17},{1,16},{2,19},{3,18},{4,21},{5,20},{6,23},{7,22},{8,25},{9,... | collective-permute-start | bytes 786440 | tf_op jit(solution)/shard_map/ppermute | solution.py:246
  8.8 27.9 %collective-permute-start.8 = (bf16[512,256]{1,0:T(8,128)(2,1)}, bf16[512,256]{1,0:T(8,128)(2,1)S(1)}, u32[]{:S(2)}, u32[]{:S(2)}) collective-permute-start(bf16[512,256]{1,0:T(8,128)(2,1)} %down.3), channel_id=1, source_target_pairs={{0,17},{1,16},{2,19},{3,18},{4,21},{5,20},{6,23},{7,22},{8,25},{9,... | collective-permute-start | bytes 786440 | tf_op jit(solution)/shard_map/ppermute | solution.py:246
  9.3 10.2 %collective-permute-start.1 = (bf16[144,256]{1,0:T(8,128)(2,1)}, bf16[144,256]{1,0:T(8,128)(2,1)S(1)}, u32[]{:S(2)}, u32[]{:S(2)}) collective-permute-start(bf16[144,256]{1,0:T(8,128)(2,1)} %get-tuple-element.18), channel_id=1, source_target_pairs={{0,1},{1,0},{2,3},{3,2},{4,5},{5,4},{6,7},{7,6},{8,9},{9,8},{10,11... | collective-permute-start | bytes 221192 | tf_op jit(solution)/shard_map/ppermute | solution.py:246
  19.5 0.6 copy-start.8
  19.5 0.7 copy-start.6
  23.3 6.0 %collective-permute-start.2 = (bf16[128,512]{1,0:T(8,128)(2,1)}, bf16[128,512]{1,0:T(8,128)(2,1)S(1)}, u32[]{:S(2)}, u32[]{:S(2)}) collective-permute-start(bf16[128,512]{1,0:T(8,128)(2,1)} %get-tuple-element.21), channel_id=1, source_target_pairs={{0,1},{1,0},{2,3},{3,2},{4,5},{5,4},{6,7},{7,6},{8,9},{9,8},{10,11... | collective-permute-start | bytes 393224 | tf_op jit(solution)/shard_map/ppermute | solution.py:246
  24.8 25.3 %collective-permute-start.11 = (bf16[2,128,256]{2,1,0:T(8,128)(2,1)}, bf16[2,128,256]{2,1,0:T(8,128)(2,1)S(1)}, u32[]{:S(2)}, u32[]{:S(2)}) collective-permute-start(bf16[2,128,256]{2,1,0:T(8,128)(2,1)} %get-tuple-element.27), channel_id=1, source_target_pairs={{0,1},{1,0},{2,3},{3,2},{4,5},{5,4},{6,7},{7,6},{8,9},{9,8},{10,11... | collective-permute-start | bytes 393224 | tf_op jit(solution)/shard_map/ppermute | solution.py:246
  29.2 5.6 %copy-start.4 = (bf16[128,512]{1,0:T(8,128)(2,1)}, bf16[128,512]{1,0:T(8,128)(2,1)S(1)}, u32[]{:S(2)}) copy-start(bf16[128,512]{1,0:T(8,128)(2,1)S(1)} %collective-permute-done.2.got) | copy-start | bytes 393220
  29.2 20.8 %collective-permute-start.10 = (bf16[2,128,256]{2,1,0:T(8,128)(2,1)}, bf16[2,128,256]{2,1,0:T(8,128)(2,1)S(1)}, u32[]{:S(2)}, u32[]{:S(2)}) collective-permute-start(bf16[2,128,256]{2,1,0:T(8,128)(2,1)} %get-tuple-element.26), channel_id=1, source_target_pairs={{1,2},{2,1},{3,4},{4,3},{5,6},{6,5},{7,8},{8,7},{9,10},{10,9},{11,... | collective-permute-start | bytes 393224 | tf_op jit(solution)/shard_map/ppermute | solution.py:246
  36.7 6.9 %copy-start.11 = (bf16[256,512]{1,0:T(8,128)(2,1)}, bf16[256,512]{1,0:T(8,128)(2,1)S(1)}, u32[]{:S(2)}) copy-start(bf16[256,512]{1,0:T(8,128)(2,1)S(1)} %collective-permute-done.7.got_up) | copy-start | bytes 786436
  36.7 22.5 %collective-permute-start.5 = (bf16[4,128,128]{2,1,0:T(8,128)(2,1)}, bf16[4,128,128]{2,1,0:T(8,128)(2,1)S(1)}, u32[]{:S(2)}, u32[]{:S(2)}) collective-permute-start(bf16[4,128,128]{2,1,0:T(8,128)(2,1)} %get-tuple-element.22.table_own), channel_id=1, source_target_pairs={{0,4},{1,5},{2,6},{3,7},{4,0},{5,1},{6,2},{7,3},{8,12},{9,13},{10,... | collective-permute-start | bytes 393224 | tf_op jit(solution)/shard_map/ppermute | solution.py:246
  36.7 6.8 %copy-start.12 = (bf16[512,256]{1,0:T(8,128)(2,1)}, bf16[512,256]{1,0:T(8,128)(2,1)S(1)}, u32[]{:S(2)}) copy-start(bf16[512,256]{1,0:T(8,128)(2,1)S(1)} %collective-permute-done.8.got_down) | copy-start | bytes 786436
  36.7 22.4 %collective-permute-start.4 = (bf16[4,128,128]{2,1,0:T(8,128)(2,1)}, bf16[4,128,128]{2,1,0:T(8,128)(2,1)S(1)}, u32[]{:S(2)}, u32[]{:S(2)}) collective-permute-start(bf16[4,128,128]{2,1,0:T(8,128)(2,1)} %get-tuple-element.22.table_own), channel_id=1, source_target_pairs={{4,8},{5,9},{6,10},{7,11},{8,4},{9,5},{10,6},{11,7},{12,16},{13,17... | collective-permute-start | bytes 393224 | tf_op jit(solution)/shard_map/ppermute | solution.py:246
  42.7 0.8 %copy-start.10 = (bf16[6,128,256]{2,1,0:T(8,128)(2,1)}, bf16[6,128,256]{2,1,0:T(8,128)(2,1)S(1)}, u32[]{:S(2)}) copy-start(bf16[6,128,256]{2,1,0:T(8,128)(2,1)S(1)} %collective-permute-done.9.rest_1_.rest_4_) | copy-start | bytes 1179652
  42.7 17.3 %collective-permute-start.3 = (bf16[4,128,128]{2,1,0:T(8,128)(2,1)}, bf16[4,128,128]{2,1,0:T(8,128)(2,1)S(1)}, u32[]{:S(2)}, u32[]{:S(2)}) collective-permute-start(bf16[4,128,128]{2,1,0:T(8,128)(2,1)} %get-tuple-element.22.table_own), channel_id=1, source_target_pairs={{0,2},{1,3},{2,0},{3,1},{4,6},{5,7},{6,4},{7,5},{8,10},{9,11},{10,... | collective-permute-start | bytes 393224 | tf_op jit(solution)/shard_map/ppermute | solution.py:246
  50.1 8.4 %copy-start.13 = (bf16[4,128,256]{2,1,0:T(8,128)(2,1)S(1)}, bf16[4,128,256]{2,1,0:T(8,128)(2,1)}, u32[]{:S(2)}) copy-start(bf16[4,128,256]{2,1,0:T(8,128)(2,1)} %get-tuple-element.29) | copy-start | bytes 786436
  50.1 0.6 copy-start.14
  50.1 0.7 copy-start.15
  50.8 8.6 %copy-start.9 = (s32[32,2]{0,1:T(2,128)S(1)}, s32[32,2]{0,1:T(2,128)}, u32[]{:S(2)}) copy-start(s32[32,2]{0,1:T(2,128)} %param.15) | copy-start | bytes 772
  57.1 9.4 %collective-permute-start.13 = (bf16[4,128,256]{2,1,0:T(8,128)(2,1)}, bf16[4,128,256]{2,1,0:T(8,128)(2,1)S(1)}, u32[]{:S(2)}, u32[]{:S(2)}) collective-permute-start(bf16[4,128,256]{2,1,0:T(8,128)(2,1)} %get-tuple-element.30), channel_id=1, source_target_pairs={{0,1},{1,0},{2,3},{3,2},{4,5},{5,4},{6,7},{7,6},{8,9},{9,8},{10,11... | collective-permute-start | bytes 786440 | tf_op jit(solution)/shard_map/ppermute | solution.py:246
  58.4 13.4 %collective-permute-start.12 = (bf16[4,128,256]{2,1,0:T(8,128)(2,1)S(1)}, bf16[4,128,256]{2,1,0:T(8,128)(2,1)S(1)}, u32[]{:S(2)}, u32[]{:S(2)}) collective-permute-start(bf16[4,128,256]{2,1,0:T(8,128)(2,1)S(1)} %copy-done.13), channel_id=1, source_target_pairs={{0,1},{1,0},{2,3},{3,2},{4,5},{5,4},{6,7},{7,6},{8,9},{9,8},{10,11... | collective-permute-start | bytes 786440 | tf_op jit(solution)/shard_map/ppermute | solution.py:246
  59.2 1.5 %copy-start = (bf16[4,128,128]{2,1,0:T(8,128)(2,1)}, bf16[4,128,128]{2,1,0:T(8,128)(2,1)S(1)}, u32[]{:S(2)}) copy-start(bf16[4,128,128]{2,1,0:T(8,128)(2,1)S(1)} %collective-permute-done.5.table_e2) | copy-start | bytes 393220
  59.2 1.5 %copy-start.1 = (bf16[4,128,128]{2,1,0:T(8,128)(2,1)}, bf16[4,128,128]{2,1,0:T(8,128)(2,1)S(1)}, u32[]{:S(2)}) copy-start(bf16[4,128,128]{2,1,0:T(8,128)(2,1)S(1)} %collective-permute-done.4.table_e1) | copy-start | bytes 393220
  59.2 1.4 %collective-permute-start.6 = (bf16[4,128,128]{2,1,0:T(8,128)(2,1)S(1)}, bf16[4,128,128]{2,1,0:T(8,128)(2,1)S(1)}, u32[]{:S(2)}, u32[]{:S(2)}) collective-permute-start(bf16[4,128,128]{2,1,0:T(8,128)(2,1)S(1)} %broadcast_select_fusion), channel_id=1, source_target_pairs={{0,2},{1,3},{2,0},{3,1},{4,6},{5,7},{6,4},{7,5},{8,10},{9,11},{10,... | collective-permute-start | bytes 393224 | tf_op jit(solution)/shard_map/ppermute | solution.py:246
  60.1 0.7 copy-start.5
  60.7 0.7 copy-start.7
  66.5 5.3 %copy-start.2 = (bf16[4,128,256]{2,1,0:T(8,128)(2,1)}, bf16[4,128,256]{2,1,0:T(8,128)(2,1)S(1)}, u32[]{:S(2)}) copy-start(bf16[4,128,256]{2,1,0:T(8,128)(2,1)S(1)} %collective-permute-done.13.rest_3_) | copy-start | bytes 786436
  71.8 0.7 copy-start.3

commit v2 on v1

--- a/solution.py
+++ b/solution.py
@@ -19,6 +19,8 @@
 AXES = ("tile", "comp")
 WHOLE = pl.BlockSpec()
 SMEM = pl.BlockSpec(memory_space=pltpu.SMEM)
+ANY = pl.BlockSpec(memory_space=pl.ANY)
+FINAL_STEPS = 4
 SENT = ((3, 9), (1, 3))
 MIXED = ((4, 8), (0, 4))
 
@@ -27,15 +29,15 @@
     return jax.ShapeDtypeStruct(shape, dtype)
 
 
-def call(kernel, out, ins, specs, scratch=(), flops=0, moved=1 << 20, name=None, **kw):
+def call(kernel, out, ins, specs, scratch=(), name=None, **kw):
     return pl.pallas_call(
         kernel,
         out_shape=out,
         in_specs=specs,
         out_specs=kw.pop("out_specs", jax.tree.map(lambda _: WHOLE, out)),
         scratch_shapes=list(scratch),
-        compiler_params=pltpu.CompilerParams(vmem_limit_bytes=60 << 20),
-        cost_estimate=pl.CostEstimate(flops=flops, bytes_accessed=moved, transcendentals=0),
+        compiler_params=pltpu.CompilerParams(vmem_limit_bytes=64 << 20),
+        cost_estimate=pl.CostEstimate(flops=0, bytes_accessed=0, transcendentals=0),
         name=name,
         **kw,
     )(*ins)
@@ -49,35 +51,45 @@
     return jnp.where(side == 0, j, ROWS - 1 - j)
 
 
-def prep_kernel(state, taps, atm_gain, ocean_gain, *rest):
-    sends, (head, keep, own_p, tall) = rest[: len(SENT)], rest[len(SENT) :]
+def taker(lines, side, take):
+    out = lax.broadcasted_iota(jnp.int32, (lines * 16, 256), 0)
+    into = lax.broadcasted_iota(jnp.int32, (lines * 16, 256), 1)
+    hit = ((out & 15) == (into >> 4)) & ((into & 15) == take(out >> 4))
+    return jnp.where(hit, 1.0, 0.0).astype(BF16)
+
+
+def head_kernel(state, ocean, taps, atm_gain, ocean_gain, head, own_p):
     side = side_of()
     gains = [g[...].astype(F32).reshape(1, HALF) for g in (atm_gain, ocean_gain)]
     own_p[...] = jnp.concatenate([taps[...], *gains, jnp.zeros((5, HALF), F32)], 0)
     high = own_p[...].astype(BF16)
     low = (own_p[...] - high.astype(F32)).astype(BF16)
-    head[HALF:, :LANES] = high
-    head[HALF:, LANES:] = low
-    for h in range(2):
-        part = state[:, :, h * LANES : (h + 1) * LANES].astype(F32)
-        tall[h] = part.reshape(HALF * ROWS, LANES)
-
-    def row(r):
-        parts = [tall.at[h][pl.ds(r, HALF, stride=ROWS), :] for h in range(2)]
-        return jnp.concatenate(parts, 1).astype(BF16)
-
-    for j in range(9):
-        keep[j] = row(row_at(j, side))
-        away = row(row_at(j, 1 - side))
-        if j == 0:
-            head[:HALF, :] = away
-        for (first, last), sent in zip(SENT, sends):
-            if first <= j < last:
-                sent[j - first] = away
+    head[384:, :LANES] = high
+    head[384:, LANES:] = low
+    head[:HALF, :] = ocean[:, :COLS]
+    head[HALF : 2 * HALF, :] = ocean[:, COLS:]
+    pick = taker(1, side, lambda n: row_at(0, 1 - side))
+    for b in range(HALF // 16):
+        block = state[16 * b : 16 * (b + 1)].reshape(256, COLS)
+        head[2 * HALF + 16 * b : 2 * HALF + 16 * (b + 1), :] = dot(pick, block).astype(BF16)
+
+
+def split_kernel(state, *rest):
+    sends, keep = rest[: len(SENT)], rest[len(SENT)]
+    side = side_of()
+    pick = taker(17, side, lambda n: jnp.where(n < 9, row_at(n, side), row_at(n - 8, 1 - side)))
+    for b in range(HALF // 16):
+        channels = slice(16 * b, 16 * (b + 1))
+        lines = dot(pick, state[channels].reshape(256, COLS)).astype(BF16)
+        for j in range(9):
+            keep[j, channels, :] = lines[16 * j : 16 * (j + 1)]
+            for (first, last), sent in zip(SENT, sends):
+                if first <= j < last:
+                    sent[j - first, channels, :] = lines[16 * (j + 8) : 16 * (j + 9)]
 
 
 def params_of(head):
-    return head[HALF:, :LANES].astype(F32) + head[HALF:, LANES:].astype(F32)
+    return head[384:, :LANES].astype(F32) + head[384:, LANES:].astype(F32)
 
 
 def gelu(x):
@@ -108,12 +120,13 @@
     return jnp.concatenate(halves, 1).T
 
 
-def ocean_kernel(mine, theirs, own_p, head, keep, up, down, kept, sent, pair, x):
+def ocean_kernel(mine, own_p, head, keep, up, down, kept, sent, pair, x):
     side = side_of()
     pair[0] = keep[0]
-    pair[1] = head[:HALF, :]
+    pair[1] = head[2 * HALF : 3 * HALF, :]
     gains = [own_p[...].T[:, 10:11], params_of(head).T[:, 10:11]]
-    own, other = normed([mine[...].astype(F32), theirs[...].astype(F32)], gains)
+    theirs = jnp.concatenate([head[:HALF, :], head[HALF : 2 * HALF, :]], 1)
+    own, other = normed([mine[...].astype(F32), theirs.astype(F32)], gains)
     x[:HALF, :] = own
     x[HALF:, :] = other
     total = None
@@ -143,7 +156,7 @@
 
     def fetch(place):
         ref, index = place
-        value = ins[ref][:HALF, :] if index is None else ins[ref][index]
+        value = ins[ref][2 * HALF : 3 * HALF, :] if index is None else ins[ref][index]
         return value.astype(F32)
 
     def conv(places, p):
@@ -158,16 +171,13 @@
         own, other = normed(values, [p[:, 9:10] for p in params])
         x[:HALF, i * COLS : (i + 1) * COLS] = own
         x[HALF:, i * COLS : (i + 1) * COLS] = other
-    for i in range(0, rows, 2):
-        cells = slice(i * COLS, (i + 2) * COLS)
-        delta = None
-        for j in range(4):
-            part = dot(blocks[4 + j], gelu(dot(blocks[j], x[:, cells])))
-            delta = part if delta is None else delta + part
-        for n in range(2):
-            value = delta[:, n * COLS : (n + 1) * COLS].astype(BF16)
-            kept[i + n] = value[:HALF]
-            sent[i + n] = value[HALF:]
+    up = blocks[:4].reshape(4 * 256, CHANNELS)
+    down = jnp.concatenate([blocks[4 + j] for j in range(4)], 1)
+    for i in range(rows):
+        hidden = gelu(dot(up, x[:, i * COLS : (i + 1) * COLS]))
+        value = dot(down, hidden).astype(BF16)
+        kept[i] = value[:HALF]
+        sent[i] = value[HALF:]
 
 
 def mix_first_kernel(rows, where_own, where_other, n_in, own_p, head, up, down, got_up, got_down, *rest):
@@ -185,22 +195,23 @@
     mix(rows, where_own, where_other, ins, own_p, head, blocks, kept, sent, x)
 
 
-def regrid_kernel(source, table_own, table_swap, table_e1, table_e2, table_last, w, out, table):
+def regrid_kernel(source, own, swap, e1, e2, swap_e1, swap_e2, w, later, out, table):
     step = pl.program_id(0)
     tile = lax.axis_index("tile")
     core, odd = lax.rem(tile, 2), lax.rem(tile // 2, 2)
 
     @pl.when(step == 0)
     def _():
-        for n, part in enumerate((table_own, table_swap, table_last, table_e1, table_e2)):
+        for n, part in enumerate((own, swap, e1, e2, swap_e1, swap_e2)):
             table[n * SLOTS : (n + 1) * SLOTS] = part[...]
 
     def slab(b, k):
-        slot = source[b, k]
+        slot = source[k, b]
         offset = slot // SLOTS - tile
-        near = jnp.where((offset > 0) == (core == 0), 1, 2)
-        far = jnp.where((offset > 0) == (odd == 1), 3, 4)
-        part = jnp.where(offset == 0, 0, jnp.where(abs(offset) == 1, near, far))
+        up = offset > 0
+        far = jnp.where(up == (odd == 1), 2, 3)
+        part = jnp.where(abs(offset) == 1, jnp.where(up == (core == 0), 1, far + 2), far)
+        part = jnp.where(offset == 0, 0, part)
         return table[part * SLOTS + lax.rem(slot, SLOTS)]
 
     per_step = w.shape[0]
@@ -209,24 +220,24 @@
         slabs = jnp.concatenate([slab(b, 0), slab(b, 1)], 1)
         weight = jnp.concatenate([w[n, 0], w[n, 1]], 1)
         value = lax.dot_general(slabs, weight, (((1,), (1,)), ((), ())), preferred_element_type=F32)
-        out[n // 2, :, (n % 2) * 128 : (n % 2 + 1) * 128] = value
+        out[n // 2, :, (n % 2) * 128 : (n % 2 + 1) * 128] = value.astype(BF16)
 
 
 def final_kernel(n, state, regrid, *rest):
-    kept, got, out, tall = rest[:n], rest[n : 2 * n], rest[2 * n], rest[2 * n + 1]
-    side = side_of()
-    depth = state.shape[0]
-    for refs, which in ((kept, side), (got, 1 - side)):
-        for (first, last), ref in zip(MIXED, refs):
-            for j in range(first, last):
-                r = row_at(j, which)
-                value = regrid[r] + ref[j - first].astype(F32)
-                for h in range(2):
-                    tall.at[h][pl.ds(r, depth, stride=ROWS), :] = value[:, h * LANES : (h + 1) * LANES]
-    for h in range(2):
-        lanes = slice(h * LANES, (h + 1) * LANES)
-        added = tall[h].reshape(depth, ROWS, LANES)
-        out[:, :, lanes] = (state[:, :, lanes].astype(F32) + added).astype(BF16)
+    kept, got, out = rest[:n], rest[n : 2 * n], rest[2 * n]
+    side = side_of()
+    place = taker(16, side, lambda n: jnp.where(n < 8, row_at(n, side), row_at(n - 8, 1 - side)))
+    place = jnp.concatenate([place.T, taker(16, side, lambda n: n).T], 1)
+    for b in range(state.shape[0] // 16):
+        channels = slice(16 * b, 16 * (b + 1))
+        lines = []
+        for refs in (kept, got):
+            for j in range(ROWS // 2):
+                k = [n for n, (p, q) in enumerate(MIXED) if p <= j < q][0]
+                lines.append(refs[k][j - MIXED[k][0], channels, :])
+        lines += [regrid[r, channels, :] for r in range(ROWS)]
+        added = dot(place, jnp.concatenate(lines, 0)).reshape(16, ROWS, COLS)
+        out[channels] = (state[channels].astype(F32) + added).astype(BF16)
 
 
 def on_device(
@@ -234,7 +245,6 @@
     atm_gain, atm_up, atm_down, ocean_gain, ocean_up, ocean_down,
 ):
     tiles = lax.axis_size("tile")
-    tile = lax.axis_index("tile")
 
     def move(x, to):
         route = []
@@ -253,30 +263,31 @@
     def across(x):
         return move(x, lambda t, c: (t ^ half_turn, 1 - c))
 
-    ocean_theirs = partner(ocean_state)
     got_up, got_down = across(atm_up), across(atm_down)
-    *sends, head_sent, keep, own_p = call(
-        prep_kernel,
-        [sds((b - a, HALF, COLS)) for a, b in SENT]
-        + [sds((HALF + 16, COLS)), sds((9, HALF, COLS)), sds((16, HALF), F32)],
-        (atm_state, dw_kernel, atm_gain, ocean_gain),
-        [WHOLE] * 4,
-        [pltpu.VMEM((2, HALF * ROWS, LANES), F32)],
-        moved=3 << 20,
-        name="prep",
+    head_sent, own_p = call(
+        head_kernel,
+        [sds((3 * HALF + 16, COLS)), sds((16, HALF), F32)],
+        (atm_state, ocean_state, dw_kernel, atm_gain, ocean_gain),
+        [WHOLE] * 5,
+        name="head",
     )
     head = partner(head_sent)
+    *sends, keep = call(
+        split_kernel,
+        [sds((b - a, HALF, COLS)) for a, b in SENT] + [sds((9, HALF, COLS))],
+        (atm_state,),
+        [WHOLE],
+        name="split",
+    )
     got = [partner(s) for s in sends]
 
     cells = ocean_state.shape[1]
     ocean_kept, ocean_sent, pair = call(
         ocean_kernel,
         [sds((HALF, cells), F32), sds((HALF, cells)), sds((2, HALF, COLS))],
-        (ocean_state, ocean_theirs, own_p, head, keep, ocean_up, ocean_down),
-        [WHOLE] * 7,
+        (ocean_state, own_p, head, keep, ocean_up, ocean_down),
+        [WHOLE] * 6,
         [pltpu.VMEM((256, cells), BF16)],
-        flops=2 * 2 * 256 * 512 * cells,
-        moved=2 << 20,
         name="ocean",
     )
     ocean_got = partner(ocean_sent)
@@ -286,14 +297,12 @@
         [sds((HALF, cells)), sds((SLOTS, HALF, CELLS_PER_TILE))],
         (ocean_count, ocean_state, ocean_kept, ocean_got),
         [SMEM, WHOLE, WHOLE, WHOLE],
-        moved=1 << 20,
         name="ocean_result",
     )
     swapped = move(slots, lambda t, c: (t ^ 1, c))
     e2 = move(slots, lambda t, c: (t ^ 2, c))
     e1 = move(slots, lambda t, c: (t + 2 if t // 2 % 2 else t - 2, c))
-    passed = jnp.where(tile % 2 == tile // 2 % 2, e2, e1)
-    last = move(passed, lambda t, c: (t ^ 1, c))
+    swap_e1, swap_e2 = [move(e, lambda t, c: (t ^ 1, c)) for e in (e1, e2)]
 
     kept_rows, got_rows, blocks = [], [], None
     for a, b in MIXED:
@@ -316,7 +325,6 @@
                 ins.append(got[k])
             where_other.append((place[0], j - SENT[k][0]))
         rows = b - a
-        cost = dict(flops=rows * COLS * 256 * 1024 * 4, moved=3 << 20)
         out = [sds((rows, HALF, COLS))] * 2
         x_spec = pltpu.VMEM((CHANNELS, rows * COLS), BF16)
         if blocks is None:
@@ -327,7 +335,6 @@
                 [WHOLE] * (6 + len(ins)),
                 [x_spec],
                 name="mix_first",
-                **cost,
             )
         else:
             kept, sent = call(
@@ -337,7 +344,6 @@
                 [WHOLE] * (3 + len(ins)),
                 [x_spec],
                 name="mix",
-                **cost,
             )
         kept_rows.append(kept)
         got_rows.append(partner(sent))
@@ -347,17 +353,15 @@
     table = pl.BlockSpec((SLOTS, HALF, CELLS_PER_TILE), lambda i: (0, 0, 0))
     regrid = call(
         regrid_kernel,
-        sds((ROWS, HALF, COLS), F32),
-        (regrid_src, slots, swapped, e1, e2, last, regrid_w),
-        [SMEM] + [table] * 5 + [pl.BlockSpec((per_step, 2, 128, 128), lambda i: (i, 0, 0, 0))],
-        [pltpu.VMEM((5 * SLOTS, HALF, CELLS_PER_TILE), BF16)],
+        sds((ROWS, HALF, COLS)),
+        (regrid_src.T, slots, swapped, e1, e2, swap_e1, swap_e2, regrid_w, got_rows[0]),
+        [SMEM] + [table] * 6 + [pl.BlockSpec((per_step, 2, 128, 128), lambda i: (i, 0, 0, 0)), ANY],
+        [pltpu.VMEM((6 * SLOTS, HALF, CELLS_PER_TILE), BF16)],
         grid=(steps,),
         out_specs=pl.BlockSpec((ROWS // steps, HALF, COLS), lambda i: (i, 0, 0)),
-        flops=32 * 2 * 128 * 256 * 128,
-        moved=5 << 20,
         name="regrid",
     )
-    depth = HALF // 4
+    depth = HALF // FINAL_STEPS
     rows_spec = [pl.BlockSpec((b - a, depth, COLS), lambda i: (0, i, 0)) for a, b in MIXED]
     state_spec = pl.BlockSpec((depth, ROWS, COLS), lambda i: (i, 0, 0))
     atm_out = call(
@@ -365,10 +369,8 @@
         sds((HALF, ROWS, COLS)),
         (atm_state, regrid, *kept_rows, *got_rows),
         [state_spec, pl.BlockSpec((ROWS, depth, COLS), lambda i: (0, i, 0))] + rows_spec * 2,
-        [pltpu.VMEM((2, depth * ROWS, LANES), F32)],
-        grid=(HALF // depth,),
+        grid=(FINAL_STEPS,),
         out_specs=state_spec,
-        moved=5 << 20,
         name="final",
     )
     return (atm_out, ocean_result)

time: 77.4 us -> 61.8 us (0.80)
  waiting for transfers between devices: 20.2 us -> 8.94 us
  local copies, waits for them, and re-layouts: 3.51 us -> 0 us
    ppermute x14, waiting for transfers between devices: 20.2 us -> 8.94 us  [move(): return lax.ppermute(x, AXES, route)]
    unnamed x33 -> x0, local copies, waits for them, and re-layouts: 3.51 us -> none
    pallas_call x7 -> x8, Pallas kernels: 30.3 us -> 29.9 us  [call(): pl.pallas_call(kernel, out_shape=out, in_specs=specs, out_specs=kw.pop('o...]
  transfers between devices with their start and end apart: 14 -> 14, of which waited for: 5 -> 5; matrix products, arithmetic and copies ran while one was open for 1% -> 0% of each run, Pallas kernels for 29% -> 38%
where the time goes in v2:
time: 61.8 us; the launch traced here: 61.3 us
  Pallas kernels  29.9 us (48%)
  starting transfers between devices  21.1 us (34%)
  waiting for transfers between devices  8.94 us (14%)
  between operations  1.32 us (2%)
    pallas_call x8, Pallas kernels, call(): pl.pallas_call(kernel, out_shape=out, in_specs=specs, out_specs=kw.pop('o...  29.9 us
    ppermute x14, starting transfers between devices, move(): return lax.ppermute(x, AXES, route)  21.1 us
    ppermute x14, waiting for transfers between devices, move(): return lax.ppermute(x, AXES, route)  8.94 us
  transfers between devices with their start and end apart: 14, of which 5 were waited for; matrix products, arithmetic and copies ran while one was open for 0% of the time, Pallas kernels for 38%

profile of v2, /device:TPU:24, one launch (start us, length us, event | category | flops | bytes accessed | tf_op | source)
XLA Modules:
  0.0 61.3 jit_solution(16971359224479016384)
XLA Ops:
  0.6 2.3 %head.1 = (bf16[400,256]{1,0:T(8,128)(2,1)}, f32[16,128]{1,0:T(8,128)}) custom-call(bf16[128,16,256]{2,1,0:T(8,128)(2,1)} %state.7, bf16[128,512]{1,0:T(8,128)(2,1)} %state.6, f32[9,128]{1,0:T(8,128)} %taps.1, bf16[128]{0:T(256)(128)(2,1)} %atm_gain.1, bf16[128]{0:T(256)(128)(2,1)} %ocean_gain.1), custom_call_target="tpu_custom_call" | custom-call | tf_op jit(solution)/shard_map/head/pallas_call | solution.py:33
  2.9 1.5 %collective-permute-start = (bf16[400,256]{1,0:T(8,128)(2,1)}, bf16[400,256]{1,0:T(8,128)(2,1)}, u32[]{:S(2)}, u32[]{:S(2)}) collective-permute-start(bf16[400,256]{1,0:T(8,128)(2,1)} %get-tuple-element.18), channel_id=1, source_target_pairs={{0,1},{1,0},{2,3},{3,2},{4,5},{5,4},{6,7},{7,6},{8,9},{9,8},{10,11... | collective-permute-start | bytes 614408 | tf_op jit(solution)/shard_map/ppermute | solution.py:256
  4.4 2.6 %split.1 = (bf16[6,128,256]{2,1,0:T(8,128)(2,1)}, bf16[2,128,256]{2,1,0:T(8,128)(2,1)}, bf16[9,128,256]{2,1,0:T(8,128)(2,1)}) custom-call(bf16[128,16,256]{2,1,0:T(8,128)(2,1)} %state.7), custom_call_target="tpu_custom_call" | custom-call | tf_op jit(solution)/shard_map/split/pallas_call | solution.py:33
  7.0 0.5 collective-permute-start.9
  7.6 2.8 %collective-permute-start.7 = (bf16[256,512]{1,0:T(8,128)(2,1)}, bf16[256,512]{1,0:T(8,128)(2,1)}, u32[]{:S(2)}, u32[]{:S(2)}) collective-permute-start(bf16[256,512]{1,0:T(8,128)(2,1)} %up.3), channel_id=1, source_target_pairs={{0,17},{1,16},{2,19},{3,18},{4,21},{5,20},{6,23},{7,22},{8,25},{9,... | collective-permute-start | bytes 786440 | tf_op jit(solution)/shard_map/ppermute | solution.py:256
  10.3 0.5 collective-permute-start.8
  10.8 0.0 collective-permute-done.head.rest_2_
  10.8 3.0 %ocean.3 = (f32[128,512]{1,0:T(8,128)}, bf16[128,512]{1,0:T(8,128)(2,1)}, bf16[2,128,256]{2,1,0:T(8,128)(2,1)}) custom-call(bf16[128,512]{1,0:T(8,128)(2,1)} %state.6, f32[16,128]{1,0:T(8,128)} %get-tuple-element.17.own_p, bf16[400,256]{1,0:T(8,128)(2,1)} %collective-permute-done.head.rest_2_, bf16[9,128,256]{2,1,0:T(8,128)(2,1)} %get-tuple-element.19.keep.rest_0_, ...), custom_call_target="tpu_custom_call" | custom-call | tf_op jit(solution)/shard_map/ocean/pallas_call | solution.py:33
  13.8 1.9 %collective-permute-start.1 = (bf16[128,512]{1,0:T(8,128)(2,1)}, bf16[128,512]{1,0:T(8,128)(2,1)}, u32[]{:S(2)}, u32[]{:S(2)}) collective-permute-start(bf16[128,512]{1,0:T(8,128)(2,1)} %get-tuple-element.21), channel_id=1, source_target_pairs={{0,1},{1,0},{2,3},{3,2},{4,5},{5,4},{6,7},{7,6},{8,9},{9,8},{10,11... | collective-permute-start | bytes 393224 | tf_op jit(solution)/shard_map/ppermute | solution.py:256
  15.7 0.2 collective-permute-start.12
  15.9 6.4 %collective-permute-done.1.got = bf16[128,512]{1,0:T(8,128)(2,1)} collective-permute-done((bf16[128,512]{1,0:T(8,128)(2,1)}, bf16[128,512]{1,0:T(8,128)(2,1)}, u32[]{:S(2)}, u32[]{:S(2)}) %collective-permute-start.1) | collective-permute-done | bytes 131104 | tf_op jit(solution)/shard_map/ppermute | solution.py:256
  22.2 5.9 %collective-permute-start.11 = (bf16[2,128,256]{2,1,0:T(8,128)(2,1)}, bf16[2,128,256]{2,1,0:T(8,128)(2,1)}, u32[]{:S(2)}, u32[]{:S(2)}) collective-permute-start(bf16[2,128,256]{2,1,0:T(8,128)(2,1)} %get-tuple-element.27), channel_id=1, source_target_pairs={{1,2},{2,1},{3,4},{4,3},{5,6},{6,5},{7,8},{8,7},{9,10},{10,9},{11,... | collective-permute-start | bytes 393224 | tf_op jit(solution)/shard_map/ppermute | solution.py:256
  28.8 1.8 %ocean_result.1 = (bf16[128,512]{1,0:T(8,128)(2,1)}, bf16[4,128,128]{2,1,0:T(8,128)(2,1)}) custom-call(s32[1]{0:T(128)S(6)} %copy.14.count, bf16[128,512]{1,0:T(8,128)(2,1)} %state.6, f32[128,512]{1,0:T(8,128)} %get-tuple-element.20.kept, bf16[128,512]{1,0:T(8,128)(2,1)} %collective-permute-done.1.got), custom_call_target="tpu_custom_call" | custom-call | tf_op jit(solution)/shard_map/ocean_result/pallas_call | solution.py:33
  30.6 0.0 collective-permute-done.7.got_up
  30.6 0.0 collective-permute-start.4
  30.6 0.0 collective-permute-done.8.got_down
  30.6 4.8 %collective-permute-start.3 = (bf16[4,128,128]{2,1,0:T(8,128)(2,1)}, bf16[4,128,128]{2,1,0:T(8,128)(2,1)}, u32[]{:S(2)}, u32[]{:S(2)}) collective-permute-start(bf16[4,128,128]{2,1,0:T(8,128)(2,1)} %get-tuple-element.22.own), channel_id=1, source_target_pairs={{4,8},{5,9},{6,10},{7,11},{8,4},{9,5},{10,6},{11,7},{12,16},{13,17... | collective-permute-start | bytes 393224 | tf_op jit(solution)/shard_map/ppermute | solution.py:256
  35.4 0.0 collective-permute-done.9.rest_1_.rest_4_
  35.4 5.7 %mix_first.1 = (bf16[4,128,256]{2,1,0:T(8,128)(2,1)}, bf16[4,128,256]{2,1,0:T(8,128)(2,1)}, bf16[8,256,256]{2,1,0:T(8,128)(2,1)}) custom-call(f32[16,128]{1,0:T(8,128)} %get-tuple-element.17.own_p, bf16[400,256]{1,0:T(8,128)(2,1)} %collective-permute-done.head.rest_2_, bf16[256,512]{1,0:T(8,128)(2,1)} %up.3, bf16[512,256]{1,0:T(8,128)(2,1)} %down.3, ...), custom_call_target="tpu_custom_call" | custom-call | tf_op jit(solution)/shard_map/mix_first/pallas_call | solution.py:33
  41.1 1.0 %collective-permute-start.10 = (bf16[4,128,256]{2,1,0:T(8,128)(2,1)}, bf16[4,128,256]{2,1,0:T(8,128)(2,1)}, u32[]{:S(2)}, u32[]{:S(2)}) collective-permute-start(bf16[4,128,256]{2,1,0:T(8,128)(2,1)} %get-tuple-element.24), channel_id=1, source_target_pairs={{0,1},{1,0},{2,3},{3,2},{4,5},{5,4},{6,7},{7,6},{8,9},{9,8},{10,11... | collective-permute-start | bytes 786440 | tf_op jit(solution)/shard_map/ppermute | solution.py:256
  42.1 0.0 collective-permute-done.12.rest_3_
  42.1 0.0 collective-permute-done.11.rest_1_
  42.1 5.5 %mix.1 = (bf16[4,128,256]{2,1,0:T(8,128)(2,1)}, bf16[4,128,256]{2,1,0:T(8,128)(2,1)}) custom-call(f32[16,128]{1,0:T(8,128)} %get-tuple-element.17.own_p, bf16[400,256]{1,0:T(8,128)(2,1)} %collective-permute-done.head.rest_2_, bf16[8,256,256]{2,1,0:T(8,128)(2,1)} %get-tuple-element.26.blocks, bf16[9,128,256]{2,1,0:T(8,128)(2,1)} %get-tuple-element.19.keep.rest_0_, ...), custom_call_target="tpu_custom_call" | custom-call | tf_op jit(solution)/shard_map/mix/pallas_call | solution.py:33
  47.6 1.0 %collective-permute-start.13 = (bf16[4,128,256]{2,1,0:T(8,128)(2,1)}, bf16[4,128,256]{2,1,0:T(8,128)(2,1)}, u32[]{:S(2)}, u32[]{:S(2)}) collective-permute-start(bf16[4,128,256]{2,1,0:T(8,128)(2,1)} %get-tuple-element.30), channel_id=1, source_target_pairs={{0,1},{1,0},{2,3},{3,2},{4,5},{5,4},{6,7},{7,6},{8,9},{9,8},{10,11... | collective-permute-start | bytes 786440 | tf_op jit(solution)/shard_map/ppermute | solution.py:256
  48.7 0.6 collective-permute-start.2
  49.2 0.0 collective-permute-done.4.e2
  49.2 0.0 collective-permute-start.6
  49.2 0.0 collective-permute-done.3.e1
  49.2 0.5 collective-permute-start.5
  49.8 0.8 %collective-permute-done.2.swap = bf16[4,128,128]{2,1,0:T(8,128)(2,1)} collective-permute-done((bf16[4,128,128]{2,1,0:T(8,128)(2,1)}, bf16[4,128,128]{2,1,0:T(8,128)(2,1)}, u32[]{:S(2)}, u32[]{:S(2)}) %collective-permute-start.2) | collective-permute-done | bytes 131104 | tf_op jit(solution)/shard_map/ppermute | solution.py:256
  50.6 0.4 collective-permute-done.6.swap_e2
  50.9 0.2 collective-permute-done.5.swap_e1
  51.1 0.0 collective-permute-done.10.later.rest_2_
  51.1 4.6 %regrid.1 = bf16[16,128,256]{2,1,0:T(8,128)(2,1)} custom-call(s32[2,32]{1,0:T(2,128)} %bitcast.1, bf16[4,128,128]{2,1,0:T(8,128)(2,1)} %get-tuple-element.22.own, bf16[4,128,128]{2,1,0:T(8,128)(2,1)} %collective-permute-done.2.swap, bf16[4,128,128]{2,1,0:T(8,128)(2,1)} %collective-permute-done.3.e1, bf16[4,128,128]{2,1,0:T(8,128)(2,1)} %collective-permute-done.4.e2, ...), custom_call_target="tpu_custom_call" | custom-call | tf_op jit(solution)/shard_map/regrid/pallas_call | solution.py:33
  55.7 1.2 %collective-permute-done.13.rest_3_ = bf16[4,128,256]{2,1,0:T(8,128)(2,1)} collective-permute-done((bf16[4,128,256]{2,1,0:T(8,128)(2,1)}, bf16[4,128,256]{2,1,0:T(8,128)(2,1)}, u32[]{:S(2)}, u32[]{:S(2)}) %collective-permute-start.13) | collective-permute-done | bytes 262176 | tf_op jit(solution)/shard_map/ppermute | solution.py:256
  56.9 4.4 %final.1 = bf16[128,16,256]{2,1,0:T(8,128)(2,1)} custom-call(bf16[128,16,256]{2,1,0:T(8,128)(2,1)} %state.7, bf16[16,128,256]{2,1,0:T(8,128)(2,1)} %regrid.1, bf16[4,128,256]{2,1,0:T(8,128)(2,1)} %get-tuple-element.25.rest_0_, bf16[4,128,256]{2,1,0:T(8,128)(2,1)} %get-tuple-element.29.rest_1_, bf16[4,128,256]{2,1,0:T(8,128)(2,1)} %collective-permute-done.10.later.rest_2_, ...), custom_call_target="tpu_custom_call" | custom-call | tf_op jit(solution)/shard_map/final/pallas_call | solution.py:33
Async XLA Ops:
  2.9 7.9 %collective-permute-start = (bf16[400,256]{1,0:T(8,128)(2,1)}, bf16[400,256]{1,0:T(8,128)(2,1)}, u32[]{:S(2)}, u32[]{:S(2)}) collective-permute-start(bf16[400,256]{1,0:T(8,128)(2,1)} %get-tuple-element.18), channel_id=1, source_target_pairs={{0,1},{1,0},{2,3},{3,2},{4,5},{5,4},{6,7},{7,6},{8,9},{9,8},{10,11... | collective-permute-start | bytes 614408 | tf_op jit(solution)/shard_map/ppermute | solution.py:256
  7.0 28.3 %collective-permute-start.9 = (bf16[6,128,256]{2,1,0:T(8,128)(2,1)}, bf16[6,128,256]{2,1,0:T(8,128)(2,1)}, u32[]{:S(2)}, u32[]{:S(2)}) collective-permute-start(bf16[6,128,256]{2,1,0:T(8,128)(2,1)} %get-tuple-element.23), channel_id=1, source_target_pairs={{0,1},{1,0},{2,3},{3,2},{4,5},{5,4},{6,7},{7,6},{8,9},{9,8},{10,11... | collective-permute-start | bytes 1179656 | tf_op jit(solution)/shard_map/ppermute | solution.py:256
  7.6 23.0 %collective-permute-start.7 = (bf16[256,512]{1,0:T(8,128)(2,1)}, bf16[256,512]{1,0:T(8,128)(2,1)}, u32[]{:S(2)}, u32[]{:S(2)}) collective-permute-start(bf16[256,512]{1,0:T(8,128)(2,1)} %up.3), channel_id=1, source_target_pairs={{0,17},{1,16},{2,19},{3,18},{4,21},{5,20},{6,23},{7,22},{8,25},{9,... | collective-permute-start | bytes 786440 | tf_op jit(solution)/shard_map/ppermute | solution.py:256
  10.3 20.3 %collective-permute-start.8 = (bf16[512,256]{1,0:T(8,128)(2,1)}, bf16[512,256]{1,0:T(8,128)(2,1)}, u32[]{:S(2)}, u32[]{:S(2)}) collective-permute-start(bf16[512,256]{1,0:T(8,128)(2,1)} %down.3), channel_id=1, source_target_pairs={{0,17},{1,16},{2,19},{3,18},{4,21},{5,20},{6,23},{7,22},{8,25},{9,... | collective-permute-start | bytes 786440 | tf_op jit(solution)/shard_map/ppermute | solution.py:256
  13.8 8.4 %collective-permute-start.1 = (bf16[128,512]{1,0:T(8,128)(2,1)}, bf16[128,512]{1,0:T(8,128)(2,1)}, u32[]{:S(2)}, u32[]{:S(2)}) collective-permute-start(bf16[128,512]{1,0:T(8,128)(2,1)} %get-tuple-element.21), channel_id=1, source_target_pairs={{0,1},{1,0},{2,3},{3,2},{4,5},{5,4},{6,7},{7,6},{8,9},{9,8},{10,11... | collective-permute-start | bytes 393224 | tf_op jit(solution)/shard_map/ppermute | solution.py:256
  15.7 26.5 %collective-permute-start.12 = (bf16[2,128,256]{2,1,0:T(8,128)(2,1)}, bf16[2,128,256]{2,1,0:T(8,128)(2,1)}, u32[]{:S(2)}, u32[]{:S(2)}) collective-permute-start(bf16[2,128,256]{2,1,0:T(8,128)(2,1)} %get-tuple-element.28), channel_id=1, source_target_pairs={{0,1},{1,0},{2,3},{3,2},{4,5},{5,4},{6,7},{7,6},{8,9},{9,8},{10,11... | collective-permute-start | bytes 393224 | tf_op jit(solution)/shard_map/ppermute | solution.py:256
  22.2 19.9 %collective-permute-start.11 = (bf16[2,128,256]{2,1,0:T(8,128)(2,1)}, bf16[2,128,256]{2,1,0:T(8,128)(2,1)}, u32[]{:S(2)}, u32[]{:S(2)}) collective-permute-start(bf16[2,128,256]{2,1,0:T(8,128)(2,1)} %get-tuple-element.27), channel_id=1, source_target_pairs={{1,2},{2,1},{3,4},{4,3},{5,6},{6,5},{7,8},{8,7},{9,10},{10,9},{11,... | collective-permute-start | bytes 393224 | tf_op jit(solution)/shard_map/ppermute | solution.py:256
  30.6 18.6 %collective-permute-start.4 = (bf16[4,128,128]{2,1,0:T(8,128)(2,1)}, bf16[4,128,128]{2,1,0:T(8,128)(2,1)}, u32[]{:S(2)}, u32[]{:S(2)}) collective-permute-start(bf16[4,128,128]{2,1,0:T(8,128)(2,1)} %get-tuple-element.22.own), channel_id=1, source_target_pairs={{0,4},{1,5},{2,6},{3,7},{4,0},{5,1},{6,2},{7,3},{8,12},{9,13},{10,... | collective-permute-start | bytes 393224 | tf_op jit(solution)/shard_map/ppermute | solution.py:256
  30.6 18.6 %collective-permute-start.3 = (bf16[4,128,128]{2,1,0:T(8,128)(2,1)}, bf16[4,128,128]{2,1,0:T(8,128)(2,1)}, u32[]{:S(2)}, u32[]{:S(2)}) collective-permute-start(bf16[4,128,128]{2,1,0:T(8,128)(2,1)} %get-tuple-element.22.own), channel_id=1, source_target_pairs={{4,8},{5,9},{6,10},{7,11},{8,4},{9,5},{10,6},{11,7},{12,16},{13,17... | collective-permute-start | bytes 393224 | tf_op jit(solution)/shard_map/ppermute | solution.py:256
  41.1 10.0 %collective-permute-start.10 = (bf16[4,128,256]{2,1,0:T(8,128)(2,1)}, bf16[4,128,256]{2,1,0:T(8,128)(2,1)}, u32[]{:S(2)}, u32[]{:S(2)}) collective-permute-start(bf16[4,128,256]{2,1,0:T(8,128)(2,1)} %get-tuple-element.24), channel_id=1, source_target_pairs={{0,1},{1,0},{2,3},{3,2},{4,5},{5,4},{6,7},{7,6},{8,9},{9,8},{10,11... | collective-permute-start | bytes 786440 | tf_op jit(solution)/shard_map/ppermute | solution.py:256
  47.6 9.3 %collective-permute-start.13 = (bf16[4,128,256]{2,1,0:T(8,128)(2,1)}, bf16[4,128,256]{2,1,0:T(8,128)(2,1)}, u32[]{:S(2)}, u32[]{:S(2)}) collective-permute-start(bf16[4,128,256]{2,1,0:T(8,128)(2,1)} %get-tuple-element.30), channel_id=1, source_target_pairs={{0,1},{1,0},{2,3},{3,2},{4,5},{5,4},{6,7},{7,6},{8,9},{9,8},{10,11... | collective-permute-start | bytes 786440 | tf_op jit(solution)/shard_map/ppermute | solution.py:256
  48.7 1.9 %collective-permute-start.2 = (bf16[4,128,128]{2,1,0:T(8,128)(2,1)}, bf16[4,128,128]{2,1,0:T(8,128)(2,1)}, u32[]{:S(2)}, u32[]{:S(2)}) collective-permute-start(bf16[4,128,128]{2,1,0:T(8,128)(2,1)} %get-tuple-element.22.own), channel_id=1, source_target_pairs={{0,2},{1,3},{2,0},{3,1},{4,6},{5,7},{6,4},{7,5},{8,10},{9,11},{10,... | collective-permute-start | bytes 393224 | tf_op jit(solution)/shard_map/ppermute | solution.py:256
  49.2 1.7 %collective-permute-start.6 = (bf16[4,128,128]{2,1,0:T(8,128)(2,1)}, bf16[4,128,128]{2,1,0:T(8,128)(2,1)}, u32[]{:S(2)}, u32[]{:S(2)}) collective-permute-start(bf16[4,128,128]{2,1,0:T(8,128)(2,1)} %collective-permute-done.4.e2), channel_id=1, source_target_pairs={{0,2},{1,3},{2,0},{3,1},{4,6},{5,7},{6,4},{7,5},{8,10},{9,11},{10,... | collective-permute-start | bytes 393224 | tf_op jit(solution)/shard_map/ppermute | solution.py:256
  49.2 1.9 %collective-permute-start.5 = (bf16[4,128,128]{2,1,0:T(8,128)(2,1)}, bf16[4,128,128]{2,1,0:T(8,128)(2,1)}, u32[]{:S(2)}, u32[]{:S(2)}) collective-permute-start(bf16[4,128,128]{2,1,0:T(8,128)(2,1)} %collective-permute-done.3.e1), channel_id=1, source_target_pairs={{0,2},{1,3},{2,0},{3,1},{4,6},{5,7},{6,4},{7,5},{8,10},{9,11},{10,... | collective-permute-start | bytes 393224 | tf_op jit(solution)/shard_map/ppermute | solution.py:256

commit v3 on v2

v3 whole, which is shorter than its diff:
```python
import functools

import jax
import jax.numpy as jnp
from jax import lax
from jax.experimental import pallas as pl
from jax.experimental.pallas import tpu as pltpu
from jax.sharding import PartitionSpec as P

CHANNELS = 256
HALF = 128
ROWS = 16
COLS = 256
LANES = 128
CELLS_PER_TILE = 128
SLOTS = 4
F32 = jnp.float32
BF16 = jnp.bfloat16
AXES = ("tile", "comp")
WHOLE = pl.BlockSpec()
SMEM = pl.BlockSpec(memory_space=pltpu.SMEM)
ANY = pl.BlockSpec(memory_space=pl.ANY)
FINAL_STEPS = 2
OCEAN_COST = 8 * 10**9
SENT = ((3, 9), (1, 3))
MIXED = ((4, 8), (0, 4))


def sds(shape, dtype=BF16):
    return jax.ShapeDtypeStruct(shape, dtype)


def call(kernel, out, ins, specs, scratch=(), name=None, flops=0, **kw):
    return pl.pallas_call(
        kernel,
        out_shape=out,
        in_specs=specs,
        out_specs=kw.pop("out_specs", jax.tree.map(lambda _: WHOLE, out)),
        scratch_shapes=list(scratch),
        compiler_params=pltpu.CompilerParams(vmem_limit_bytes=64 << 20),
        cost_estimate=pl.CostEstimate(flops=flops, bytes_accessed=0, transcendentals=0),
        name=name,
        **kw,
    )(*ins)


def half_of():
    return lax.axis_index("comp")


def side_of():
    return lax.rem(lax.axis_index("comp") + lax.axis_index("tile"), 2)


def row_at(j, side):
    return jnp.where(side == 0, j, ROWS - 1 - j)


def taker(lines, side, take):
    out = lax.broadcasted_iota(jnp.int32, (lines * 16, 256), 0)
    into = lax.broadcasted_iota(jnp.int32, (lines * 16, 256), 1)
    hit = ((out & 15) == (into >> 4)) & ((into & 15) == take(out >> 4))
    return jnp.where(hit, 1.0, 0.0).astype(BF16)


def open_kernel(state, taps, atm_gain, ocean_gain, head, own_p, *rest):
    sends, keep = rest[: len(SENT)], rest[len(SENT)]
    side = side_of()
    gains = [g[...].astype(F32).reshape(1, HALF) for g in (atm_gain, ocean_gain)]
    own_p[...] = jnp.concatenate([taps[...], *gains, jnp.zeros((5, HALF), F32)], 0)
    high = own_p[...].astype(BF16)
    low = (own_p[...] - high.astype(F32)).astype(BF16)
    head[HALF:, :LANES] = high
    head[HALF:, LANES:] = low
    pick = taker(18, side, lambda n: jnp.where(n < 9, row_at(n, side), row_at(n - 9, 1 - side)))
    for b in range(HALF // 16):
        channels = slice(16 * b, 16 * (b + 1))
        lines = dot(pick, state[channels].reshape(256, COLS)).astype(BF16)
        head[channels, :] = lines[16 * 9 : 16 * 10]
        for j in range(9):
            keep[j, channels, :] = lines[16 * j : 16 * (j + 1)]
            for (first, last), sent in zip(SENT, sends):
                if first <= j < last:
                    sent[j - first, channels, :] = lines[16 * (j + 9) : 16 * (j + 10)]


def params_of(head):
    return head[HALF:, :LANES].astype(F32) + head[HALF:, LANES:].astype(F32)


def gelu(x):
    inner = x * (0.7978845608028654 + 0.035677408136300125 * (x * x))
    return (x * (0.5 + 0.5 * jnp.tanh(inner))).astype(BF16)


def dot(a, b):
    return jnp.dot(a, b, preferred_element_type=F32)


def normed(values, gains):
    total = sum(jnp.sum(v, 0, keepdims=True) for v in values)
    squares = sum(jnp.sum(v * v, 0, keepdims=True) for v in values)
    center = total / CHANNELS
    spread = squares / CHANNELS - center * center
    scale = lax.rsqrt(spread + 1e-06)
    return [((v - center) * scale * g).astype(BF16) for v, g in zip(values, gains)]


def turned_up(up, j, half):
    halves = [up[pl.ds(pl.multiple_of(s * HALF, HALF), HALF), j * 256 : (j + 1) * 256] for s in (half, 1 - half)]
    return jnp.concatenate(halves, 0).T


def turned_down(down, j, half):
    halves = [down[j * 256 : (j + 1) * 256, pl.ds(pl.multiple_of(s * HALF, HALF), HALF)] for s in (half, 1 - half)]
    return jnp.concatenate(halves, 1).T


def ocean_kernel(mine, theirs, own_p, head, keep, up, down, passing, kept, sent, pair, passed, x):
    pair[0] = keep[0]
    pair[1] = head[:HALF, :]
    gains = [own_p[...].T[:, 10:11], params_of(head).T[:, 10:11]]
    own, other = normed([mine[...].astype(F32), theirs[...].astype(F32)], gains)
    x[:HALF, :] = own
    x[HALF:, :] = other
    total = None
    for j in range(2):
        hidden = gelu(dot(turned_up(up, j, half_of()), x[...]))
        part = dot(turned_down(down, j, half_of()), hidden)
        total = part if total is None else total + part
    kept[...] = total[:HALF]
    sent[...] = total[HALF:].astype(BF16)


def start(pairs, sems, at):
    moves = [pltpu.make_async_copy(src, dst, sems.at[at + n]) for n, (src, dst) in enumerate(pairs)]
    for m in moves:
        m.start()
    return moves


def wait(moves):
    for m in moves:
        m.wait()


def mix_kernel(rows, runs_own, runs_other, n_in, leads, *refs):
    refs = list(refs)
    take = lambda n: [refs.pop(0) for _ in range(n)]
    (count,) = take(1) if leads else (None,)
    own_p, head, *weights = take(6 if leads else 3)
    take(0 if leads else 1)
    ocean_ins = take(3) if leads else []
    ins = take(n_in)
    kept, sent = take(2)
    blocks_out, result, slots = take(3) if leads else (None, None, None)
    own_pv, head_pv, own_lines, other_lines, x, blocks, kept_v, sent_v, sems = take(9)
    side = side_of()

    def lines_of(runs, lines):
        for ref, src, n, dst in runs:
            if src is None:
                yield ins[ref].at[pl.ds(0, HALF)], lines.at[dst]
            else:
                yield ins[ref].at[pl.ds(src, n)], lines.at[pl.ds(dst, n)]

    pairs = [(own_p, own_pv), (head.at[pl.ds(HALF, 16)], head_pv)]
    pairs += [*lines_of(runs_own, own_lines), *lines_of(runs_other, other_lines)]
    loads = start(pairs, sems, 0)
    used = len(pairs)
    if leads:
        raw, ocean_v, (result_v, slots_v) = take(4), take(3), take(2)
        ocean_loads = start(list(zip(ocean_ins, ocean_v)), sems, used)
        weight_loads = start(list(zip(weights, raw)), sems, used + 3)
        used += 7
    else:
        weight_loads = start([(weights[0], blocks)], sems, used)
        used += 1
    wait(loads)
    params = []
    for taps in (own_pv[...], head_pv[:, :LANES].astype(F32) + head_pv[:, LANES:].astype(F32)):
        flipped = jnp.concatenate([taps[6:9], taps[3:6], taps[0:3], taps[9:]], 0)
        params.append(jnp.where(side == 0, taps, flipped).T)

    def conv(lines, i, p):
        near = [lines[i + a].astype(F32) for a in range(3)]
        left, middle, right = [
            sum(p[:, 3 * a + b : 3 * a + b + 1] * near[a] for a in range(3)) for b in range(3)
        ]
        return middle + pltpu.roll(left, 1, 1) + pltpu.roll(right, COLS - 1, 1)

    for i in range(rows):
        values = [conv(own_lines, i, params[0]), conv(other_lines, i, params[1])]
        own, other = normed(values, [p[:, 9:10] for p in params])
        x[:HALF, i * COLS : (i + 1) * COLS] = own
        x[HALF:, i * COLS : (i + 1) * COLS] = other
    stores = []
    if leads:
        wait(ocean_loads)
        for s in range(SLOTS):
            cells = slice(s * CELLS_PER_TILE, (s + 1) * CELLS_PER_TILE)
            value = ocean_v[0][:, cells].astype(F32) + (ocean_v[1][:, cells] + ocean_v[2][:, cells].astype(F32))
            value = jnp.where(s < count[0], value, 0.0).astype(BF16)
            result_v[:, cells] = value
            slots_v[s] = value
        stores += start([(result_v, result), (slots_v, slots)], sems, used)
        used += 2
    wait(weight_loads)
    if leads:
        for n, (u, d) in enumerate((raw[:2], raw[2:])):
            for j in range(2):
                blocks[2 * n + j] = turned_up(u, j, half_of())
                blocks[4 + 2 * n + j] = turned_down(d, j, half_of())
        stores += start([(blocks, blocks_out)], sems, used)
        used += 1
    up = blocks[:4].reshape(4 * 256, CHANNELS)
    down = jnp.concatenate([blocks[4 + j] for j in range(4)], 1)
    for i in range(rows):
        hidden = gelu(dot(up, x[:, i * COLS : (i + 1) * COLS]))
        value = dot(down, hidden).astype(BF16)
        kept_v[i] = value[:HALF]
        sent_v[i] = value[HALF:]
        stores += start([(sent_v.at[i], sent.at[i]), (kept_v.at[i], kept.at[i])], sems, used)
        used += 2
    wait(stores)


def regrid_kernel(source, own, swap, e1, e2, swap_e1, swap_e2, w, later, out, table):
    step = pl.program_id(0)
    tile = lax.axis_index("tile")
    core, odd = lax.rem(tile, 2), lax.rem(tile // 2, 2)

    @pl.when(step == 0)
    def _():
        for n, part in enumerate((own, swap, e1, e2, swap_e1, swap_e2)):
            table[n * SLOTS : (n + 1) * SLOTS] = part[...]

    def slab(b, k):
        slot = source[k, b]
        offset = slot // SLOTS - tile
        up = offset > 0
        far = jnp.where(up == (odd == 1), 2, 3)
        part = jnp.where(abs(offset) == 1, jnp.where(up == (core == 0), 1, far + 2), far)
        part = jnp.where(offset == 0, 0, part)
        return table[part * SLOTS + lax.rem(slot, SLOTS)]

    per_step = w.shape[0]
    for n in range(per_step):
        b = step * per_step + n
        slabs = jnp.concatenate([slab(b, 0), slab(b, 1)], 1)
        weight = jnp.concatenate([w[n, 0], w[n, 1]], 1)
        value = lax.dot_general(slabs, weight, (((1,), (1,)), ((), ())), preferred_element_type=F32)
        out[n // 2, :, (n % 2) * 128 : (n % 2 + 1) * 128] = value.astype(BF16)


def final_kernel(n, state, regrid, *rest):
    kept, got, out = rest[:n], rest[n : 2 * n], rest[2 * n]
    side = side_of()
    place = taker(16, side, lambda n: jnp.where(n < 8, row_at(n, side), row_at(n - 8, 1 - side)))
    place = jnp.concatenate([place.T, taker(16, side, lambda n: n).T], 1)
    for b in range(state.shape[0] // 16):
        channels = slice(16 * b, 16 * (b + 1))
        lines = []
        for refs in (kept, got):
            for j in range(ROWS // 2):
                k = [n for n, (p, q) in enumerate(MIXED) if p <= j < q][0]
                lines.append(refs[k][j - MIXED[k][0], channels, :])
        lines += [regrid[r, channels, :] for r in range(ROWS)]
        added = dot(place, jnp.concatenate(lines, 0)).reshape(16, ROWS, COLS)
        out[channels] = (state[channels].astype(F32) + added).astype(BF16)


def on_device(
    atm_state, ocean_state, ocean_count, regrid_src, regrid_w, dw_kernel,
    atm_gain, atm_up, atm_down, ocean_gain, ocean_up, ocean_down,
):
    tiles = lax.axis_size("tile")

    def move(x, to):
        route = []
        for t in range(tiles):
            for c in range(2):
                u, d = to(t, c)
                if 0 <= u < tiles:
                    route.append((t * 2 + c, u * 2 + d))
        return lax.ppermute(x, AXES, route)

    def partner(x):
        return move(x, lambda t, c: (t, 1 - c))

    half_turn = 8 if tiles >= 16 else 0

    def across(x):
        return move(x, lambda t, c: (t ^ half_turn, 1 - c))

    got_up, got_down = across(atm_up), across(atm_down)
    ocean_theirs = partner(ocean_state)
    head_sent, own_p, *sends, keep = call(
        open_kernel,
        [sds((HALF + 16, COLS)), sds((16, HALF), F32)]
        + [sds((b - a, HALF, COLS)) for a, b in SENT]
        + [sds((9, HALF, COLS))],
        (atm_state, dw_kernel, atm_gain, ocean_gain),
        [WHOLE] * 4,
        name="open",
    )
    head = partner(head_sent)
    cells = ocean_state.shape[1]
    ocean_kept, ocean_sent, pair, last_sent = call(
        ocean_kernel,
        [sds((HALF, cells), F32), sds((HALF, cells)), sds((2, HALF, COLS)), sds(sends[-1].shape)],
        (ocean_state, ocean_theirs, own_p, head, keep, ocean_up, ocean_down, sends[-1]),
        [WHOLE] * 7 + [ANY],
        [pltpu.VMEM((256, cells), BF16)],
        out_specs=[WHOLE] * 3 + [ANY],
        input_output_aliases={7: 3},
        name="ocean",
        flops=OCEAN_COST,
    )
    got = [partner(s) for s in (*sends[:-1], last_sent)]
    ocean_got = partner(ocean_sent)
    edges = move(pair, lambda t, c: (t - 1 + 2 * ((t + c) % 2), c))
    kept_rows, got_rows, blocks = [], [], None
    for a, b in MIXED:
        ins, runs_own, runs_other = [keep], [], []
        first = max(a - 1, 0)
        if a == 0:
            runs_own.append((1, 0, 1, 0))
            runs_other += [(1, 1, 1, 0), (2, None, 1, 1)]
            ins += [edges, head]
        runs_own.append((0, first, b + 1 - first, first - a + 1))
        for (p, q), g in zip(SENT, got):
            p, q = max(p, first), min(q, b + 1)
            if p < q:
                runs_other.append((len(ins), p - SENT[[x is g for x in got].index(True)][0], q - p, p - a + 1))
                ins.append(g)
        rows, leads = b - a, blocks is None
        lead_ins = (atm_up, atm_down, got_up, got_down, ocean_state, ocean_kept, ocean_got)
        out = [sds((rows, HALF, COLS))] * 2
        scratch = [
            pltpu.VMEM((16, HALF), F32),
            pltpu.VMEM((16, COLS), BF16),
            pltpu.VMEM((rows + 2, HALF, COLS), BF16),
            pltpu.VMEM((rows + 2, HALF, COLS), BF16),
            pltpu.VMEM((CHANNELS, rows * COLS), BF16),
            pltpu.VMEM((8, 256, 256), BF16),
            pltpu.VMEM((rows, HALF, COLS), BF16),
            pltpu.VMEM((rows, HALF, COLS), BF16),
            pltpu.SemaphoreType.DMA((40,)),
        ]
        if leads:
            out += [sds((8, 256, 256)), sds((HALF, cells)), sds((SLOTS, HALF, CELLS_PER_TILE))]
            scratch += [pltpu.VMEM(w.shape, w.dtype) for w in lead_ins]
            scratch += [pltpu.VMEM((HALF, cells), BF16), pltpu.VMEM((SLOTS, HALF, CELLS_PER_TILE), BF16)]
        args = (ocean_count, own_p, head, *lead_ins, *ins) if leads else (own_p, head, blocks, swapped, *ins)
        kept, sent, *more = call(
            functools.partial(mix_kernel, rows, runs_own, runs_other, len(ins), leads),
            out,
            args,
            ([SMEM] if leads else []) + [ANY] * (len(args) - leads),
            scratch,
            out_specs=[ANY] * len(out),
            name="mix",
        )
        if leads:
            blocks, ocean_result, slots = more
            swapped = move(slots, lambda t, c: (t ^ 1, c))
        kept_rows.append(kept)
        got_rows.append(partner(sent))
    e2 = move(slots, lambda t, c: (t ^ 2, c))
    e1 = move(slots, lambda t, c: (t + 2 if t // 2 % 2 else t - 2, c))
    swap_e1, swap_e2 = [move(e, lambda t, c: (t ^ 1, c)) for e in (e1, e2)]

    steps = 2
    per_step = regrid_src.shape[0] // steps
    table = pl.BlockSpec((SLOTS, HALF, CELLS_PER_TILE), lambda i: (0, 0, 0))
    regrid = call(
        regrid_kernel,
        sds((ROWS, HALF, COLS)),
        (regrid_src.T, slots, swapped, e1, e2, swap_e1, swap_e2, regrid_w, got_rows[0]),
        [SMEM] + [table] * 6 + [pl.BlockSpec((per_step, 2, 128, 128), lambda i: (i, 0, 0, 0)), ANY],
        [pltpu.VMEM((6 * SLOTS, HALF, CELLS_PER_TILE), BF16)],
        grid=(steps,),
        out_specs=pl.BlockSpec((ROWS // steps, HALF, COLS), lambda i: (i, 0, 0)),
        name="regrid",
    )
    depth = HALF // FINAL_STEPS
    rows_spec = [pl.BlockSpec((b - a, depth, COLS), lambda i: (0, i, 0)) for a, b in MIXED]
    state_spec = pl.BlockSpec((depth, ROWS, COLS), lambda i: (i, 0, 0))
    atm_out = call(
        functools.partial(final_kernel, len(MIXED)),
        sds((HALF, ROWS, COLS)),
        (atm_state, regrid, *kept_rows, *got_rows),
        [state_spec, pl.BlockSpec((ROWS, depth, COLS), lambda i: (0, i, 0))] + rows_spec * 2,
        grid=(FINAL_STEPS,),
        out_specs=state_spec,
        name="final",
    )
    return (atm_out, ocean_result)


def solution(mesh):
    return jax.shard_map(
        on_device,
        mesh=mesh,
        in_specs=(
            P("comp", "tile", None),
            P("comp", "tile"),
            P("tile"),
            P("tile", None),
            P("tile", None, None, None),
            P(None, "comp"),
            P("comp"),
            P(None, "comp"),
            P("comp", None),
            P("comp"),
            P(None, "comp"),
            P("comp", None),
        ),
        out_specs=(P("comp", "tile", None), P("comp", "tile")),
        check_vma=False,
    )
```

time: 61.8 us -> 55.5 us (0.90)
  the two profiles are of different devices: /device:TPU:24 before, /device:TPU:26 now
where the time goes in v3:
time: 55.5 us; the launch traced here: 55.2 us
  Pallas kernels  23.2 us (42%)
  starting transfers between devices  20.7 us (37%)
  waiting for transfers between devices  9.95 us (18%)
  between operations  1.36 us (2%)
    pallas_call x6, Pallas kernels, call(): pl.pallas_call(kernel, out_shape=out, in_specs=specs, out_specs=kw.pop('o...  23.2 us
    ppermute x15, starting transfers between devices, move(): return lax.ppermute(x, AXES, route)  20.7 us
    ppermute x15, waiting for transfers between devices, move(): return lax.ppermute(x, AXES, route)  9.95 us
  transfers between devices with their start and end apart: 15, of which 6 were waited for; matrix products, arithmetic and copies ran while one was open for 0% of the time, Pallas kernels for 36%

profile of v3, /device:TPU:26, one launch (start us, length us, event | category | flops | bytes accessed | tf_op | source)
XLA Modules:
  0.0 55.2 jit_solution(6718041923377668123)
XLA Ops:
  0.6 0.6 %collective-permute-start.3 = (bf16[128,512]{1,0:T(8,128)(2,1)}, bf16[128,512]{1,0:T(8,128)(2,1)}, u32[]{:S(2)}, u32[]{:S(2)}) collective-permute-start(bf16[128,512]{1,0:T(8,128)(2,1)} %refs_7_.1), channel_id=1, source_target_pairs={{0,1},{1,0},{2,3},{3,2},{4,5},{5,4},{6,7},{7,6},{8,9},{9,8},{10,11... | collective-permute-start | bytes 393224 | tf_op jit(solution)/shard_map/ppermute | solution.py:286
  1.2 2.7 %open.1 = (bf16[144,256]{1,0:T(8,128)(2,1)}, f32[16,128]{1,0:T(8,128)}, bf16[6,128,256]{2,1,0:T(8,128)(2,1)}, bf16[2,128,256]{2,1,0:T(8,128)(2,1)}, bf16[9,128,256]{2,1,0:T(8,128)(2,1)}) custom-call(bf16[128,16,256]{2,1,0:T(8,128)(2,1)} %state.3, f32[9,128]{1,0:T(8,128)} %taps.1, bf16[128]{0:T(256)(128)(2,1)} %atm_gain.1, bf16[128]{0:T(256)(128)(2,1)} %ocean_gain.1), custom_call_target="tpu_custom_call" | custom-call | tf_op jit(solution)/shard_map/open/pallas_call | solution.py:34
  4.0 1.5 %collective-permute-start = (bf16[144,256]{1,0:T(8,128)(2,1)}, bf16[144,256]{1,0:T(8,128)(2,1)}, u32[]{:S(2)}, u32[]{:S(2)}) collective-permute-start(bf16[144,256]{1,0:T(8,128)(2,1)} %get-tuple-element.19), channel_id=1, source_target_pairs={{0,1},{1,0},{2,3},{3,2},{4,5},{5,4},{6,7},{7,6},{8,9},{9,8},{10,11... | collective-permute-start | bytes 221192 | tf_op jit(solution)/shard_map/ppermute | solution.py:286
  5.4 0.5 collective-permute-start.5
  6.0 2.2 %collective-permute-start.1 = (bf16[256,512]{1,0:T(8,128)(2,1)}, bf16[256,512]{1,0:T(8,128)(2,1)}, u32[]{:S(2)}, u32[]{:S(2)}) collective-permute-start(bf16[256,512]{1,0:T(8,128)(2,1)} %refs_3_.1), channel_id=1, source_target_pairs={{0,17},{1,16},{2,19},{3,18},{4,21},{5,20},{6,23},{7,22},{8,25},{9,... | collective-permute-start | bytes 786440 | tf_op jit(solution)/shard_map/ppermute | solution.py:286
  8.1 0.0 collective-permute-start.2
  8.2 1.2 %collective-permute-done.head.refs_2_.refs_1_.refs_6_ = bf16[144,256]{1,0:T(8,128)(2,1)} collective-permute-done((bf16[144,256]{1,0:T(8,128)(2,1)}, bf16[144,256]{1,0:T(8,128)(2,1)}, u32[]{:S(2)}, u32[]{:S(2)}) %collective-permute-start) | collective-permute-done | bytes 73760 | tf_op jit(solution)/shard_map/ppermute | solution.py:286
  9.4 0.0 collective-permute-done.3.theirs
  9.4 3.1 %ocean.1 = (f32[128,512]{1,0:T(8,128)}, bf16[128,512]{1,0:T(8,128)(2,1)}, bf16[2,128,256]{2,1,0:T(8,128)(2,1)}, bf16[2,128,256]{2,1,0:T(8,128)(2,1)}) custom-call(bf16[128,512]{1,0:T(8,128)(2,1)} %refs_7_.1, bf16[128,512]{1,0:T(8,128)(2,1)} %collective-permute-done.3.theirs, ...), custom_call_target="tpu_custom_call", output_to_operand_aliasing={{3}: (7, {})} | custom-call | flops 8000000000 | tf_op jit(solution)/shard_map/ocean/pallas_call | solution.py:34
  12.5 1.5 %collective-permute-start.4 = (bf16[128,512]{1,0:T(8,128)(2,1)}, bf16[128,512]{1,0:T(8,128)(2,1)}, u32[]{:S(2)}, u32[]{:S(2)}) collective-permute-start(bf16[128,512]{1,0:T(8,128)(2,1)} %get-tuple-element.23), channel_id=1, source_target_pairs={{0,1},{1,0},{2,3},{3,2},{4,5},{5,4},{6,7},{7,6},{8,9},{9,8},{10,11... | collective-permute-start | bytes 393224 | tf_op jit(solution)/shard_map/ppermute | solution.py:286
  14.7 1.9 %collective-permute-start.12 = (bf16[2,128,256]{2,1,0:T(8,128)(2,1)}, bf16[2,128,256]{2,1,0:T(8,128)(2,1)}, u32[]{:S(2)}, u32[]{:S(2)}) collective-permute-start(bf16[2,128,256]{2,1,0:T(8,128)(2,1)} %get-tuple-element.29), channel_id=1, source_target_pairs={{1,3},{2,4},{3,1},{4,2},{5,7},{6,8},{7,5},{8,6},{9,11},{10,12},{11... | collective-permute-start | bytes 393224 | tf_op jit(solution)/shard_map/ppermute | solution.py:286
  16.6 3.1 %collective-permute-done.4.refs_9_ = bf16[128,512]{1,0:T(8,128)(2,1)} collective-permute-done((bf16[128,512]{1,0:T(8,128)(2,1)}, bf16[128,512]{1,0:T(8,128)(2,1)}, u32[]{:S(2)}, u32[]{:S(2)}) %collective-permute-start.4) | collective-permute-done | bytes 131104 | tf_op jit(solution)/shard_map/ppermute | solution.py:286
  19.7 1.8 %collective-permute-start.13 = (bf16[2,128,256]{2,1,0:T(8,128)(2,1)}, bf16[2,128,256]{2,1,0:T(8,128)(2,1)}, u32[]{:S(2)}, u32[]{:S(2)}) collective-permute-start(bf16[2,128,256]{2,1,0:T(8,128)(2,1)} %get-tuple-element.30), channel_id=1, source_target_pairs={{0,1},{1,0},{2,3},{3,2},{4,5},{5,4},{6,7},{7,6},{8,9},{9,8},{10,11... | collective-permute-start | bytes 393224 | tf_op jit(solution)/shard_map/ppermute | solution.py:286
  21.4 0.0 collective-permute-done.1.refs_5_
  21.4 0.0 collective-permute-done.2.refs_6_
  21.4 0.0 collective-permute-done.5.refs_11_.refs_7_
  21.4 5.4 %mix.2 = (bf16[4,128,256]{2,1,0:T(8,128)(2,1)}, bf16[4,128,256]{2,1,0:T(8,128)(2,1)}, bf16[8,256,256]{2,1,0:T(8,128)(2,1)}, bf16[128,512]{1,0:T(8,128)(2,1)}, bf16[4,128,128]{2,1,0:T(8,128)(2,1)}) custom-call(s32[1]{0:T(128)S(6)} %copy.16.refs_0_, f32[16,128]{1,0:T(8,128)} %get-tuple-element.18.own_p.refs_1_.refs_0_, ...), custom_call_target="tpu_custom_call" | custom-call | tf_op jit(solution)/shard_map/mix/pallas_call | solution.py:34
  26.8 0.1 collective-permute-start.6
  26.9 1.3 %collective-permute-start.8 = (bf16[4,128,128]{2,1,0:T(8,128)(2,1)}, bf16[4,128,128]{2,1,0:T(8,128)(2,1)}, u32[]{:S(2)}, u32[]{:S(2)}) collective-permute-start(bf16[4,128,128]{2,1,0:T(8,128)(2,1)} %get-tuple-element.25.own), channel_id=1, source_target_pairs={{0,4},{1,5},{2,6},{3,7},{4,0},{5,1},{6,2},{7,3},{8,12},{9,13},{10,... | collective-permute-start | bytes 393224 | tf_op jit(solution)/shard_map/ppermute | solution.py:286
  28.2 6.2 %collective-permute-start.7 = (bf16[4,128,128]{2,1,0:T(8,128)(2,1)}, bf16[4,128,128]{2,1,0:T(8,128)(2,1)}, u32[]{:S(2)}, u32[]{:S(2)}) collective-permute-start(bf16[4,128,128]{2,1,0:T(8,128)(2,1)} %get-tuple-element.25.own), channel_id=1, source_target_pairs={{4,8},{5,9},{6,10},{7,11},{8,4},{9,5},{10,6},{11,7},{12,16},{13,17... | collective-permute-start | bytes 393224 | tf_op jit(solution)/shard_map/ppermute | solution.py:286
  34.4 0.0 collective-permute-done.12.refs_5_
  34.4 2.4 %collective-permute-start.11 = (bf16[4,128,256]{2,1,0:T(8,128)(2,1)}, bf16[4,128,256]{2,1,0:T(8,128)(2,1)}, u32[]{:S(2)}, u32[]{:S(2)}) collective-permute-start(bf16[4,128,256]{2,1,0:T(8,128)(2,1)} %get-tuple-element.26), channel_id=1, source_target_pairs={{0,1},{1,0},{2,3},{3,2},{4,5},{5,4},{6,7},{7,6},{8,9},{9,8},{10,11... | collective-permute-start | bytes 786440 | tf_op jit(solution)/shard_map/ppermute | solution.py:286
  36.8 0.0 collective-permute-done.13.refs_8_
  36.8 0.0 collective-permute-done.6.swap.refs_3_
  36.8 5.3 %mix.3 = (bf16[4,128,256]{2,1,0:T(8,128)(2,1)}, bf16[4,128,256]{2,1,0:T(8,128)(2,1)}) custom-call(f32[16,128]{1,0:T(8,128)} %get-tuple-element.18.own_p.refs_1_.refs_0_, bf16[144,256]{1,0:T(8,128)(2,1)} %collective-permute-done.head.refs_2_.refs_1_.refs_6_, bf16[8,256,256]{2,1,0:T(8,128)(2,1)} %get-tuple-element.28.refs_2_, ...), custom_call_target="tpu_custom_call" | custom-call | tf_op jit(solution)/shard_map/mix/pallas_call | solution.py:34
  42.1 0.1 collective-permute-start.14
  42.2 0.0 collective-permute-done.8.e2
  42.2 0.1 collective-permute-start.10
  42.3 0.0 collective-permute-done.7.e1
  42.3 0.5 collective-permute-start.9
  42.8 1.2 %collective-permute-done.10.swap_e2 = bf16[4,128,128]{2,1,0:T(8,128)(2,1)} collective-permute-done((bf16[4,128,128]{2,1,0:T(8,128)(2,1)}, bf16[4,128,128]{2,1,0:T(8,128)(2,1)}, u32[]{:S(2)}, u32[]{:S(2)}) %collective-permute-start.10) | collective-permute-done | bytes 131104 | tf_op jit(solution)/shard_map/ppermute | solution.py:286
  44.0 0.2 collective-permute-done.9.swap_e1
  44.1 2.8 %collective-permute-done.11.later.rest_2_ = bf16[4,128,256]{2,1,0:T(8,128)(2,1)} collective-permute-done((bf16[4,128,256]{2,1,0:T(8,128)(2,1)}, bf16[4,128,256]{2,1,0:T(8,128)(2,1)}, u32[]{:S(2)}, u32[]{:S(2)}) %collective-permute-start.11) | collective-permute-done | bytes 262176 | tf_op jit(solution)/shard_map/ppermute | solution.py:286
  46.9 3.6 %regrid.1 = bf16[16,128,256]{2,1,0:T(8,128)(2,1)} custom-call(s32[2,32]{1,0:T(2,128)} %bitcast.1, bf16[4,128,128]{2,1,0:T(8,128)(2,1)} %get-tuple-element.25.own, bf16[4,128,128]{2,1,0:T(8,128)(2,1)} %collective-permute-done.6.swap.refs_3_, bf16[4,128,128]{2,1,0:T(8,128)(2,1)} %collective-permute-done.7.e1, bf16[4,128,128]{2,1,0:T(8,128)(2,1)} %collective-permute-done.8.e2, ...), custom_call_target="tpu_custom_call" | custom-call | tf_op jit(solution)/shard_map/regrid/pallas_call | solution.py:34
  50.5 1.5 %collective-permute-done.14.rest_3_ = bf16[4,128,256]{2,1,0:T(8,128)(2,1)} collective-permute-done((bf16[4,128,256]{2,1,0:T(8,128)(2,1)}, bf16[4,128,256]{2,1,0:T(8,128)(2,1)}, u32[]{:S(2)}, u32[]{:S(2)}) %collective-permute-start.14) | collective-permute-done | bytes 262176 | tf_op jit(solution)/shard_map/ppermute | solution.py:286
  52.0 3.2 %final.1 = bf16[128,16,256]{2,1,0:T(8,128)(2,1)} custom-call(bf16[128,16,256]{2,1,0:T(8,128)(2,1)} %state.3, bf16[16,128,256]{2,1,0:T(8,128)(2,1)} %regrid.1, bf16[4,128,256]{2,1,0:T(8,128)(2,1)} %get-tuple-element.27.rest_0_, bf16[4,128,256]{2,1,0:T(8,128)(2,1)} %get-tuple-element.31.rest_1_, bf16[4,128,256]{2,1,0:T(8,128)(2,1)} %collective-permute-done.11.later.rest_2_, ...), custom_call_target="tpu_custom_call" | custom-call | tf_op jit(solution)/shard_map/final/pallas_call | solution.py:34
Async XLA Ops:
  0.6 8.8 %collective-permute-start.3 = (bf16[128,512]{1,0:T(8,128)(2,1)}, bf16[128,512]{1,0:T(8,128)(2,1)}, u32[]{:S(2)}, u32[]{:S(2)}) collective-permute-start(bf16[128,512]{1,0:T(8,128)(2,1)} %refs_7_.1), channel_id=1, source_target_pairs={{0,1},{1,0},{2,3},{3,2},{4,5},{5,4},{6,7},{7,6},{8,9},{9,8},{10,11... | collective-permute-start | bytes 393224 | tf_op jit(solution)/shard_map/ppermute | solution.py:286
  4.0 5.5 %collective-permute-start = (bf16[144,256]{1,0:T(8,128)(2,1)}, bf16[144,256]{1,0:T(8,128)(2,1)}, u32[]{:S(2)}, u32[]{:S(2)}) collective-permute-start(bf16[144,256]{1,0:T(8,128)(2,1)} %get-tuple-element.19), channel_id=1, source_target_pairs={{0,1},{1,0},{2,3},{3,2},{4,5},{5,4},{6,7},{7,6},{8,9},{9,8},{10,11... | collective-permute-start | bytes 221192 | tf_op jit(solution)/shard_map/ppermute | solution.py:286
  5.4 16.0 %collective-permute-start.5 = (bf16[6,128,256]{2,1,0:T(8,128)(2,1)}, bf16[6,128,256]{2,1,0:T(8,128)(2,1)}, u32[]{:S(2)}, u32[]{:S(2)}) collective-permute-start(bf16[6,128,256]{2,1,0:T(8,128)(2,1)} %get-tuple-element.24), channel_id=1, source_target_pairs={{0,1},{1,0},{2,3},{3,2},{4,5},{5,4},{6,7},{7,6},{8,9},{9,8},{10,11... | collective-permute-start | bytes 1179656 | tf_op jit(solution)/shard_map/ppermute | solution.py:286
  6.0 15.4 %collective-permute-start.1 = (bf16[256,512]{1,0:T(8,128)(2,1)}, bf16[256,512]{1,0:T(8,128)(2,1)}, u32[]{:S(2)}, u32[]{:S(2)}) collective-permute-start(bf16[256,512]{1,0:T(8,128)(2,1)} %refs_3_.1), channel_id=1, source_target_pairs={{0,17},{1,16},{2,19},{3,18},{4,21},{5,20},{6,23},{7,22},{8,25},{9,... | collective-permute-start | bytes 786440 | tf_op jit(solution)/shard_map/ppermute | solution.py:286
  8.1 13.3 %collective-permute-start.2 = (bf16[512,256]{1,0:T(8,128)(2,1)}, bf16[512,256]{1,0:T(8,128)(2,1)}, u32[]{:S(2)}, u32[]{:S(2)}) collective-permute-start(bf16[512,256]{1,0:T(8,128)(2,1)} %refs_4_.1), channel_id=1, source_target_pairs={{0,17},{1,16},{2,19},{3,18},{4,21},{5,20},{6,23},{7,22},{8,25},{9,... | collective-permute-start | bytes 786440 | tf_op jit(solution)/shard_map/ppermute | solution.py:286
  12.5 7.2 %collective-permute-start.4 = (bf16[128,512]{1,0:T(8,128)(2,1)}, bf16[128,512]{1,0:T(8,128)(2,1)}, u32[]{:S(2)}, u32[]{:S(2)}) collective-permute-start(bf16[128,512]{1,0:T(8,128)(2,1)} %get-tuple-element.23), channel_id=1, source_target_pairs={{0,1},{1,0},{2,3},{3,2},{4,5},{5,4},{6,7},{7,6},{8,9},{9,8},{10,11... | collective-permute-start | bytes 393224 | tf_op jit(solution)/shard_map/ppermute | solution.py:286
  14.7 19.7 %collective-permute-start.12 = (bf16[2,128,256]{2,1,0:T(8,128)(2,1)}, bf16[2,128,256]{2,1,0:T(8,128)(2,1)}, u32[]{:S(2)}, u32[]{:S(2)}) collective-permute-start(bf16[2,128,256]{2,1,0:T(8,128)(2,1)} %get-tuple-element.29), channel_id=1, source_target_pairs={{1,3},{2,4},{3,1},{4,2},{5,7},{6,8},{7,5},{8,6},{9,11},{10,12},{11... | collective-permute-start | bytes 393224 | tf_op jit(solution)/shard_map/ppermute | solution.py:286
  19.7 17.1 %collective-permute-start.13 = (bf16[2,128,256]{2,1,0:T(8,128)(2,1)}, bf16[2,128,256]{2,1,0:T(8,128)(2,1)}, u32[]{:S(2)}, u32[]{:S(2)}) collective-permute-start(bf16[2,128,256]{2,1,0:T(8,128)(2,1)} %get-tuple-element.30), channel_id=1, source_target_pairs={{0,1},{1,0},{2,3},{3,2},{4,5},{5,4},{6,7},{7,6},{8,9},{9,8},{10,11... | collective-permute-start | bytes 393224 | tf_op jit(solution)/shard_map/ppermute | solution.py:286
  26.8 10.0 %collective-permute-start.6 = (bf16[4,128,128]{2,1,0:T(8,128)(2,1)}, bf16[4,128,128]{2,1,0:T(8,128)(2,1)}, u32[]{:S(2)}, u32[]{:S(2)}) collective-permute-start(bf16[4,128,128]{2,1,0:T(8,128)(2,1)} %get-tuple-element.25.own), channel_id=1, source_target_pairs={{0,2},{1,3},{2,0},{3,1},{4,6},{5,7},{6,4},{7,5},{8,10},{9,11},{10,... | collective-permute-start | bytes 393224 | tf_op jit(solution)/shard_map/ppermute | solution.py:286
  26.9 15.3 %collective-permute-start.8 = (bf16[4,128,128]{2,1,0:T(8,128)(2,1)}, bf16[4,128,128]{2,1,0:T(8,128)(2,1)}, u32[]{:S(2)}, u32[]{:S(2)}) collective-permute-start(bf16[4,128,128]{2,1,0:T(8,128)(2,1)} %get-tuple-element.25.own), channel_id=1, source_target_pairs={{0,4},{1,5},{2,6},{3,7},{4,0},{5,1},{6,2},{7,3},{8,12},{9,13},{10,... | collective-permute-start | bytes 393224 | tf_op jit(solution)/shard_map/ppermute | solution.py:286
  28.2 14.1 %collective-permute-start.7 = (bf16[4,128,128]{2,1,0:T(8,128)(2,1)}, bf16[4,128,128]{2,1,0:T(8,128)(2,1)}, u32[]{:S(2)}, u32[]{:S(2)}) collective-permute-start(bf16[4,128,128]{2,1,0:T(8,128)(2,1)} %get-tuple-element.25.own), channel_id=1, source_target_pairs={{4,8},{5,9},{6,10},{7,11},{8,4},{9,5},{10,6},{11,7},{12,16},{13,17... | collective-permute-start | bytes 393224 | tf_op jit(solution)/shard_map/ppermute | solution.py:286
  34.4 12.5 %collective-permute-start.11 = (bf16[4,128,256]{2,1,0:T(8,128)(2,1)}, bf16[4,128,256]{2,1,0:T(8,128)(2,1)}, u32[]{:S(2)}, u32[]{:S(2)}) collective-permute-start(bf16[4,128,256]{2,1,0:T(8,128)(2,1)} %get-tuple-element.26), channel_id=1, source_target_pairs={{0,1},{1,0},{2,3},{3,2},{4,5},{5,4},{6,7},{7,6},{8,9},{9,8},{10,11... | collective-permute-start | bytes 786440 | tf_op jit(solution)/shard_map/ppermute | solution.py:286
  42.1 9.9 %collective-permute-start.14 = (bf16[4,128,256]{2,1,0:T(8,128)(2,1)}, bf16[4,128,256]{2,1,0:T(8,128)(2,1)}, u32[]{:S(2)}, u32[]{:S(2)}) collective-permute-start(bf16[4,128,256]{2,1,0:T(8,128)(2,1)} %get-tuple-element.32), channel_id=1, source_target_pairs={{0,1},{1,0},{2,3},{3,2},{4,5},{5,4},{6,7},{7,6},{8,9},{9,8},{10,11... | collective-permute-start | bytes 786440 | tf_op jit(solution)/shard_map/ppermute | solution.py:286
  42.2 1.8 %collective-permute-start.10 = (bf16[4,128,128]{2,1,0:T(8,128)(2,1)}, bf16[4,128,128]{2,1,0:T(8,128)(2,1)}, u32[]{:S(2)}, u32[]{:S(2)}) collective-permute-start(bf16[4,128,128]{2,1,0:T(8,128)(2,1)} %collective-permute-done.8.e2), channel_id=1, source_target_pairs={{0,2},{1,3},{2,0},{3,1},{4,6},{5,7},{6,4},{7,5},{8,10},{9,11},{10,... | collective-permute-start | bytes 393224 | tf_op jit(solution)/shard_map/ppermute | solution.py:286
  42.3 1.9 %collective-permute-start.9 = (bf16[4,128,128]{2,1,0:T(8,128)(2,1)}, bf16[4,128,128]{2,1,0:T(8,128)(2,1)}, u32[]{:S(2)}, u32[]{:S(2)}) collective-permute-start(bf16[4,128,128]{2,1,0:T(8,128)(2,1)} %collective-permute-done.7.e1), channel_id=1, source_target_pairs={{0,2},{1,3},{2,0},{3,1},{4,6},{5,7},{6,4},{7,5},{8,10},{9,11},{10,... | collective-permute-start | bytes 393224 | tf_op jit(solution)/shard_map/ppermute | solution.py:286

commit v4 on v3

--- a/solution.py
+++ b/solution.py
@@ -21,6 +21,7 @@
 SMEM = pl.BlockSpec(memory_space=pltpu.SMEM)
 ANY = pl.BlockSpec(memory_space=pl.ANY)
 FINAL_STEPS = 2
+MIX_COST = 30 * 10**9
 OCEAN_COST = 8 * 10**9
 SENT = ((3, 9), (1, 3))
 MIXED = ((4, 8), (0, 4))
@@ -89,8 +90,9 @@
 
 
 def gelu(x):
-    inner = x * (0.7978845608028654 + 0.035677408136300125 * (x * x))
-    return (x * (0.5 + 0.5 * jnp.tanh(inner))).astype(BF16)
+    x = x.astype(BF16)
+    inner = x * (BF16(0.7978845608028654) + BF16(0.035677408136300125) * (x * x))
+    return x * (BF16(0.5) + BF16(0.5) * jnp.tanh(inner))
 
 
 def dot(a, b):
@@ -116,7 +118,15 @@
     return jnp.concatenate(halves, 1).T
 
 
-def ocean_kernel(mine, theirs, own_p, head, keep, up, down, passing, kept, sent, pair, passed, x):
+def turn_kernel(up, down, own, sent):
+    half = half_of()
+    for blocks, first in ((own, half), (sent, 1 - half)):
+        for j in range(2):
+            blocks[j * 256 : (j + 1) * 256] = turned_up(up, j, first)
+            blocks[(2 + j) * 256 : (3 + j) * 256] = turned_down(down, j, first)
+
+
+def ocean_kernel(mine, theirs, own_p, head, keep, up, down, before, kept, sent, pair, x):
     pair[0] = keep[0]
     pair[1] = head[:HALF, :]
     gains = [own_p[...].T[:, 10:11], params_of(head).T[:, 10:11]]
@@ -132,6 +142,15 @@
     sent[...] = total[HALF:].astype(BF16)
 
 
+def ocean_result_kernel(count, state, kept, got, passing, result, slots, passed):
+    for s in range(SLOTS):
+        cells = slice(s * CELLS_PER_TILE, (s + 1) * CELLS_PER_TILE)
+        value = state[:, cells].astype(F32) + (kept[:, cells] + got[:, cells].astype(F32))
+        value = jnp.where(s < count[0], value, 0.0).astype(BF16)
+        result[:, cells] = value
+        slots[s] = value
+
+
 def start(pairs, sems, at):
     moves = [pltpu.make_async_copy(src, dst, sems.at[at + n]) for n, (src, dst) in enumerate(pairs)]
     for m in moves:
@@ -147,14 +166,11 @@
 def mix_kernel(rows, runs_own, runs_other, n_in, leads, *refs):
     refs = list(refs)
     take = lambda n: [refs.pop(0) for _ in range(n)]
-    (count,) = take(1) if leads else (None,)
-    own_p, head, *weights = take(6 if leads else 3)
-    take(0 if leads else 1)
-    ocean_ins = take(3) if leads else []
+    own_p, head, *weights = take(4)
     ins = take(n_in)
+    take(2 if leads else 0)
     kept, sent = take(2)
-    blocks_out, result, slots = take(3) if leads else (None, None, None)
-    own_pv, head_pv, own_lines, other_lines, x, blocks, kept_v, sent_v, sems = take(9)
+    own_pv, head_pv, own_lines, other_lines, x, up, down, kept_v, sent_v, sems = take(10)
     side = side_of()
 
     def lines_of(runs, lines):
@@ -168,14 +184,14 @@
     pairs += [*lines_of(runs_own, own_lines), *lines_of(runs_other, other_lines)]
     loads = start(pairs, sems, 0)
     used = len(pairs)
-    if leads:
-        raw, ocean_v, (result_v, slots_v) = take(4), take(3), take(2)
-        ocean_loads = start(list(zip(ocean_ins, ocean_v)), sems, used)
-        weight_loads = start(list(zip(weights, raw)), sems, used + 3)
-        used += 7
-    else:
-        weight_loads = start([(weights[0], blocks)], sems, used)
-        used += 1
+    pairs = []
+    for n, w in enumerate(weights):
+        pairs.append((w.at[pl.ds(0, 512)], up.at[pl.ds(512 * n, 512)]))
+        pairs += [
+            (w.at[pl.ds(512 + 256 * j, 256)], down.at[:, pl.ds(512 * n + 256 * j, 256)]) for j in range(2)
+        ]
+    weight_loads = start(pairs, sems, used)
+    used += len(pairs)
     wait(loads)
     params = []
     for taps in (own_pv[...], head_pv[:, :LANES].astype(F32) + head_pv[:, LANES:].astype(F32)):
@@ -195,29 +211,10 @@
         x[:HALF, i * COLS : (i + 1) * COLS] = own
         x[HALF:, i * COLS : (i + 1) * COLS] = other
     stores = []
-    if leads:
-        wait(ocean_loads)
-        for s in range(SLOTS):
-            cells = slice(s * CELLS_PER_TILE, (s + 1) * CELLS_PER_TILE)
-            value = ocean_v[0][:, cells].astype(F32) + (ocean_v[1][:, cells] + ocean_v[2][:, cells].astype(F32))
-            value = jnp.where(s < count[0], value, 0.0).astype(BF16)
-            result_v[:, cells] = value
-            slots_v[s] = value
-        stores += start([(result_v, result), (slots_v, slots)], sems, used)
-        used += 2
     wait(weight_loads)
-    if leads:
-        for n, (u, d) in enumerate((raw[:2], raw[2:])):
-            for j in range(2):
-                blocks[2 * n + j] = turned_up(u, j, half_of())
-                blocks[4 + 2 * n + j] = turned_down(d, j, half_of())
-        stores += start([(blocks, blocks_out)], sems, used)
-        used += 1
-    up = blocks[:4].reshape(4 * 256, CHANNELS)
-    down = jnp.concatenate([blocks[4 + j] for j in range(4)], 1)
     for i in range(rows):
-        hidden = gelu(dot(up, x[:, i * COLS : (i + 1) * COLS]))
-        value = dot(down, hidden).astype(BF16)
+        hidden = gelu(dot(up[...], x[:, i * COLS : (i + 1) * COLS]))
+        value = dot(down[...], hidden).astype(BF16)
         kept_v[i] = value[:HALF]
         sent_v[i] = value[HALF:]
         stores += start([(sent_v.at[i], sent.at[i]), (kept_v.at[i], kept.at[i])], sems, used)
@@ -293,7 +290,14 @@
     def across(x):
         return move(x, lambda t, c: (t ^ half_turn, 1 - c))
 
-    got_up, got_down = across(atm_up), across(atm_down)
+    blocks, blocks_sent = call(
+        turn_kernel,
+        [sds((1024, 256))] * 2,
+        (atm_up, atm_down),
+        [WHOLE] * 2,
+        name="turn",
+    )
+    got_blocks = across(blocks_sent)
     ocean_theirs = partner(ocean_state)
     head_sent, own_p, *sends, keep = call(
         open_kernel,
@@ -306,21 +310,30 @@
     )
     head = partner(head_sent)
     cells = ocean_state.shape[1]
-    ocean_kept, ocean_sent, pair, last_sent = call(
+    ocean_kept, ocean_sent, pair = call(
         ocean_kernel,
-        [sds((HALF, cells), F32), sds((HALF, cells)), sds((2, HALF, COLS)), sds(sends[-1].shape)],
-        (ocean_state, ocean_theirs, own_p, head, keep, ocean_up, ocean_down, sends[-1]),
+        [sds((HALF, cells), F32), sds((HALF, cells)), sds((2, HALF, COLS))],
+        (ocean_state, ocean_theirs, own_p, head, keep, ocean_up, ocean_down, blocks),
         [WHOLE] * 7 + [ANY],
         [pltpu.VMEM((256, cells), BF16)],
-        out_specs=[WHOLE] * 3 + [ANY],
-        input_output_aliases={7: 3},
+        out_specs=[WHOLE] * 3,
         name="ocean",
         flops=OCEAN_COST,
     )
-    got = [partner(s) for s in (*sends[:-1], last_sent)]
     ocean_got = partner(ocean_sent)
     edges = move(pair, lambda t, c: (t - 1 + 2 * ((t + c) % 2), c))
-    kept_rows, got_rows, blocks = [], [], None
+    ocean_result, slots, last_sent = call(
+        ocean_result_kernel,
+        [sds((HALF, cells)), sds((SLOTS, HALF, CELLS_PER_TILE)), sds(sends[-1].shape)],
+        (ocean_count, ocean_state, ocean_kept, ocean_got, sends[-1]),
+        [SMEM, WHOLE, WHOLE, WHOLE, ANY],
+        out_specs=[WHOLE, WHOLE, ANY],
+        input_output_aliases={4: 2},
+        name="result",
+    )
+    got = [partner(s) for s in (*sends[:-1], last_sent)]
+    swapped = move(slots, lambda t, c: (t ^ 1, c))
+    kept_rows, got_rows = [], []
     for a, b in MIXED:
         ins, runs_own, runs_other = [keep], [], []
         first = max(a - 1, 0)
@@ -334,8 +347,7 @@
             if p < q:
                 runs_other.append((len(ins), p - SENT[[x is g for x in got].index(True)][0], q - p, p - a + 1))
                 ins.append(g)
-        rows, leads = b - a, blocks is None
-        lead_ins = (atm_up, atm_down, got_up, got_down, ocean_state, ocean_kept, ocean_got)
+        rows, leads = b - a, not kept_rows
         out = [sds((rows, HALF, COLS))] * 2
         scratch = [
             pltpu.VMEM((16, HALF), F32),
@@ -343,28 +355,23 @@
             pltpu.VMEM((rows + 2, HALF, COLS), BF16),
             pltpu.VMEM((rows + 2, HALF, COLS), BF16),
             pltpu.VMEM((CHANNELS, rows * COLS), BF16),
-            pltpu.VMEM((8, 256, 256), BF16),
+            pltpu.VMEM((1024, 256), BF16),
+            pltpu.VMEM((256, 1024), BF16),
             pltpu.VMEM((rows, HALF, COLS), BF16),
             pltpu.VMEM((rows, HALF, COLS), BF16),
             pltpu.SemaphoreType.DMA((40,)),
         ]
-        if leads:
-            out += [sds((8, 256, 256)), sds((HALF, cells)), sds((SLOTS, HALF, CELLS_PER_TILE))]
-            scratch += [pltpu.VMEM(w.shape, w.dtype) for w in lead_ins]
-            scratch += [pltpu.VMEM((HALF, cells), BF16), pltpu.VMEM((SLOTS, HALF, CELLS_PER_TILE), BF16)]
-        args = (ocean_count, own_p, head, *lead_ins, *ins) if leads else (own_p, head, blocks, swapped, *ins)
-        kept, sent, *more = call(
+        args = (own_p, head, blocks, got_blocks, *ins, *((edges, got[-1]) if leads else ()))
+        kept, sent = call(
             functools.partial(mix_kernel, rows, runs_own, runs_other, len(ins), leads),
             out,
             args,
-            ([SMEM] if leads else []) + [ANY] * (len(args) - leads),
+            [ANY] * len(args),
             scratch,
             out_specs=[ANY] * len(out),
             name="mix",
+            flops=MIX_COST if leads else 0,
         )
-        if leads:
-            blocks, ocean_result, slots = more
-            swapped = move(slots, lambda t, c: (t ^ 1, c))
         kept_rows.append(kept)
         got_rows.append(partner(sent))
     e2 = move(slots, lambda t, c: (t ^ 2, c))

time: 55.5 us -> 53.9 us (0.971)
  the two profiles are of different devices: /device:TPU:26 before, /device:TPU:24 now
where the time goes in v4:
time: 53.9 us; the launch traced here: 53.2 us
  Pallas kernels  26.8 us (50%)
  starting transfers between devices  23.4 us (43%)
  waiting for transfers between devices  1.63 us (3%)
  between operations  1.37 us (3%)
    pallas_call x8, Pallas kernels, call(): pl.pallas_call(kernel, out_shape=out, in_specs=specs, out_specs=kw.pop('o...  26.8 us
    ppermute x14, starting transfers between devices, move(): return lax.ppermute(x, AXES, route)  23.4 us
    ppermute x14, waiting for transfers between devices, move(): return lax.ppermute(x, AXES, route)  1.63 us
  transfers between devices with their start and end apart: 14, of which 3 were waited for; matrix products, arithmetic and copies ran while one was open for 0% of the time, Pallas kernels for 44%

profile of v4, /device:TPU:24, one launch (start us, length us, event | category | flops | bytes accessed | tf_op | source)
XLA Modules:
  0.0 53.2 jit_solution(17464827118793157494)
XLA Ops:
  0.6 1.6 %collective-permute-start = (bf16[128,512]{1,0:T(8,128)(2,1)}, bf16[128,512]{1,0:T(8,128)(2,1)}, u32[]{:S(2)}, u32[]{:S(2)}) collective-permute-start(bf16[128,512]{1,0:T(8,128)(2,1)} %state.4), channel_id=1, source_target_pairs={{0,1},{1,0},{2,3},{3,2},{4,5},{5,4},{6,7},{7,6},{8,9},{9,8},{10,11... | collective-permute-start | bytes 393224 | tf_op jit(solution)/shard_map/ppermute | solution.py:283
  2.2 2.7 %open.1 = (bf16[144,256]{1,0:T(8,128)(2,1)}, f32[16,128]{1,0:T(8,128)}, bf16[6,128,256]{2,1,0:T(8,128)(2,1)}, bf16[2,128,256]{2,1,0:T(8,128)(2,1)}, bf16[9,128,256]{2,1,0:T(8,128)(2,1)}) custom-call(bf16[128,16,256]{2,1,0:T(8,128)(2,1)} %state.5, f32[9,128]{1,0:T(8,128)} %taps.1, bf16[128]{0:T(256)(128)(2,1)} %atm_gain.1, bf16[128]{0:T(256)(128)(2,1)} %ocean_gain.1), custom_call_target="tpu_custom_call" | custom-call | tf_op jit(solution)/shard_map/open/pallas_call | solution.py:35
  4.9 0.5 %collective-permute-start.1 = (bf16[144,256]{1,0:T(8,128)(2,1)}, bf16[144,256]{1,0:T(8,128)(2,1)}, u32[]{:S(2)}, u32[]{:S(2)}) collective-permute-start(bf16[144,256]{1,0:T(8,128)(2,1)} %get-tuple-element.20), channel_id=1, source_target_pairs={{0,1},{1,0},{2,3},{3,2},{4,5},{5,4},{6,7},{7,6},{8,9},{9,8},{10,11... | collective-permute-start | bytes 221192 | tf_op jit(solution)/shard_map/ppermute | solution.py:283
  5.5 1.5 %collective-permute-start.9 = (bf16[6,128,256]{2,1,0:T(8,128)(2,1)}, bf16[6,128,256]{2,1,0:T(8,128)(2,1)}, u32[]{:S(2)}, u32[]{:S(2)}) collective-permute-start(bf16[6,128,256]{2,1,0:T(8,128)(2,1)} %get-tuple-element.28), channel_id=1, source_target_pairs={{0,1},{1,0},{2,3},{3,2},{4,5},{5,4},{6,7},{7,6},{8,9},{9,8},{10,11... | collective-permute-start | bytes 1179656 | tf_op jit(solution)/shard_map/ppermute | solution.py:283
  6.9 2.2 %turn.1 = (bf16[1024,256]{1,0:T(8,128)(2,1)}, bf16[1024,256]{1,0:T(8,128)(2,1)}) custom-call(bf16[256,512]{1,0:T(8,128)(2,1)} %up.2, bf16[512,256]{1,0:T(8,128)(2,1)} %down.2), custom_call_target="tpu_custom_call" | custom-call | tf_op jit(solution)/shard_map/turn/pallas_call | solution.py:35
  9.2 2.1 %collective-permute-start.8 = (bf16[1024,256]{1,0:T(8,128)(2,1)}, bf16[1024,256]{1,0:T(8,128)(2,1)}, u32[]{:S(2)}, u32[]{:S(2)}) collective-permute-start(bf16[1024,256]{1,0:T(8,128)(2,1)} %get-tuple-element.27), channel_id=1, source_target_pairs={{0,17},{1,16},{2,19},{3,18},{4,21},{5,20},{6,23},{7,22},{8,25},{9,... | collective-permute-start | bytes 1572872 | tf_op jit(solution)/shard_map/ppermute | solution.py:283
  11.3 0.0 collective-permute-done.1.head.refs_1_.refs_6_
  11.3 0.0 collective-permute-done.theirs
  11.3 2.9 %ocean.1 = (f32[128,512]{1,0:T(8,128)}, bf16[128,512]{1,0:T(8,128)(2,1)}, bf16[2,128,256]{2,1,0:T(8,128)(2,1)}) custom-call(bf16[128,512]{1,0:T(8,128)(2,1)} %state.4, bf16[128,512]{1,0:T(8,128)(2,1)} %collective-permute-done.theirs, f32[16,128]{1,0:T(8,128)} %get-tuple-element.19.own_p.refs_0_, ...), custom_call_target="tpu_custom_call" | custom-call | flops 8000000000 | tf_op jit(solution)/shard_map/ocean/pallas_call | solution.py:35
  14.2 0.6 %collective-permute-start.2 = (bf16[128,512]{1,0:T(8,128)(2,1)}, bf16[128,512]{1,0:T(8,128)(2,1)}, u32[]{:S(2)}, u32[]{:S(2)}) collective-permute-start(bf16[128,512]{1,0:T(8,128)(2,1)} %get-tuple-element.24), channel_id=1, source_target_pairs={{0,1},{1,0},{2,3},{3,2},{4,5},{5,4},{6,7},{7,6},{8,9},{9,8},{10,11... | collective-permute-start | bytes 393224 | tf_op jit(solution)/shard_map/ppermute | solution.py:283
  15.4 5.6 %collective-permute-start.10 = (bf16[2,128,256]{2,1,0:T(8,128)(2,1)}, bf16[2,128,256]{2,1,0:T(8,128)(2,1)}, u32[]{:S(2)}, u32[]{:S(2)}) collective-permute-start(bf16[2,128,256]{2,1,0:T(8,128)(2,1)} %get-tuple-element.29), channel_id=1, source_target_pairs={{1,3},{2,4},{3,1},{4,2},{5,7},{6,8},{7,5},{8,6},{9,11},{10,12},{11... | collective-permute-start | bytes 393224 | tf_op jit(solution)/shard_map/ppermute | solution.py:283
  21.1 0.0 collective-permute-done.2.got
  21.1 1.8 %result.1 = (bf16[128,512]{1,0:T(8,128)(2,1)}, bf16[4,128,128]{2,1,0:T(8,128)(2,1)}, bf16[2,128,256]{2,1,0:T(8,128)(2,1)}) custom-call(s32[1]{0:T(128)S(6)} %copy.16.count, bf16[128,512]{1,0:T(8,128)(2,1)} %state.4, f32[128,512]{1,0:T(8,128)} %get-tuple-element.23.kept, ...), custom_call_target="tpu_custom_call", output_to_operand_aliasing={{2}: (4, {})} | custom-call | tf_op jit(solution)/shard_map/result/pallas_call | solution.py:35
  22.9 0.1 collective-permute-start.11
  23.0 8.6 %collective-permute-start.4 = (bf16[4,128,128]{2,1,0:T(8,128)(2,1)}, bf16[4,128,128]{2,1,0:T(8,128)(2,1)}, u32[]{:S(2)}, u32[]{:S(2)}) collective-permute-start(bf16[4,128,128]{2,1,0:T(8,128)(2,1)} %get-tuple-element.26.own), channel_id=1, source_target_pairs={{4,8},{5,9},{6,10},{7,11},{8,4},{9,5},{10,6},{11,7},{12,16},{13,17... | collective-permute-start | bytes 393224 | tf_op jit(solution)/shard_map/ppermute | solution.py:283
  31.6 0.0 collective-permute-done.10.refs_6_.refs_5_
  31.6 0.1 collective-permute-start.5
  31.7 0.0 collective-permute-done.11.refs_7_.refs_8_
  31.7 0.0 collective-permute-done.9.refs_5_.refs_7_
  31.7 0.0 collective-permute-done.8.refs_3_
  31.7 5.1 %mix.2 = (bf16[4,128,256]{2,1,0:T(8,128)(2,1)}, bf16[4,128,256]{2,1,0:T(8,128)(2,1)}) custom-call(f32[16,128]{1,0:T(8,128)} %get-tuple-element.19.own_p.refs_0_, bf16[144,256]{1,0:T(8,128)(2,1)} %collective-permute-done.1.head.refs_1_.refs_6_, bf16[1024,256]{1,0:T(8,128)(2,1)} %get-tuple-element.22.before.refs_2_, ...), custom_call_target="tpu_custom_call" | custom-call | flops 30000001024 | tf_op jit(solution)/shard_map/mix/pallas_call | solution.py:35
  36.8 0.2 collective-permute-start.12
  37.1 5.2 %mix.3 = (bf16[4,128,256]{2,1,0:T(8,128)(2,1)}, bf16[4,128,256]{2,1,0:T(8,128)(2,1)}) custom-call(f32[16,128]{1,0:T(8,128)} %get-tuple-element.19.own_p.refs_0_, bf16[144,256]{1,0:T(8,128)(2,1)} %collective-permute-done.1.head.refs_1_.refs_6_, bf16[1024,256]{1,0:T(8,128)(2,1)} %get-tuple-element.22.before.refs_2_, ...), custom_call_target="tpu_custom_call" | custom-call | tf_op jit(solution)/shard_map/mix/pallas_call | solution.py:35
  42.2 1.9 %collective-permute-start.13 = (bf16[4,128,256]{2,1,0:T(8,128)(2,1)}, bf16[4,128,256]{2,1,0:T(8,128)(2,1)}, u32[]{:S(2)}, u32[]{:S(2)}) collective-permute-start(bf16[4,128,256]{2,1,0:T(8,128)(2,1)} %get-tuple-element.34), channel_id=1, source_target_pairs={{0,1},{1,0},{2,3},{3,2},{4,5},{5,4},{6,7},{7,6},{8,9},{9,8},{10,11... | collective-permute-start | bytes 786440 | tf_op jit(solution)/shard_map/ppermute | solution.py:283
  44.2 0.0 collective-permute-start.3
  44.2 0.0 collective-permute-done.4.e1
  44.2 0.5 collective-permute-start.6
  44.7 0.0 collective-permute-done.5.e2
  44.7 0.1 collective-permute-start.7
  44.8 1.1 %collective-permute-done.3.swap = bf16[4,128,128]{2,1,0:T(8,128)(2,1)} collective-permute-done((bf16[4,128,128]{2,1,0:T(8,128)(2,1)}, bf16[4,128,128]{2,1,0:T(8,128)(2,1)}, u32[]{:S(2)}, u32[]{:S(2)}) %collective-permute-start.3) | collective-permute-done | bytes 131104 | tf_op jit(solution)/shard_map/ppermute | solution.py:283
  45.9 0.2 collective-permute-done.6.swap_e1
  46.1 0.3 collective-permute-done.7.swap_e2
  46.4 0.0 collective-permute-done.12.later.rest_2_
  46.4 3.6 %regrid.1 = bf16[16,128,256]{2,1,0:T(8,128)(2,1)} custom-call(s32[2,32]{1,0:T(2,128)} %bitcast.1, bf16[4,128,128]{2,1,0:T(8,128)(2,1)} %get-tuple-element.26.own, bf16[4,128,128]{2,1,0:T(8,128)(2,1)} %collective-permute-done.3.swap, bf16[4,128,128]{2,1,0:T(8,128)(2,1)} %collective-permute-done.4.e1, bf16[4,128,128]{2,1,0:T(8,128)(2,1)} %collective-permute-done.5.e2, ...), custom_call_target="tpu_custom_call" | custom-call | tf_op jit(solution)/shard_map/regrid/pallas_call | solution.py:35
  50.0 0.0 collective-permute-done.13.rest_3_
  50.0 3.2 %final.1 = bf16[128,16,256]{2,1,0:T(8,128)(2,1)} custom-call(bf16[128,16,256]{2,1,0:T(8,128)(2,1)} %state.5, bf16[16,128,256]{2,1,0:T(8,128)(2,1)} %regrid.1, bf16[4,128,256]{2,1,0:T(8,128)(2,1)} %get-tuple-element.32.rest_0_, bf16[4,128,256]{2,1,0:T(8,128)(2,1)} %get-tuple-element.33.rest_1_, bf16[4,128,256]{2,1,0:T(8,128)(2,1)} %collective-permute-done.12.later.rest_2_, ...), custom_call_target="tpu_custom_call" | custom-call | tf_op jit(solution)/shard_map/final/pallas_call | solution.py:35
Async XLA Ops:
  0.6 10.6 %collective-permute-start = (bf16[128,512]{1,0:T(8,128)(2,1)}, bf16[128,512]{1,0:T(8,128)(2,1)}, u32[]{:S(2)}, u32[]{:S(2)}) collective-permute-start(bf16[128,512]{1,0:T(8,128)(2,1)} %state.4), channel_id=1, source_target_pairs={{0,1},{1,0},{2,3},{3,2},{4,5},{5,4},{6,7},{7,6},{8,9},{9,8},{10,11... | collective-permute-start | bytes 393224 | tf_op jit(solution)/shard_map/ppermute | solution.py:283
  4.9 6.3 %collective-permute-start.1 = (bf16[144,256]{1,0:T(8,128)(2,1)}, bf16[144,256]{1,0:T(8,128)(2,1)}, u32[]{:S(2)}, u32[]{:S(2)}) collective-permute-start(bf16[144,256]{1,0:T(8,128)(2,1)} %get-tuple-element.20), channel_id=1, source_target_pairs={{0,1},{1,0},{2,3},{3,2},{4,5},{5,4},{6,7},{7,6},{8,9},{9,8},{10,11... | collective-permute-start | bytes 221192 | tf_op jit(solution)/shard_map/ppermute | solution.py:283
  5.5 26.2 %collective-permute-start.9 = (bf16[6,128,256]{2,1,0:T(8,128)(2,1)}, bf16[6,128,256]{2,1,0:T(8,128)(2,1)}, u32[]{:S(2)}, u32[]{:S(2)}) collective-permute-start(bf16[6,128,256]{2,1,0:T(8,128)(2,1)} %get-tuple-element.28), channel_id=1, source_target_pairs={{0,1},{1,0},{2,3},{3,2},{4,5},{5,4},{6,7},{7,6},{8,9},{9,8},{10,11... | collective-permute-start | bytes 1179656 | tf_op jit(solution)/shard_map/ppermute | solution.py:283
  9.2 22.5 %collective-permute-start.8 = (bf16[1024,256]{1,0:T(8,128)(2,1)}, bf16[1024,256]{1,0:T(8,128)(2,1)}, u32[]{:S(2)}, u32[]{:S(2)}) collective-permute-start(bf16[1024,256]{1,0:T(8,128)(2,1)} %get-tuple-element.27), channel_id=1, source_target_pairs={{0,17},{1,16},{2,19},{3,18},{4,21},{5,20},{6,23},{7,22},{8,25},{9,... | collective-permute-start | bytes 1572872 | tf_op jit(solution)/shard_map/ppermute | solution.py:283
  14.2 6.9 %collective-permute-start.2 = (bf16[128,512]{1,0:T(8,128)(2,1)}, bf16[128,512]{1,0:T(8,128)(2,1)}, u32[]{:S(2)}, u32[]{:S(2)}) collective-permute-start(bf16[128,512]{1,0:T(8,128)(2,1)} %get-tuple-element.24), channel_id=1, source_target_pairs={{0,1},{1,0},{2,3},{3,2},{4,5},{5,4},{6,7},{7,6},{8,9},{9,8},{10,11... | collective-permute-start | bytes 393224 | tf_op jit(solution)/shard_map/ppermute | solution.py:283
  15.4 16.1 %collective-permute-start.10 = (bf16[2,128,256]{2,1,0:T(8,128)(2,1)}, bf16[2,128,256]{2,1,0:T(8,128)(2,1)}, u32[]{:S(2)}, u32[]{:S(2)}) collective-permute-start(bf16[2,128,256]{2,1,0:T(8,128)(2,1)} %get-tuple-element.29), channel_id=1, source_target_pairs={{1,3},{2,4},{3,1},{4,2},{5,7},{6,8},{7,5},{8,6},{9,11},{10,12},{11... | collective-permute-start | bytes 393224 | tf_op jit(solution)/shard_map/ppermute | solution.py:283
  22.9 8.8 %collective-permute-start.11 = (bf16[2,128,256]{2,1,0:T(8,128)(2,1)}, bf16[2,128,256]{2,1,0:T(8,128)(2,1)}, u32[]{:S(2)}, u32[]{:S(2)}) collective-permute-start(bf16[2,128,256]{2,1,0:T(8,128)(2,1)} %get-tuple-element.30), channel_id=1, source_target_pairs={{0,1},{1,0},{2,3},{3,2},{4,5},{5,4},{6,7},{7,6},{8,9},{9,8},{10,11... | collective-permute-start | bytes 393224 | tf_op jit(solution)/shard_map/ppermute | solution.py:283
  23.0 21.2 %collective-permute-start.4 = (bf16[4,128,128]{2,1,0:T(8,128)(2,1)}, bf16[4,128,128]{2,1,0:T(8,128)(2,1)}, u32[]{:S(2)}, u32[]{:S(2)}) collective-permute-start(bf16[4,128,128]{2,1,0:T(8,128)(2,1)} %get-tuple-element.26.own), channel_id=1, source_target_pairs={{4,8},{5,9},{6,10},{7,11},{8,4},{9,5},{10,6},{11,7},{12,16},{13,17... | collective-permute-start | bytes 393224 | tf_op jit(solution)/shard_map/ppermute | solution.py:283
  31.6 13.1 %collective-permute-start.5 = (bf16[4,128,128]{2,1,0:T(8,128)(2,1)}, bf16[4,128,128]{2,1,0:T(8,128)(2,1)}, u32[]{:S(2)}, u32[]{:S(2)}) collective-permute-start(bf16[4,128,128]{2,1,0:T(8,128)(2,1)} %get-tuple-element.26.own), channel_id=1, source_target_pairs={{0,4},{1,5},{2,6},{3,7},{4,0},{5,1},{6,2},{7,3},{8,12},{9,13},{10,... | collective-permute-start | bytes 393224 | tf_op jit(solution)/shard_map/ppermute | solution.py:283
  36.8 9.6 %collective-permute-start.12 = (bf16[4,128,256]{2,1,0:T(8,128)(2,1)}, bf16[4,128,256]{2,1,0:T(8,128)(2,1)}, u32[]{:S(2)}, u32[]{:S(2)}) collective-permute-start(bf16[4,128,256]{2,1,0:T(8,128)(2,1)} %get-tuple-element.31), channel_id=1, source_target_pairs={{0,1},{1,0},{2,3},{3,2},{4,5},{5,4},{6,7},{7,6},{8,9},{9,8},{10,11... | collective-permute-start | bytes 786440 | tf_op jit(solution)/shard_map/ppermute | solution.py:283
  42.2 7.7 %collective-permute-start.13 = (bf16[4,128,256]{2,1,0:T(8,128)(2,1)}, bf16[4,128,256]{2,1,0:T(8,128)(2,1)}, u32[]{:S(2)}, u32[]{:S(2)}) collective-permute-start(bf16[4,128,256]{2,1,0:T(8,128)(2,1)} %get-tuple-element.34), channel_id=1, source_target_pairs={{0,1},{1,0},{2,3},{3,2},{4,5},{5,4},{6,7},{7,6},{8,9},{9,8},{10,11... | collective-permute-start | bytes 786440 | tf_op jit(solution)/shard_map/ppermute | solution.py:283
  44.2 1.7 %collective-permute-start.3 = (bf16[4,128,128]{2,1,0:T(8,128)(2,1)}, bf16[4,128,128]{2,1,0:T(8,128)(2,1)}, u32[]{:S(2)}, u32[]{:S(2)}) collective-permute-start(bf16[4,128,128]{2,1,0:T(8,128)(2,1)} %get-tuple-element.26.own), channel_id=1, source_target_pairs={{0,2},{1,3},{2,0},{3,1},{4,6},{5,7},{6,4},{7,5},{8,10},{9,11},{10,... | collective-permute-start | bytes 393224 | tf_op jit(solution)/shard_map/ppermute | solution.py:283
  44.2 1.9 %collective-permute-start.6 = (bf16[4,128,128]{2,1,0:T(8,128)(2,1)}, bf16[4,128,128]{2,1,0:T(8,128)(2,1)}, u32[]{:S(2)}, u32[]{:S(2)}) collective-permute-start(bf16[4,128,128]{2,1,0:T(8,128)(2,1)} %collective-permute-done.4.e1), channel_id=1, source_target_pairs={{0,2},{1,3},{2,0},{3,1},{4,6},{5,7},{6,4},{7,5},{8,10},{9,11},{10,... | collective-permute-start | bytes 393224 | tf_op jit(solution)/shard_map/ppermute | solution.py:283
  44.7 1.7 %collective-permute-start.7 = (bf16[4,128,128]{2,1,0:T(8,128)(2,1)}, bf16[4,128,128]{2,1,0:T(8,128)(2,1)}, u32[]{:S(2)}, u32[]{:S(2)}) collective-permute-start(bf16[4,128,128]{2,1,0:T(8,128)(2,1)} %collective-permute-done.5.e2), channel_id=1, source_target_pairs={{0,2},{1,3},{2,0},{3,1},{4,6},{5,7},{6,4},{7,5},{8,10},{9,11},{10,... | collective-permute-start | bytes 393224 | tf_op jit(solution)/shard_map/ppermute | solution.py:283

commit v5 on v4

--- a/solution.py
+++ b/solution.py
@@ -38,11 +38,23 @@
         in_specs=specs,
         out_specs=kw.pop("out_specs", jax.tree.map(lambda _: WHOLE, out)),
         scratch_shapes=list(scratch),
-        compiler_params=pltpu.CompilerParams(vmem_limit_bytes=64 << 20),
+        compiler_params=pltpu.CompilerParams(vmem_limit_bytes=40 << 20),
         cost_estimate=pl.CostEstimate(flops=flops, bytes_accessed=0, transcendentals=0),
         name=name,
         **kw,
     )(*ins)
+
+
+def start(pairs, sems, at):
+    moves = [pltpu.make_async_copy(src, dst, sems.at[at + n]) for n, (src, dst) in enumerate(pairs)]
+    for m in moves:
+        m.start()
+    return moves
+
+
+def wait(moves):
+    for m in moves:
+        m.wait()
 
 
 def half_of():
@@ -64,8 +76,13 @@
     return jnp.where(hit, 1.0, 0.0).astype(BF16)
 
 
-def open_kernel(state, taps, atm_gain, ocean_gain, head, own_p, *rest):
-    sends, keep = rest[: len(SENT)], rest[len(SENT)]
+def open_kernel(state_in, taps_in, atm_gain_in, ocean_gain_in, head, own_p, *rest):
+    sends, (keep, state, taps, atm_gain, ocean_gain, sems) = rest[: len(SENT)], rest[len(SENT) :]
+    pairs = [(taps_in, taps), (atm_gain_in, atm_gain), (ocean_gain_in, ocean_gain)]
+    pieces = [pl.ds(64 * n, 64) for n in range(2)]
+    pairs += [(state_in.at[p], state.at[p]) for p in pieces]
+    loads = start(pairs, sems, 0)
+    wait(loads[:3])
     side = side_of()
     gains = [g[...].astype(F32).reshape(1, HALF) for g in (atm_gain, ocean_gain)]
     own_p[...] = jnp.concatenate([taps[...], *gains, jnp.zeros((5, HALF), F32)], 0)
@@ -75,6 +92,8 @@
     head[HALF:, LANES:] = low
     pick = taker(18, side, lambda n: jnp.where(n < 9, row_at(n, side), row_at(n - 9, 1 - side)))
     for b in range(HALF // 16):
+        if b % 4 == 0:
+            loads[3 + b // 4].wait()
         channels = slice(16 * b, 16 * (b + 1))
         lines = dot(pick, state[channels].reshape(256, COLS)).astype(BF16)
         head[channels, :] = lines[16 * 9 : 16 * 10]
@@ -118,7 +137,8 @@
     return jnp.concatenate(halves, 1).T
 
 
-def turn_kernel(up, down, own, sent):
+def turn_kernel(up_in, down_in, own, sent, up, down, sems):
+    wait(start([(up_in, up), (down_in, down)], sems, 0))
     half = half_of()
     for blocks, first in ((own, half), (sent, 1 - half)):
         for j in range(2):
@@ -126,10 +146,14 @@
             blocks[(2 + j) * 256 : (3 + j) * 256] = turned_down(down, j, first)
 
 
-def ocean_kernel(mine, theirs, own_p, head, keep, up, down, before, kept, sent, pair, x):
+def ocean_kernel(
+    mine_in, theirs, own_p, head, keep, up_in, down_in, before, kept, sent, pair, x, mine, up, down, sems
+):
+    loads = start([(mine_in, mine), (up_in, up), (down_in, down)], sems, 0)
     pair[0] = keep[0]
     pair[1] = head[:HALF, :]
     gains = [own_p[...].T[:, 10:11], params_of(head).T[:, 10:11]]
+    wait(loads)
     own, other = normed([mine[...].astype(F32), theirs[...].astype(F32)], gains)
     x[:HALF, :] = own
     x[HALF:, :] = other
@@ -151,75 +175,37 @@
         slots[s] = value
 
 
-def start(pairs, sems, at):
-    moves = [pltpu.make_async_copy(src, dst, sems.at[at + n]) for n, (src, dst) in enumerate(pairs)]
-    for m in moves:
-        m.start()
-    return moves
-
-
-def wait(moves):
-    for m in moves:
-        m.wait()
-
-
-def mix_kernel(rows, runs_own, runs_other, n_in, leads, *refs):
-    refs = list(refs)
-    take = lambda n: [refs.pop(0) for _ in range(n)]
-    own_p, head, *weights = take(4)
-    ins = take(n_in)
-    take(2 if leads else 0)
-    kept, sent = take(2)
-    own_pv, head_pv, own_lines, other_lines, x, up, down, kept_v, sent_v, sems = take(10)
+def mix_kernel(rows, own_lines, other_lines, n_in, n_order, own_p, head, own_w, got_w, *refs):
+    ins, (kept, sent, x) = refs[:n_in], refs[n_in + n_order :]
     side = side_of()
-
-    def lines_of(runs, lines):
-        for ref, src, n, dst in runs:
-            if src is None:
-                yield ins[ref].at[pl.ds(0, HALF)], lines.at[dst]
-            else:
-                yield ins[ref].at[pl.ds(src, n)], lines.at[pl.ds(dst, n)]
-
-    pairs = [(own_p, own_pv), (head.at[pl.ds(HALF, 16)], head_pv)]
-    pairs += [*lines_of(runs_own, own_lines), *lines_of(runs_other, other_lines)]
-    loads = start(pairs, sems, 0)
-    used = len(pairs)
-    pairs = []
-    for n, w in enumerate(weights):
-        pairs.append((w.at[pl.ds(0, 512)], up.at[pl.ds(512 * n, 512)]))
-        pairs += [
-            (w.at[pl.ds(512 + 256 * j, 256)], down.at[:, pl.ds(512 * n + 256 * j, 256)]) for j in range(2)
-        ]
-    weight_loads = start(pairs, sems, used)
-    used += len(pairs)
-    wait(loads)
     params = []
-    for taps in (own_pv[...], head_pv[:, :LANES].astype(F32) + head_pv[:, LANES:].astype(F32)):
+    for taps in (own_p[...], params_of(head)):
         flipped = jnp.concatenate([taps[6:9], taps[3:6], taps[0:3], taps[9:]], 0)
         params.append(jnp.where(side == 0, taps, flipped).T)
 
-    def conv(lines, i, p):
-        near = [lines[i + a].astype(F32) for a in range(3)]
+    def line(place):
+        ref, index = place
+        return (ins[ref][:HALF, :] if index is None else ins[ref][index]).astype(F32)
+
+    def conv(places, p):
+        near = [line(place) for place in places]
         left, middle, right = [
             sum(p[:, 3 * a + b : 3 * a + b + 1] * near[a] for a in range(3)) for b in range(3)
         ]
         return middle + pltpu.roll(left, 1, 1) + pltpu.roll(right, COLS - 1, 1)
 
     for i in range(rows):
-        values = [conv(own_lines, i, params[0]), conv(other_lines, i, params[1])]
+        values = [conv(own_lines[i : i + 3], params[0]), conv(other_lines[i : i + 3], params[1])]
         own, other = normed(values, [p[:, 9:10] for p in params])
         x[:HALF, i * COLS : (i + 1) * COLS] = own
         x[HALF:, i * COLS : (i + 1) * COLS] = other
-    stores = []
-    wait(weight_loads)
+    up = jnp.concatenate([own_w[:512], got_w[:512]], 0)
+    down = jnp.concatenate([w[512 + 256 * j : 768 + 256 * j] for w in (own_w, got_w) for j in range(2)], 1)
     for i in range(rows):
-        hidden = gelu(dot(up[...], x[:, i * COLS : (i + 1) * COLS]))
-        value = dot(down[...], hidden).astype(BF16)
-        kept_v[i] = value[:HALF]
-        sent_v[i] = value[HALF:]
-        stores += start([(sent_v.at[i], sent.at[i]), (kept_v.at[i], kept.at[i])], sems, used)
-        used += 2
-    wait(stores)
+        hidden = gelu(dot(up, x[:, i * COLS : (i + 1) * COLS]))
+        value = dot(down, hidden).astype(BF16)
+        kept[i] = value[:HALF]
+        sent[i] = value[HALF:]
 
 
 def regrid_kernel(source, own, swap, e1, e2, swap_e1, swap_e2, w, later, out, table):
@@ -294,7 +280,8 @@
         turn_kernel,
         [sds((1024, 256))] * 2,
         (atm_up, atm_down),
-        [WHOLE] * 2,
+        [ANY] * 2,
+        [pltpu.VMEM(v.shape, v.dtype) for v in (atm_up, atm_down)] + [pltpu.SemaphoreType.DMA((2,))],
         name="turn",
     )
     got_blocks = across(blocks_sent)
@@ -305,7 +292,9 @@
         + [sds((b - a, HALF, COLS)) for a, b in SENT]
         + [sds((9, HALF, COLS))],
         (atm_state, dw_kernel, atm_gain, ocean_gain),
-        [WHOLE] * 4,
+        [ANY] * 4,
+        [pltpu.VMEM(v.shape, v.dtype) for v in (atm_state, dw_kernel, atm_gain, ocean_gain)]
+        + [pltpu.SemaphoreType.DMA((5,))],
         name="open",
     )
     head = partner(head_sent)
@@ -314,8 +303,10 @@
         ocean_kernel,
         [sds((HALF, cells), F32), sds((HALF, cells)), sds((2, HALF, COLS))],
         (ocean_state, ocean_theirs, own_p, head, keep, ocean_up, ocean_down, blocks),
-        [WHOLE] * 7 + [ANY],
-        [pltpu.VMEM((256, cells), BF16)],
+        [ANY] + [WHOLE] * 4 + [ANY] * 3,
+        [pltpu.VMEM((256, cells), BF16)]
+        + [pltpu.VMEM(v.shape, v.dtype) for v in (ocean_state, ocean_up, ocean_down)]
+        + [pltpu.SemaphoreType.DMA((3,))],
         out_specs=[WHOLE] * 3,
         name="ocean",
         flops=OCEAN_COST,
@@ -335,40 +326,30 @@
     swapped = move(slots, lambda t, c: (t ^ 1, c))
     kept_rows, got_rows = [], []
     for a, b in MIXED:
-        ins, runs_own, runs_other = [keep], [], []
-        first = max(a - 1, 0)
-        if a == 0:
-            runs_own.append((1, 0, 1, 0))
-            runs_other += [(1, 1, 1, 0), (2, None, 1, 1)]
-            ins += [edges, head]
-        runs_own.append((0, first, b + 1 - first, first - a + 1))
-        for (p, q), g in zip(SENT, got):
-            p, q = max(p, first), min(q, b + 1)
-            if p < q:
-                runs_other.append((len(ins), p - SENT[[x is g for x in got].index(True)][0], q - p, p - a + 1))
-                ins.append(g)
+        ins, own_lines, other_lines = [keep], [], []
+        for j in range(a - 1, b + 1):
+            if j < 0:
+                own_lines.append((len(ins), 0))
+                other_lines.append((len(ins), 1))
+                ins.append(edges)
+                continue
+            own_lines.append((0, j))
+            if j == 0:
+                other_lines.append((len(ins), None))
+                ins.append(head)
+                continue
+            k = [n for n, (p, q) in enumerate(SENT) if p <= j < q][0]
+            place = [n for n, x in enumerate(ins) if x is got[k]] or [len(ins)]
+            ins += [got[k]] * (place[0] == len(ins))
+            other_lines.append((place[0], j - SENT[k][0]))
         rows, leads = b - a, not kept_rows
-        out = [sds((rows, HALF, COLS))] * 2
-        scratch = [
-            pltpu.VMEM((16, HALF), F32),
-            pltpu.VMEM((16, COLS), BF16),
-            pltpu.VMEM((rows + 2, HALF, COLS), BF16),
-            pltpu.VMEM((rows + 2, HALF, COLS), BF16),
-            pltpu.VMEM((CHANNELS, rows * COLS), BF16),
-            pltpu.VMEM((1024, 256), BF16),
-            pltpu.VMEM((256, 1024), BF16),
-            pltpu.VMEM((rows, HALF, COLS), BF16),
-            pltpu.VMEM((rows, HALF, COLS), BF16),
-            pltpu.SemaphoreType.DMA((40,)),
-        ]
-        args = (own_p, head, blocks, got_blocks, *ins, *((edges, got[-1]) if leads else ()))
+        order = (edges, got[-1]) if leads else ()
         kept, sent = call(
-            functools.partial(mix_kernel, rows, runs_own, runs_other, len(ins), leads),
-            out,
-            args,
-            [ANY] * len(args),
-            scratch,
-            out_specs=[ANY] * len(out),
+            functools.partial(mix_kernel, rows, own_lines, other_lines, len(ins), len(order)),
+            [sds((rows, HALF, COLS))] * 2,
+            (own_p, head, blocks, got_blocks, *ins, *order),
+            [WHOLE] * (4 + len(ins)) + [ANY] * len(order),
+            [pltpu.VMEM((CHANNELS, rows * COLS), BF16)],
             name="mix",
             flops=MIX_COST if leads else 0,
         )

time: 53.9 us -> 48.8 us (0.905)
  Pallas kernels: 26.8 us -> 12.3 us
  local copies, waits for them, and re-layouts: 0 us -> 7.95 us
  waiting for transfers between devices: 1.63 us -> 4.89 us
  starting transfers between devices: 23.4 us -> 21.9 us
    pallas_call x8, Pallas kernels: 26.8 us -> 12.3 us  [call(): pl.pallas_call(kernel, out_shape=out, in_specs=specs, out_specs=kw.pop('o...]
    unnamed x0 -> x26, local copies, waits for them, and re-layouts: none -> 7.95 us
    ppermute x14, waiting for transfers between devices: 1.63 us -> 4.89 us  [move(): return lax.ppermute(x, AXES, route)]
    ppermute x14, starting transfers between devices: 23.4 us -> 21.9 us  [move(): return lax.ppermute(x, AXES, route)]
  transfers between devices with their start and end apart: 14 -> 14, of which waited for: 3 -> 5; matrix products, arithmetic and copies ran while one was open for 0% -> 0% of each run, Pallas kernels for 44% -> 21%
where the time goes in v5:
time: 48.8 us; the launch traced here: 48.4 us
  starting transfers between devices  21.9 us (45%)
  Pallas kernels  12.3 us (25%)
  local copies, waits for them, and re-layouts  7.95 us (16%)
  waiting for transfers between devices  4.89 us (10%)
  between operations  1.44 us (3%)
    ppermute x14, starting transfers between devices, move(): return lax.ppermute(x, AXES, route)  21.9 us
    pallas_call x8, Pallas kernels, call(): pl.pallas_call(kernel, out_shape=out, in_specs=specs, out_specs=kw.pop('o...  12.3 us
    unnamed x26, local copies, waits for them, and re-layouts  7.95 us
    ppermute x14, waiting for transfers between devices, move(): return lax.ppermute(x, AXES, route)  4.89 us
  transfers between devices with their start and end apart: 14, of which 5 were waited for; matrix products, arithmetic and copies ran while one was open for 0% of the time, Pallas kernels for 21%

profile of v5, /device:TPU:24, one launch (start us, length us, event | category | flops | bytes accessed | tf_op | source)
XLA Modules:
  0.0 48.4 jit_solution(571734214840746555)
XLA Ops:
  0.6 1.6 %collective-permute-start = (bf16[128,512]{1,0:T(8,128)(2,1)}, bf16[128,512]{1,0:T(8,128)(2,1)S(1)}, u32[]{:S(2)}, u32[]{:S(2)}) collective-permute-start(bf16[128,512]{1,0:T(8,128)(2,1)} %state.2), channel_id=1, source_target_pairs={{0,1},{1,0},{2,3},{3,2},{4,5},{5,4},{6,7},{7,6},{8,9},{9,8},{10,11... | collective-permute-start | bytes 393224 | tf_op jit(solution)/shard_map/ppermute | solution.py:269
  2.2 1.2 %copy-done = bf16[128,16,256]{2,1,0:T(8,128)(2,1)S(1)} copy-done((bf16[128,16,256]{2,1,0:T(8,128)(2,1)S(1)}, bf16[128,16,256]{2,1,0:T(8,128)(2,1)}, u32[]{:S(2)}) %copy-start) | copy-done | bytes 1048600
  3.4 0.7 %copy-done.7 = f32[9,128]{1,0:T(8,128)S(1)} copy-done((f32[9,128]{1,0:T(8,128)S(1)}, f32[9,128]{1,0:T(8,128)}, u32[]{:S(2)}) %copy-start.7) | copy-done | bytes 4632
  4.1 0.7 %copy-done.9 = bf16[128]{0:T(256)(128)(2,1)S(1)} copy-done((bf16[128]{0:T(256)(128)(2,1)S(1)}, bf16[128]{0:T(256)(128)(2,1)}, u32[]{:S(2)}) %copy-start.9) | copy-done | bytes 280
  4.8 0.7 %copy-done.10 = bf16[128]{0:T(256)(128)(2,1)S(1)} copy-done((bf16[128]{0:T(256)(128)(2,1)S(1)}, bf16[128]{0:T(256)(128)(2,1)}, u32[]{:S(2)}) %copy-start.10) | copy-done | bytes 280
  5.4 0.9 %open.1 = (bf16[144,256]{1,0:T(8,128)(2,1)S(1)}, f32[16,128]{1,0:T(8,128)S(1)}, bf16[6,128,256]{2,1,0:T(8,128)(2,1)S(1)}, bf16[2,128,256]{2,1,0:T(8,128)(2,1)S(1)}, bf16[9,128,256]{2,1,0:T(8,128)(2,1)S(1)}) custom-call(bf16[128,16,256]{2,1,0:T(8,128)(2,1)S(1)} %copy-done, f32[9,128]{1,0:T(8,128)S(1)} %copy-done.7, bf16[128]{0:T(256)(128)(2,1)S(1)} %copy-done.9, ...), custom_call_target="tpu_custom_call" | custom-call | tf_op jit(solution)/shard_map/open/pallas_call | solution.py:35
  6.3 0.6 %collective-permute-start.1 = (bf16[144,256]{1,0:T(8,128)(2,1)S(1)}, bf16[144,256]{1,0:T(8,128)(2,1)S(1)}, u32[]{:S(2)}, u32[]{:S(2)}) collective-permute-start(bf16[144,256]{1,0:T(8,128)(2,1)S(1)} %get-tuple-element.20), channel_id=1, source_target_pairs={{0,1},{1,0},{2,3},{3,2},{4,5},{5,4},{6,7},{7,6},{8,9},{9,8},{10,11... | collective-permute-start | bytes 221192 | tf_op jit(solution)/shard_map/ppermute | solution.py:269
  6.9 1.5 %collective-permute-start.9 = (bf16[6,128,256]{2,1,0:T(8,128)(2,1)S(1)}, bf16[6,128,256]{2,1,0:T(8,128)(2,1)S(1)}, u32[]{:S(2)}, u32[]{:S(2)}) collective-permute-start(bf16[6,128,256]{2,1,0:T(8,128)(2,1)S(1)} %get-tuple-element.28), channel_id=1, source_target_pairs={{0,1},{1,0},{2,3},{3,2},{4,5},{5,4},{6,7},{7,6},{8,9},{9,8},{10,11... | collective-permute-start | bytes 1179656 | tf_op jit(solution)/shard_map/ppermute | solution.py:269
  8.4 0.9 %copy-done.3 = bf16[256,512]{1,0:T(8,128)(2,1)S(1)} copy-done((bf16[256,512]{1,0:T(8,128)(2,1)S(1)}, bf16[256,512]{1,0:T(8,128)(2,1)}, u32[]{:S(2)}) %copy-start.3) | copy-done | bytes 262168
  9.4 0.9 %copy-done.4 = bf16[512,256]{1,0:T(8,128)(2,1)S(1)} copy-done((bf16[512,256]{1,0:T(8,128)(2,1)S(1)}, bf16[512,256]{1,0:T(8,128)(2,1)}, u32[]{:S(2)}) %copy-start.4) | copy-done | bytes 262168
  10.3 0.4 turn.1
  10.7 2.2 %collective-permute-start.8 = (bf16[1024,256]{1,0:T(8,128)(2,1)S(1)}, bf16[1024,256]{1,0:T(8,128)(2,1)S(1)}, u32[]{:S(2)}, u32[]{:S(2)}) collective-permute-start(bf16[1024,256]{1,0:T(8,128)(2,1)S(1)} %get-tuple-element.27), channel_id=1, source_target_pairs={{0,17},{1,16},{2,19},{3,18},{4,21},{5,20},{6,23},{7,22},{8,25},{9,... | collective-permute-start | bytes 1572872 | tf_op jit(solution)/shard_map/ppermute | solution.py:269
  12.9 0.0 collective-permute-done.1.head.refs_2_
  12.9 0.0 collective-permute-done.theirs
  12.9 0.9 %copy-done.5 = bf16[128,512]{1,0:T(8,128)(2,1)S(1)} copy-done((bf16[128,512]{1,0:T(8,128)(2,1)S(1)}, bf16[128,512]{1,0:T(8,128)(2,1)}, u32[]{:S(2)}) %copy-start.5) | copy-done | bytes 131096
  13.8 0.9 %copy-done.11 = bf16[256,512]{1,0:T(8,128)(2,1)S(1)} copy-done((bf16[256,512]{1,0:T(8,128)(2,1)S(1)}, bf16[256,512]{1,0:T(8,128)(2,1)}, u32[]{:S(2)}) %copy-start.11) | copy-done | bytes 262168
  14.7 0.9 %copy-done.12 = bf16[512,256]{1,0:T(8,128)(2,1)S(1)} copy-done((bf16[512,256]{1,0:T(8,128)(2,1)S(1)}, bf16[512,256]{1,0:T(8,128)(2,1)}, u32[]{:S(2)}) %copy-start.12) | copy-done | bytes 262168
  15.7 1.1 %ocean.1 = (f32[128,512]{1,0:T(8,128)S(1)}, bf16[128,512]{1,0:T(8,128)(2,1)S(1)}, bf16[2,128,256]{2,1,0:T(8,128)(2,1)S(1)}) custom-call(bf16[128,512]{1,0:T(8,128)(2,1)S(1)} %copy-done.5, bf16[128,512]{1,0:T(8,128)(2,1)S(1)} %collective-permute-done.theirs, f32[16,128]{1,0:T(8,128)S(1)} %get-tuple-element.19.own_p, ...), custom_call_target="tpu_custom_call" | custom-call | flops 8000000000 | tf_op jit(solution)/shard_map/ocean/pallas_call | solution.py:35
  16.8 0.7 %collective-permute-start.2 = (bf16[128,512]{1,0:T(8,128)(2,1)S(1)}, bf16[128,512]{1,0:T(8,128)(2,1)S(1)}, u32[]{:S(2)}, u32[]{:S(2)}) collective-permute-start(bf16[128,512]{1,0:T(8,128)(2,1)S(1)} %get-tuple-element.24), channel_id=1, source_target_pairs={{0,1},{1,0},{2,3},{3,2},{4,5},{5,4},{6,7},{7,6},{8,9},{9,8},{10,11... | collective-permute-start | bytes 393224 | tf_op jit(solution)/shard_map/ppermute | solution.py:269
  18.1 5.6 %collective-permute-start.10 = (bf16[2,128,256]{2,1,0:T(8,128)(2,1)S(1)}, bf16[2,128,256]{2,1,0:T(8,128)(2,1)S(1)}, u32[]{:S(2)}, u32[]{:S(2)}) collective-permute-start(bf16[2,128,256]{2,1,0:T(8,128)(2,1)S(1)} %get-tuple-element.29), channel_id=1, source_target_pairs={{1,3},{2,4},{3,1},{4,2},{5,7},{6,8},{7,5},{8,6},{9,11},{10,12},{11... | collective-permute-start | bytes 393224 | tf_op jit(solution)/shard_map/ppermute | solution.py:269
  23.7 0.0 collective-permute-done.2.got
  23.7 0.0 copy-done.6
  23.7 0.7 %result.1 = (bf16[128,512]{1,0:T(8,128)(2,1)}, bf16[4,128,128]{2,1,0:T(8,128)(2,1)S(1)}, bf16[2,128,256]{2,1,0:T(8,128)(2,1)S(1)}) custom-call(s32[1]{0:T(128)S(6)} %copy.16.count, bf16[128,512]{1,0:T(8,128)(2,1)S(1)} %copy-done.6, f32[128,512]{1,0:T(8,128)S(1)} %get-tuple-element.23.kept, ...), custom_call_target="tpu_custom_call", output_to_operand_aliasing={{2}: (4, {})} | custom-call | tf_op jit(solution)/shard_map/result/pallas_call | solution.py:35
  24.4 0.0 collective-permute-start.11
  24.4 6.9 %collective-permute-start.4 = (bf16[4,128,128]{2,1,0:T(8,128)(2,1)S(1)}, bf16[4,128,128]{2,1,0:T(8,128)(2,1)S(1)}, u32[]{:S(2)}, u32[]{:S(2)}) collective-permute-start(bf16[4,128,128]{2,1,0:T(8,128)(2,1)S(1)} %get-tuple-element.26.own), channel_id=1, source_target_pairs={{4,8},{5,9},{6,10},{7,11},{8,4},{9,5},{10,6},{11,7},{12,16},{13,17... | collective-permute-start | bytes 393224 | tf_op jit(solution)/shard_map/ppermute | solution.py:269
  31.3 0.0 collective-permute-done.10.refs_2_.refs_1_
  31.3 0.1 collective-permute-start.5
  31.4 0.0 collective-permute-done.11.refs_3_
  31.4 0.0 collective-permute-done.9.refs_1_.refs_4_
  31.4 0.0 collective-permute-done.8.got_w
  31.5 2.7 %mix.2 = (bf16[4,128,256]{2,1,0:T(8,128)(2,1)S(1)}, bf16[4,128,256]{2,1,0:T(8,128)(2,1)S(1)}) custom-call(f32[16,128]{1,0:T(8,128)S(1)} %get-tuple-element.19.own_p, bf16[144,256]{1,0:T(8,128)(2,1)S(1)} %collective-permute-done.1.head.refs_2_, bf16[1024,256]{1,0:T(8,128)(2,1)S(1)} %get-tuple-element.22.before.own_w, ...), custom_call_target="tpu_custom_call" | custom-call | flops 30000001024 | tf_op jit(solution)/shard_map/mix/pallas_call | solution.py:35
  34.1 0.0 copy-start.2
  34.1 0.0 copy-start.8
  34.2 0.5 %collective-permute-start.12 = (bf16[4,128,256]{2,1,0:T(8,128)(2,1)S(1)}, bf16[4,128,256]{2,1,0:T(8,128)(2,1)S(1)}, u32[]{:S(2)}, u32[]{:S(2)}) collective-permute-start(bf16[4,128,256]{2,1,0:T(8,128)(2,1)S(1)} %get-tuple-element.31), channel_id=1, source_target_pairs={{0,1},{1,0},{2,3},{3,2},{4,5},{5,4},{6,7},{7,6},{8,9},{9,8},{10,11... | collective-permute-start | bytes 786440 | tf_op jit(solution)/shard_map/ppermute | solution.py:269
  34.7 2.7 %mix.3 = (bf16[4,128,256]{2,1,0:T(8,128)(2,1)S(1)}, bf16[4,128,256]{2,1,0:T(8,128)(2,1)S(1)}) custom-call(f32[16,128]{1,0:T(8,128)S(1)} %get-tuple-element.19.own_p, bf16[144,256]{1,0:T(8,128)(2,1)S(1)} %collective-permute-done.1.head.refs_2_, bf16[1024,256]{1,0:T(8,128)(2,1)S(1)} %get-tuple-element.22.before.own_w, ...), custom_call_target="tpu_custom_call" | custom-call | tf_op jit(solution)/shard_map/mix/pallas_call | solution.py:35
  37.4 1.6 %collective-permute-start.13 = (bf16[4,128,256]{2,1,0:T(8,128)(2,1)S(1)}, bf16[4,128,256]{2,1,0:T(8,128)(2,1)S(1)}, u32[]{:S(2)}, u32[]{:S(2)}) collective-permute-start(bf16[4,128,256]{2,1,0:T(8,128)(2,1)S(1)} %get-tuple-element.34), channel_id=1, source_target_pairs={{0,1},{1,0},{2,3},{3,2},{4,5},{5,4},{6,7},{7,6},{8,9},{9,8},{10,11... | collective-permute-start | bytes 786440 | tf_op jit(solution)/shard_map/ppermute | solution.py:269
  39.1 0.0 collective-permute-start.3
  39.1 0.0 collective-permute-done.4.e1
  39.1 0.5 %collective-permute-start.6 = (bf16[4,128,128]{2,1,0:T(8,128)(2,1)S(1)}, bf16[4,128,128]{2,1,0:T(8,128)(2,1)S(1)}, u32[]{:S(2)}, u32[]{:S(2)}) collective-permute-start(bf16[4,128,128]{2,1,0:T(8,128)(2,1)S(1)} %collective-permute-done.4.e1), channel_id=1, source_target_pairs={{0,2},{1,3},{2,0},{3,1},{4,6},{5,7},{6,4},{7,5},{8,10},{9,11},{10,... | collective-permute-start | bytes 393224 | tf_op jit(solution)/shard_map/ppermute | solution.py:269
  39.6 0.0 collective-permute-done.5.e2
  39.6 0.1 collective-permute-start.7
  39.7 0.7 %collective-permute-done.3.swap = bf16[4,128,128]{2,1,0:T(8,128)(2,1)S(1)} collective-permute-done((bf16[4,128,128]{2,1,0:T(8,128)(2,1)S(1)}, bf16[4,128,128]{2,1,0:T(8,128)(2,1)S(1)}, u32[]{:S(2)}, u32[]{:S(2)}) %collective-permute-start.3) | collective-permute-done | bytes 131104 | tf_op jit(solution)/shard_map/ppermute | solution.py:269
  40.4 0.2 collective-permute-done.6.swap_e1
  40.6 0.3 collective-permute-done.7.swap_e2
  40.9 2.5 %collective-permute-done.12.later.rest_2_ = bf16[4,128,256]{2,1,0:T(8,128)(2,1)S(1)} collective-permute-done((bf16[4,128,256]{2,1,0:T(8,128)(2,1)S(1)}, bf16[4,128,256]{2,1,0:T(8,128)(2,1)S(1)}, u32[]{:S(2)}, u32[]{:S(2)}) %collective-permute-start.12) | collective-permute-done | bytes 262176 | tf_op jit(solution)/shard_map/ppermute | solution.py:269
  43.4 1.9 %regrid.1 = bf16[16,128,256]{2,1,0:T(8,128)(2,1)S(1)} custom-call(s32[2,32]{1,0:T(2,128)S(1)} %bitcast.1, bf16[4,128,128]{2,1,0:T(8,128)(2,1)S(1)} %get-tuple-element.26.own, bf16[4,128,128]{2,1,0:T(8,128)(2,1)S(1)} %collective-permute-done.3.swap, bf16[4,128,128]{2,1,0:T(8,128)(2,1)S(1)} %collective-permute-done.4.e1, ...), custom_call_target="tpu_custom_call" | custom-call | tf_op jit(solution)/shard_map/regrid/pallas_call | solution.py:35
  45.3 1.1 %collective-permute-done.13.rest_3_ = bf16[4,128,256]{2,1,0:T(8,128)(2,1)S(1)} collective-permute-done((bf16[4,128,256]{2,1,0:T(8,128)(2,1)S(1)}, bf16[4,128,256]{2,1,0:T(8,128)(2,1)S(1)}, u32[]{:S(2)}, u32[]{:S(2)}) %collective-permute-start.13) | collective-permute-done | bytes 262176 | tf_op jit(solution)/shard_map/ppermute | solution.py:269
  46.4 2.0 %final.1 = bf16[128,16,256]{2,1,0:T(8,128)(2,1)} custom-call(bf16[128,16,256]{2,1,0:T(8,128)(2,1)S(1)} %copy-done.1, bf16[16,128,256]{2,1,0:T(8,128)(2,1)S(1)} %regrid.1, bf16[4,128,256]{2,1,0:T(8,128)(2,1)S(1)} %get-tuple-element.32.rest_0_, bf16[4,128,256]{2,1,0:T(8,128)(2,1)S(1)} %get-tuple-element.33.rest_1_, ...), custom_call_target="tpu_custom_call" | custom-call | tf_op jit(solution)/shard_map/final/pallas_call | solution.py:35
  (14 shorter events, 0.0 us)
Async XLA Ops:
  0.6 12.3 %collective-permute-start = (bf16[128,512]{1,0:T(8,128)(2,1)}, bf16[128,512]{1,0:T(8,128)(2,1)S(1)}, u32[]{:S(2)}, u32[]{:S(2)}) collective-permute-start(bf16[128,512]{1,0:T(8,128)(2,1)} %state.2), channel_id=1, source_target_pairs={{0,1},{1,0},{2,3},{3,2},{4,5},{5,4},{6,7},{7,6},{8,9},{9,8},{10,11... | collective-permute-start | bytes 393224 | tf_op jit(solution)/shard_map/ppermute | solution.py:269
  2.2 1.2 %copy-start = (bf16[128,16,256]{2,1,0:T(8,128)(2,1)S(1)}, bf16[128,16,256]{2,1,0:T(8,128)(2,1)}, u32[]{:S(2)}) copy-start(bf16[128,16,256]{2,1,0:T(8,128)(2,1)} %state.3) | copy-start | bytes 3145732
  3.4 0.7 %copy-start.7 = (f32[9,128]{1,0:T(8,128)S(1)}, f32[9,128]{1,0:T(8,128)}, u32[]{:S(2)}) copy-start(f32[9,128]{1,0:T(8,128)} %taps_in.1) | copy-start | bytes 13828
  4.1 0.7 %copy-start.9 = (bf16[128]{0:T(256)(128)(2,1)S(1)}, bf16[128]{0:T(256)(128)(2,1)}, u32[]{:S(2)}) copy-start(bf16[128]{0:T(256)(128)(2,1)} %atm_gain_in.1) | copy-start | bytes 772
  4.8 0.7 %copy-start.10 = (bf16[128]{0:T(256)(128)(2,1)S(1)}, bf16[128]{0:T(256)(128)(2,1)}, u32[]{:S(2)}) copy-start(bf16[128]{0:T(256)(128)(2,1)} %ocean_gain_in.1) | copy-start | bytes 772
  6.3 6.6 %collective-permute-start.1 = (bf16[144,256]{1,0:T(8,128)(2,1)S(1)}, bf16[144,256]{1,0:T(8,128)(2,1)S(1)}, u32[]{:S(2)}, u32[]{:S(2)}) collective-permute-start(bf16[144,256]{1,0:T(8,128)(2,1)S(1)} %get-tuple-element.20), channel_id=1, source_target_pairs={{0,1},{1,0},{2,3},{3,2},{4,5},{5,4},{6,7},{7,6},{8,9},{9,8},{10,11... | collective-permute-start | bytes 221192 | tf_op jit(solution)/shard_map/ppermute | solution.py:269
  6.9 24.5 %collective-permute-start.9 = (bf16[6,128,256]{2,1,0:T(8,128)(2,1)S(1)}, bf16[6,128,256]{2,1,0:T(8,128)(2,1)S(1)}, u32[]{:S(2)}, u32[]{:S(2)}) collective-permute-start(bf16[6,128,256]{2,1,0:T(8,128)(2,1)S(1)} %get-tuple-element.28), channel_id=1, source_target_pairs={{0,1},{1,0},{2,3},{3,2},{4,5},{5,4},{6,7},{7,6},{8,9},{9,8},{10,11... | collective-permute-start | bytes 1179656 | tf_op jit(solution)/shard_map/ppermute | solution.py:269
  8.4 0.9 %copy-start.3 = (bf16[256,512]{1,0:T(8,128)(2,1)S(1)}, bf16[256,512]{1,0:T(8,128)(2,1)}, u32[]{:S(2)}) copy-start(bf16[256,512]{1,0:T(8,128)(2,1)} %up_in.2) | copy-start | bytes 786436
  9.4 0.9 %copy-start.4 = (bf16[512,256]{1,0:T(8,128)(2,1)S(1)}, bf16[512,256]{1,0:T(8,128)(2,1)}, u32[]{:S(2)}) copy-start(bf16[512,256]{1,0:T(8,128)(2,1)} %down_in.2) | copy-start | bytes 786436
  10.7 20.7 %collective-permute-start.8 = (bf16[1024,256]{1,0:T(8,128)(2,1)S(1)}, bf16[1024,256]{1,0:T(8,128)(2,1)S(1)}, u32[]{:S(2)}, u32[]{:S(2)}) collective-permute-start(bf16[1024,256]{1,0:T(8,128)(2,1)S(1)} %get-tuple-element.27), channel_id=1, source_target_pairs={{0,17},{1,16},{2,19},{3,18},{4,21},{5,20},{6,23},{7,22},{8,25},{9,... | collective-permute-start | bytes 1572872 | tf_op jit(solution)/shard_map/ppermute | solution.py:269
  12.9 0.9 %copy-start.5 = (bf16[128,512]{1,0:T(8,128)(2,1)S(1)}, bf16[128,512]{1,0:T(8,128)(2,1)}, u32[]{:S(2)}) copy-start(bf16[128,512]{1,0:T(8,128)(2,1)} %state.2) | copy-start | bytes 393220
  13.8 0.9 %copy-start.11 = (bf16[256,512]{1,0:T(8,128)(2,1)S(1)}, bf16[256,512]{1,0:T(8,128)(2,1)}, u32[]{:S(2)}) copy-start(bf16[256,512]{1,0:T(8,128)(2,1)} %up_in.3) | copy-start | bytes 786436
  14.7 0.9 %copy-start.12 = (bf16[512,256]{1,0:T(8,128)(2,1)S(1)}, bf16[512,256]{1,0:T(8,128)(2,1)}, u32[]{:S(2)}) copy-start(bf16[512,256]{1,0:T(8,128)(2,1)} %down_in.3) | copy-start | bytes 786436
  15.7 8.0 %copy-start.6 = (bf16[128,512]{1,0:T(8,128)(2,1)S(1)}, bf16[128,512]{1,0:T(8,128)(2,1)}, u32[]{:S(2)}) copy-start(bf16[128,512]{1,0:T(8,128)(2,1)} %state.2) | copy-start | bytes 393220
  16.8 6.9 %collective-permute-start.2 = (bf16[128,512]{1,0:T(8,128)(2,1)S(1)}, bf16[128,512]{1,0:T(8,128)(2,1)S(1)}, u32[]{:S(2)}, u32[]{:S(2)}) collective-permute-start(bf16[128,512]{1,0:T(8,128)(2,1)S(1)} %get-tuple-element.24), channel_id=1, source_target_pairs={{0,1},{1,0},{2,3},{3,2},{4,5},{5,4},{6,7},{7,6},{8,9},{9,8},{10,11... | collective-permute-start | bytes 393224 | tf_op jit(solution)/shard_map/ppermute | solution.py:269
  18.1 13.2 %collective-permute-start.10 = (bf16[2,128,256]{2,1,0:T(8,128)(2,1)S(1)}, bf16[2,128,256]{2,1,0:T(8,128)(2,1)S(1)}, u32[]{:S(2)}, u32[]{:S(2)}) collective-permute-start(bf16[2,128,256]{2,1,0:T(8,128)(2,1)S(1)} %get-tuple-element.29), channel_id=1, source_target_pairs={{1,3},{2,4},{3,1},{4,2},{5,7},{6,8},{7,5},{8,6},{9,11},{10,12},{11... | collective-permute-start | bytes 393224 | tf_op jit(solution)/shard_map/ppermute | solution.py:269
  24.4 7.0 %collective-permute-start.11 = (bf16[2,128,256]{2,1,0:T(8,128)(2,1)S(1)}, bf16[2,128,256]{2,1,0:T(8,128)(2,1)S(1)}, u32[]{:S(2)}, u32[]{:S(2)}) collective-permute-start(bf16[2,128,256]{2,1,0:T(8,128)(2,1)S(1)} %get-tuple-element.30), channel_id=1, source_target_pairs={{0,1},{1,0},{2,3},{3,2},{4,5},{5,4},{6,7},{7,6},{8,9},{9,8},{10,11... | collective-permute-start | bytes 393224 | tf_op jit(solution)/shard_map/ppermute | solution.py:269
  24.4 14.6 %collective-permute-start.4 = (bf16[4,128,128]{2,1,0:T(8,128)(2,1)S(1)}, bf16[4,128,128]{2,1,0:T(8,128)(2,1)S(1)}, u32[]{:S(2)}, u32[]{:S(2)}) collective-permute-start(bf16[4,128,128]{2,1,0:T(8,128)(2,1)S(1)} %get-tuple-element.26.own), channel_id=1, source_target_pairs={{4,8},{5,9},{6,10},{7,11},{8,4},{9,5},{10,6},{11,7},{12,16},{13,17... | collective-permute-start | bytes 393224 | tf_op jit(solution)/shard_map/ppermute | solution.py:269
  31.3 8.3 %collective-permute-start.5 = (bf16[4,128,128]{2,1,0:T(8,128)(2,1)S(1)}, bf16[4,128,128]{2,1,0:T(8,128)(2,1)S(1)}, u32[]{:S(2)}, u32[]{:S(2)}) collective-permute-start(bf16[4,128,128]{2,1,0:T(8,128)(2,1)S(1)} %get-tuple-element.26.own), channel_id=1, source_target_pairs={{0,4},{1,5},{2,6},{3,7},{4,0},{5,1},{6,2},{7,3},{8,12},{9,13},{10,... | collective-permute-start | bytes 393224 | tf_op jit(solution)/shard_map/ppermute | solution.py:269
  34.1 9.2 %copy-start.2 = (bf16[32,2,128,128]{3,2,1,0:T(8,128)(2,1)S(1)}, bf16[32,2,128,128]{3,2,1,0:T(8,128)(2,1)}, u32[]{:S(2)}) copy-start(bf16[32,2,128,128]{3,2,1,0:T(8,128)(2,1)} %w.1) | copy-start | bytes 6291460
  34.1 9.2 %copy-start.8 = (s32[32,2]{0,1:T(2,128)S(1)}, s32[32,2]{0,1:T(2,128)}, u32[]{:S(2)}) copy-start(s32[32,2]{0,1:T(2,128)} %param.15) | copy-start | bytes 772
  34.2 9.2 %collective-permute-start.12 = (bf16[4,128,256]{2,1,0:T(8,128)(2,1)S(1)}, bf16[4,128,256]{2,1,0:T(8,128)(2,1)S(1)}, u32[]{:S(2)}, u32[]{:S(2)}) collective-permute-start(bf16[4,128,256]{2,1,0:T(8,128)(2,1)S(1)} %get-tuple-element.31), channel_id=1, source_target_pairs={{0,1},{1,0},{2,3},{3,2},{4,5},{5,4},{6,7},{7,6},{8,9},{9,8},{10,11... | collective-permute-start | bytes 786440 | tf_op jit(solution)/shard_map/ppermute | solution.py:269
  37.4 9.0 %collective-permute-start.13 = (bf16[4,128,256]{2,1,0:T(8,128)(2,1)S(1)}, bf16[4,128,256]{2,1,0:T(8,128)(2,1)S(1)}, u32[]{:S(2)}, u32[]{:S(2)}) collective-permute-start(bf16[4,128,256]{2,1,0:T(8,128)(2,1)S(1)} %get-tuple-element.34), channel_id=1, source_target_pairs={{0,1},{1,0},{2,3},{3,2},{4,5},{5,4},{6,7},{7,6},{8,9},{9,8},{10,11... | collective-permute-start | bytes 786440 | tf_op jit(solution)/shard_map/ppermute | solution.py:269
  39.1 1.3 %collective-permute-start.3 = (bf16[4,128,128]{2,1,0:T(8,128)(2,1)S(1)}, bf16[4,128,128]{2,1,0:T(8,128)(2,1)S(1)}, u32[]{:S(2)}, u32[]{:S(2)}) collective-permute-start(bf16[4,128,128]{2,1,0:T(8,128)(2,1)S(1)} %get-tuple-element.26.own), channel_id=1, source_target_pairs={{0,2},{1,3},{2,0},{3,1},{4,6},{5,7},{6,4},{7,5},{8,10},{9,11},{10,... | collective-permute-start | bytes 393224 | tf_op jit(solution)/shard_map/ppermute | solution.py:269
  39.1 1.5 %collective-permute-start.6 = (bf16[4,128,128]{2,1,0:T(8,128)(2,1)S(1)}, bf16[4,128,128]{2,1,0:T(8,128)(2,1)S(1)}, u32[]{:S(2)}, u32[]{:S(2)}) collective-permute-start(bf16[4,128,128]{2,1,0:T(8,128)(2,1)S(1)} %collective-permute-done.4.e1), channel_id=1, source_target_pairs={{0,2},{1,3},{2,0},{3,1},{4,6},{5,7},{6,4},{7,5},{8,10},{9,11},{10,... | collective-permute-start | bytes 393224 | tf_op jit(solution)/shard_map/ppermute | solution.py:269
  39.6 1.3 %collective-permute-start.7 = (bf16[4,128,128]{2,1,0:T(8,128)(2,1)S(1)}, bf16[4,128,128]{2,1,0:T(8,128)(2,1)S(1)}, u32[]{:S(2)}, u32[]{:S(2)}) collective-permute-start(bf16[4,128,128]{2,1,0:T(8,128)(2,1)S(1)} %collective-permute-done.5.e2), channel_id=1, source_target_pairs={{0,2},{1,3},{2,0},{3,1},{4,6},{5,7},{6,4},{7,5},{8,10},{9,11},{10,... | collective-permute-start | bytes 393224 | tf_op jit(solution)/shard_map/ppermute | solution.py:269
  43.4 3.0 %copy-start.1 = (bf16[128,16,256]{2,1,0:T(8,128)(2,1)S(1)}, bf16[128,16,256]{2,1,0:T(8,128)(2,1)}, u32[]{:S(2)}) copy-start(bf16[128,16,256]{2,1,0:T(8,128)(2,1)} %state.3) | copy-start | bytes 3145732

commit v6 on v5

--- a/solution.py
+++ b/solution.py
@@ -147,7 +147,7 @@
 
 
 def ocean_kernel(
-    mine_in, theirs, own_p, head, keep, up_in, down_in, before, kept, sent, pair, x, mine, up, down, sems
+    mine_in, theirs, own_p, head, keep, up_in, down_in, before, passing, kept, sent, pair, passed, x, mine, up, down, sems
 ):
     loads = start([(mine_in, mine), (up_in, up), (down_in, down)], sems, 0)
     pair[0] = keep[0]
@@ -166,7 +166,7 @@
     sent[...] = total[HALF:].astype(BF16)
 
 
-def ocean_result_kernel(count, state, kept, got, passing, result, slots, passed):
+def ocean_result_kernel(count, state, kept, got, result, slots):
     for s in range(SLOTS):
         cells = slice(s * CELLS_PER_TILE, (s + 1) * CELLS_PER_TILE)
         value = state[:, cells].astype(F32) + (kept[:, cells] + got[:, cells].astype(F32))
@@ -296,30 +296,30 @@
         [pltpu.VMEM(v.shape, v.dtype) for v in (atm_state, dw_kernel, atm_gain, ocean_gain)]
         + [pltpu.SemaphoreType.DMA((5,))],
         name="open",
+        flops=4 * 10**9,
     )
     head = partner(head_sent)
     cells = ocean_state.shape[1]
-    ocean_kept, ocean_sent, pair = call(
+    ocean_kept, ocean_sent, pair, last_sent = call(
         ocean_kernel,
-        [sds((HALF, cells), F32), sds((HALF, cells)), sds((2, HALF, COLS))],
-        (ocean_state, ocean_theirs, own_p, head, keep, ocean_up, ocean_down, blocks),
-        [ANY] + [WHOLE] * 4 + [ANY] * 3,
+        [sds((HALF, cells), F32), sds((HALF, cells)), sds((2, HALF, COLS)), sds(sends[-1].shape)],
+        (ocean_state, ocean_theirs, own_p, head, keep, ocean_up, ocean_down, blocks, sends[-1]),
+        [ANY] + [WHOLE] * 4 + [ANY] * 4,
         [pltpu.VMEM((256, cells), BF16)]
         + [pltpu.VMEM(v.shape, v.dtype) for v in (ocean_state, ocean_up, ocean_down)]
         + [pltpu.SemaphoreType.DMA((3,))],
-        out_specs=[WHOLE] * 3,
+        out_specs=[WHOLE] * 3 + [ANY],
+        input_output_aliases={8: 3},
         name="ocean",
         flops=OCEAN_COST,
     )
     ocean_got = partner(ocean_sent)
     edges = move(pair, lambda t, c: (t - 1 + 2 * ((t + c) % 2), c))
-    ocean_result, slots, last_sent = call(
+    ocean_result, slots = call(
         ocean_result_kernel,
-        [sds((HALF, cells)), sds((SLOTS, HALF, CELLS_PER_TILE)), sds(sends[-1].shape)],
-        (ocean_count, ocean_state, ocean_kept, ocean_got, sends[-1]),
-        [SMEM, WHOLE, WHOLE, WHOLE, ANY],
-        out_specs=[WHOLE, WHOLE, ANY],
-        input_output_aliases={4: 2},
+        [sds((HALF, cells)), sds((SLOTS, HALF, CELLS_PER_TILE))],
+        (ocean_count, ocean_state, ocean_kept, ocean_got),
+        [SMEM, WHOLE, WHOLE, WHOLE],
         name="result",
     )
     got = [partner(s) for s in (*sends[:-1], last_sent)]

time: 48.8 us -> 48.4 us (level)
  local copies, waits for them, and re-layouts: 7.95 us -> 3.27 us
  waiting for transfers between devices: 4.89 us -> 7.89 us
  starting transfers between devices: 21.9 us -> 23.2 us
    unnamed x26 -> x24, local copies, waits for them, and re-layouts: 7.95 us -> 3.27 us
    ppermute x14, waiting for transfers between devices: 4.89 us -> 7.89 us  [move(): return lax.ppermute(x, AXES, route)]
    ppermute x14, starting transfers between devices: 21.9 us -> 23.2 us  [move(): return lax.ppermute(x, AXES, route)]
  transfers between devices with their start and end apart: 14 -> 14, of which waited for: 5 -> 7; matrix products, arithmetic and copies ran while one was open for 0% -> 0% of each run, Pallas kernels for 21% -> 21%
where the time goes in v6:
time: 48.4 us; the launch traced here: 48.1 us
  starting transfers between devices  23.2 us (48%)
  Pallas kernels  12.4 us (26%)
  waiting for transfers between devices  7.89 us (16%)
  local copies, waits for them, and re-layouts  3.27 us (7%)
  between operations  1.45 us (3%)
    ppermute x14, starting transfers between devices, move(): return lax.ppermute(x, AXES, route)  23.2 us
    pallas_call x8, Pallas kernels, call(): pl.pallas_call(kernel, out_shape=out, in_specs=specs, out_specs=kw.pop('o...  12.4 us
    ppermute x14, waiting for transfers between devices, move(): return lax.ppermute(x, AXES, route)  7.89 us
    unnamed x24, local copies, waits for them, and re-layouts  3.27 us
  transfers between devices with their start and end apart: 14, of which 7 were waited for; matrix products, arithmetic and copies ran while one was open for 0% of the time, Pallas kernels for 21%

profile of v6, /device:TPU:24, one launch (start us, length us, event | category | flops | bytes accessed | tf_op | source)
XLA Modules:
  0.0 48.1 jit_solution(17056898796089482630)
XLA Ops:
  0.6 1.6 %collective-permute-start = (bf16[128,512]{1,0:T(8,128)(2,1)}, bf16[128,512]{1,0:T(8,128)(2,1)S(1)}, u32[]{:S(2)}, u32[]{:S(2)}) collective-permute-start(bf16[128,512]{1,0:T(8,128)(2,1)} %state.2), channel_id=1, source_target_pairs={{0,1},{1,0},{2,3},{3,2},{4,5},{5,4},{6,7},{7,6},{8,9},{9,8},{10,11... | collective-permute-start | bytes 393224 | tf_op jit(solution)/shard_map/ppermute | solution.py:269
  2.2 1.2 %copy-done.1 = bf16[128,16,256]{2,1,0:T(8,128)(2,1)S(1)} copy-done((bf16[128,16,256]{2,1,0:T(8,128)(2,1)S(1)}, bf16[128,16,256]{2,1,0:T(8,128)(2,1)}, u32[]{:S(2)}) %copy-start.1) | copy-done | bytes 1048600
  3.4 0.7 %copy-done.9 = f32[9,128]{1,0:T(8,128)S(1)} copy-done((f32[9,128]{1,0:T(8,128)S(1)}, f32[9,128]{1,0:T(8,128)}, u32[]{:S(2)}) %copy-start.9) | copy-done | bytes 4632
  4.1 0.7 %copy-done.10 = bf16[128]{0:T(256)(128)(2,1)S(1)} copy-done((bf16[128]{0:T(256)(128)(2,1)S(1)}, bf16[128]{0:T(256)(128)(2,1)}, u32[]{:S(2)}) %copy-start.10) | copy-done | bytes 280
  4.8 0.7 %copy-done.11 = bf16[128]{0:T(256)(128)(2,1)S(1)} copy-done((bf16[128]{0:T(256)(128)(2,1)S(1)}, bf16[128]{0:T(256)(128)(2,1)}, u32[]{:S(2)}) %copy-start.11) | copy-done | bytes 280
  5.4 0.0 copy-start.8
  5.5 0.9 %open.1 = (bf16[144,256]{1,0:T(8,128)(2,1)S(1)}, f32[16,128]{1,0:T(8,128)S(1)}, bf16[6,128,256]{2,1,0:T(8,128)(2,1)S(1)}, bf16[2,128,256]{2,1,0:T(8,128)(2,1)S(1)}, bf16[9,128,256]{2,1,0:T(8,128)(2,1)S(1)}) custom-call(bf16[128,16,256]{2,1,0:T(8,128)(2,1)S(1)} %copy-done.1, f32[9,128]{1,0:T(8,128)S(1)} %copy-done.9, bf16[128]{0:T(256)(128)(2,1)S(1)} %copy-done.10, ...), custom_call_target="tpu_custom_call" | custom-call | flops 4000000000 | tf_op jit(solution)/shard_map/open/pallas_call | solution.py:35
  6.3 0.6 %collective-permute-start.1 = (bf16[144,256]{1,0:T(8,128)(2,1)S(1)}, bf16[144,256]{1,0:T(8,128)(2,1)S(1)}, u32[]{:S(2)}, u32[]{:S(2)}) collective-permute-start(bf16[144,256]{1,0:T(8,128)(2,1)S(1)} %get-tuple-element.20), channel_id=1, source_target_pairs={{0,1},{1,0},{2,3},{3,2},{4,5},{5,4},{6,7},{7,6},{8,9},{9,8},{10,11... | collective-permute-start | bytes 221192 | tf_op jit(solution)/shard_map/ppermute | solution.py:269
  6.9 1.5 %collective-permute-start.9 = (bf16[6,128,256]{2,1,0:T(8,128)(2,1)S(1)}, bf16[6,128,256]{2,1,0:T(8,128)(2,1)S(1)}, u32[]{:S(2)}, u32[]{:S(2)}) collective-permute-start(bf16[6,128,256]{2,1,0:T(8,128)(2,1)S(1)} %get-tuple-element.28), channel_id=1, source_target_pairs={{0,1},{1,0},{2,3},{3,2},{4,5},{5,4},{6,7},{7,6},{8,9},{9,8},{10,11... | collective-permute-start | bytes 1179656 | tf_op jit(solution)/shard_map/ppermute | solution.py:269
  8.4 0.0 copy-done.3
  8.4 0.0 copy-done.4
  8.4 0.4 turn.1
  8.8 2.2 %collective-permute-start.8 = (bf16[1024,256]{1,0:T(8,128)(2,1)S(1)}, bf16[1024,256]{1,0:T(8,128)(2,1)S(1)}, u32[]{:S(2)}, u32[]{:S(2)}) collective-permute-start(bf16[1024,256]{1,0:T(8,128)(2,1)S(1)} %get-tuple-element.27), channel_id=1, source_target_pairs={{0,17},{1,16},{2,19},{3,18},{4,21},{5,20},{6,23},{7,22},{8,25},{9,... | collective-permute-start | bytes 1572872 | tf_op jit(solution)/shard_map/ppermute | solution.py:269
  11.0 0.6 %collective-permute-done.1.head.refs_2_ = bf16[144,256]{1,0:T(8,128)(2,1)S(1)} collective-permute-done((bf16[144,256]{1,0:T(8,128)(2,1)S(1)}, bf16[144,256]{1,0:T(8,128)(2,1)S(1)}, u32[]{:S(2)}, u32[]{:S(2)}) %collective-permute-start.1) | collective-permute-done | bytes 73760 | tf_op jit(solution)/shard_map/ppermute | solution.py:269
  11.6 0.0 collective-permute-done.theirs
  11.6 0.0 copy-done.5
  11.6 0.0 copy-done.7
  11.6 1.1 %ocean.1 = (f32[128,512]{1,0:T(8,128)S(1)}, bf16[128,512]{1,0:T(8,128)(2,1)S(1)}, bf16[2,128,256]{2,1,0:T(8,128)(2,1)S(1)}, bf16[2,128,256]{2,1,0:T(8,128)(2,1)S(1)}) custom-call(bf16[128,512]{1,0:T(8,128)(2,1)S(1)} %copy-done.5, bf16[128,512]{1,0:T(8,128)(2,1)S(1)} %collective-permute-done.theirs, ...), custom_call_target="tpu_custom_call", output_to_operand_aliasing={{3}: (8, {})} | custom-call | flops 8000000000 | tf_op jit(solution)/shard_map/ocean/pallas_call | solution.py:35
  12.7 0.6 %collective-permute-start.2 = (bf16[128,512]{1,0:T(8,128)(2,1)S(1)}, bf16[128,512]{1,0:T(8,128)(2,1)S(1)}, u32[]{:S(2)}, u32[]{:S(2)}) collective-permute-start(bf16[128,512]{1,0:T(8,128)(2,1)S(1)} %get-tuple-element.25), channel_id=1, source_target_pairs={{0,1},{1,0},{2,3},{3,2},{4,5},{5,4},{6,7},{7,6},{8,9},{9,8},{10,11... | collective-permute-start | bytes 393224 | tf_op jit(solution)/shard_map/ppermute | solution.py:269
  13.3 5.5 %collective-permute-start.10 = (bf16[2,128,256]{2,1,0:T(8,128)(2,1)S(1)}, bf16[2,128,256]{2,1,0:T(8,128)(2,1)S(1)}, u32[]{:S(2)}, u32[]{:S(2)}) collective-permute-start(bf16[2,128,256]{2,1,0:T(8,128)(2,1)S(1)} %get-tuple-element.29), channel_id=1, source_target_pairs={{1,3},{2,4},{3,1},{4,2},{5,7},{6,8},{7,5},{8,6},{9,11},{10,12},{11... | collective-permute-start | bytes 393224 | tf_op jit(solution)/shard_map/ppermute | solution.py:269
  18.8 0.1 collective-permute-start.11
  19.5 3.2 %collective-permute-done.2.got = bf16[128,512]{1,0:T(8,128)(2,1)S(1)} collective-permute-done((bf16[128,512]{1,0:T(8,128)(2,1)S(1)}, bf16[128,512]{1,0:T(8,128)(2,1)S(1)}, u32[]{:S(2)}, u32[]{:S(2)}) %collective-permute-start.2) | collective-permute-done | bytes 131104 | tf_op jit(solution)/shard_map/ppermute | solution.py:269
  22.8 0.7 %result.1 = (bf16[128,512]{1,0:T(8,128)(2,1)}, bf16[4,128,128]{2,1,0:T(8,128)(2,1)S(1)}) custom-call(s32[1]{0:T(128)S(6)} %copy.16.count, bf16[128,512]{1,0:T(8,128)(2,1)S(1)} %copy-done.5, f32[128,512]{1,0:T(8,128)S(1)} %get-tuple-element.24.kept, bf16[128,512]{1,0:T(8,128)(2,1)S(1)} %collective-permute-done.2.got), custom_call_target="tpu_custom_call" | custom-call | tf_op jit(solution)/shard_map/result/pallas_call | solution.py:35
  23.5 8.3 %collective-permute-start.4 = (bf16[4,128,128]{2,1,0:T(8,128)(2,1)S(1)}, bf16[4,128,128]{2,1,0:T(8,128)(2,1)S(1)}, u32[]{:S(2)}, u32[]{:S(2)}) collective-permute-start(bf16[4,128,128]{2,1,0:T(8,128)(2,1)S(1)} %get-tuple-element.26.own), channel_id=1, source_target_pairs={{4,8},{5,9},{6,10},{7,11},{8,4},{9,5},{10,6},{11,7},{12,16},{13,17... | collective-permute-start | bytes 393224 | tf_op jit(solution)/shard_map/ppermute | solution.py:269
  31.8 0.0 collective-permute-done.10.refs_2_.refs_1_
  31.8 0.1 collective-permute-start.5
  31.9 0.0 collective-permute-done.11.refs_3_
  31.9 0.0 collective-permute-done.9.refs_1_.refs_4_
  31.9 0.0 collective-permute-done.8.got_w
  31.9 2.7 %mix.2 = (bf16[4,128,256]{2,1,0:T(8,128)(2,1)S(1)}, bf16[4,128,256]{2,1,0:T(8,128)(2,1)S(1)}) custom-call(f32[16,128]{1,0:T(8,128)S(1)} %get-tuple-element.19.own_p, bf16[144,256]{1,0:T(8,128)(2,1)S(1)} %collective-permute-done.1.head.refs_2_, bf16[1024,256]{1,0:T(8,128)(2,1)S(1)} %get-tuple-element.22.before.own_w, ...), custom_call_target="tpu_custom_call" | custom-call | flops 30000001024 | tf_op jit(solution)/shard_map/mix/pallas_call | solution.py:35
  34.6 0.0 copy-start
  34.6 0.0 copy-start.6
  34.7 0.2 collective-permute-start.12
  34.9 2.7 %mix.3 = (bf16[4,128,256]{2,1,0:T(8,128)(2,1)S(1)}, bf16[4,128,256]{2,1,0:T(8,128)(2,1)S(1)}) custom-call(f32[16,128]{1,0:T(8,128)S(1)} %get-tuple-element.19.own_p, bf16[144,256]{1,0:T(8,128)(2,1)S(1)} %collective-permute-done.1.head.refs_2_, bf16[1024,256]{1,0:T(8,128)(2,1)S(1)} %get-tuple-element.22.before.own_w, ...), custom_call_target="tpu_custom_call" | custom-call | tf_op jit(solution)/shard_map/mix/pallas_call | solution.py:35
  37.6 1.9 %collective-permute-start.13 = (bf16[4,128,256]{2,1,0:T(8,128)(2,1)S(1)}, bf16[4,128,256]{2,1,0:T(8,128)(2,1)S(1)}, u32[]{:S(2)}, u32[]{:S(2)}) collective-permute-start(bf16[4,128,256]{2,1,0:T(8,128)(2,1)S(1)} %get-tuple-element.34), channel_id=1, source_target_pairs={{0,1},{1,0},{2,3},{3,2},{4,5},{5,4},{6,7},{7,6},{8,9},{9,8},{10,11... | collective-permute-start | bytes 786440 | tf_op jit(solution)/shard_map/ppermute | solution.py:269
  39.6 0.0 collective-permute-start.3
  39.6 0.0 collective-permute-done.4.e1
  39.6 0.5 %collective-permute-start.6 = (bf16[4,128,128]{2,1,0:T(8,128)(2,1)S(1)}, bf16[4,128,128]{2,1,0:T(8,128)(2,1)S(1)}, u32[]{:S(2)}, u32[]{:S(2)}) collective-permute-start(bf16[4,128,128]{2,1,0:T(8,128)(2,1)S(1)} %collective-permute-done.4.e1), channel_id=1, source_target_pairs={{0,2},{1,3},{2,0},{3,1},{4,6},{5,7},{6,4},{7,5},{8,10},{9,11},{10,... | collective-permute-start | bytes 393224 | tf_op jit(solution)/shard_map/ppermute | solution.py:269
  40.1 0.0 collective-permute-done.5.e2
  40.1 0.1 collective-permute-start.7
  40.2 0.7 %collective-permute-done.3.swap = bf16[4,128,128]{2,1,0:T(8,128)(2,1)S(1)} collective-permute-done((bf16[4,128,128]{2,1,0:T(8,128)(2,1)S(1)}, bf16[4,128,128]{2,1,0:T(8,128)(2,1)S(1)}, u32[]{:S(2)}, u32[]{:S(2)}) %collective-permute-start.3) | collective-permute-done | bytes 131104 | tf_op jit(solution)/shard_map/ppermute | solution.py:269
  40.9 0.2 collective-permute-done.6.swap_e1
  41.1 0.3 collective-permute-done.7.swap_e2
  41.4 1.8 %collective-permute-done.12.later.rest_2_ = bf16[4,128,256]{2,1,0:T(8,128)(2,1)S(1)} collective-permute-done((bf16[4,128,256]{2,1,0:T(8,128)(2,1)S(1)}, bf16[4,128,256]{2,1,0:T(8,128)(2,1)S(1)}, u32[]{:S(2)}, u32[]{:S(2)}) %collective-permute-start.12) | collective-permute-done | bytes 262176 | tf_op jit(solution)/shard_map/ppermute | solution.py:269
  43.3 0.0 copy-done
  43.3 1.9 %regrid.1 = bf16[16,128,256]{2,1,0:T(8,128)(2,1)S(1)} custom-call(s32[2,32]{1,0:T(2,128)S(1)} %bitcast.1, bf16[4,128,128]{2,1,0:T(8,128)(2,1)S(1)} %get-tuple-element.26.own, bf16[4,128,128]{2,1,0:T(8,128)(2,1)S(1)} %collective-permute-done.3.swap, bf16[4,128,128]{2,1,0:T(8,128)(2,1)S(1)} %collective-permute-done.4.e1, ...), custom_call_target="tpu_custom_call" | custom-call | tf_op jit(solution)/shard_map/regrid/pallas_call | solution.py:35
  45.2 0.9 %collective-permute-done.13.rest_3_ = bf16[4,128,256]{2,1,0:T(8,128)(2,1)S(1)} collective-permute-done((bf16[4,128,256]{2,1,0:T(8,128)(2,1)S(1)}, bf16[4,128,256]{2,1,0:T(8,128)(2,1)S(1)}, u32[]{:S(2)}, u32[]{:S(2)}) %collective-permute-start.13) | collective-permute-done | bytes 262176 | tf_op jit(solution)/shard_map/ppermute | solution.py:269
  46.1 2.0 %final.1 = bf16[128,16,256]{2,1,0:T(8,128)(2,1)} custom-call(bf16[128,16,256]{2,1,0:T(8,128)(2,1)S(1)} %copy-done.2, bf16[16,128,256]{2,1,0:T(8,128)(2,1)S(1)} %regrid.1, bf16[4,128,256]{2,1,0:T(8,128)(2,1)S(1)} %get-tuple-element.32.rest_0_, bf16[4,128,256]{2,1,0:T(8,128)(2,1)S(1)} %get-tuple-element.33.rest_1_, ...), custom_call_target="tpu_custom_call" | custom-call | tf_op jit(solution)/shard_map/final/pallas_call | solution.py:35
  (12 shorter events, 0.0 us)
Async XLA Ops:
  0.6 11.0 %collective-permute-start = (bf16[128,512]{1,0:T(8,128)(2,1)}, bf16[128,512]{1,0:T(8,128)(2,1)S(1)}, u32[]{:S(2)}, u32[]{:S(2)}) collective-permute-start(bf16[128,512]{1,0:T(8,128)(2,1)} %state.2), channel_id=1, source_target_pairs={{0,1},{1,0},{2,3},{3,2},{4,5},{5,4},{6,7},{7,6},{8,9},{9,8},{10,11... | collective-permute-start | bytes 393224 | tf_op jit(solution)/shard_map/ppermute | solution.py:269
  2.2 1.2 %copy-start.1 = (bf16[128,16,256]{2,1,0:T(8,128)(2,1)S(1)}, bf16[128,16,256]{2,1,0:T(8,128)(2,1)}, u32[]{:S(2)}) copy-start(bf16[128,16,256]{2,1,0:T(8,128)(2,1)} %state.3) | copy-start | bytes 3145732
  3.4 0.7 %copy-start.9 = (f32[9,128]{1,0:T(8,128)S(1)}, f32[9,128]{1,0:T(8,128)}, u32[]{:S(2)}) copy-start(f32[9,128]{1,0:T(8,128)} %taps_in.1) | copy-start | bytes 13828
  4.1 0.7 %copy-start.10 = (bf16[128]{0:T(256)(128)(2,1)S(1)}, bf16[128]{0:T(256)(128)(2,1)}, u32[]{:S(2)}) copy-start(bf16[128]{0:T(256)(128)(2,1)} %atm_gain_in.1) | copy-start | bytes 772
  4.8 0.7 %copy-start.11 = (bf16[128]{0:T(256)(128)(2,1)S(1)}, bf16[128]{0:T(256)(128)(2,1)}, u32[]{:S(2)}) copy-start(bf16[128]{0:T(256)(128)(2,1)} %ocean_gain_in.1) | copy-start | bytes 772
  5.4 3.0 %copy-start.3 = (bf16[256,512]{1,0:T(8,128)(2,1)S(1)}, bf16[256,512]{1,0:T(8,128)(2,1)}, u32[]{:S(2)}) copy-start(bf16[256,512]{1,0:T(8,128)(2,1)} %up_in.2) | copy-start | bytes 786436
  5.4 3.0 %copy-start.4 = (bf16[512,256]{1,0:T(8,128)(2,1)S(1)}, bf16[512,256]{1,0:T(8,128)(2,1)}, u32[]{:S(2)}) copy-start(bf16[512,256]{1,0:T(8,128)(2,1)} %down_in.2) | copy-start | bytes 786436
  5.4 6.2 %copy-start.5 = (bf16[128,512]{1,0:T(8,128)(2,1)S(1)}, bf16[128,512]{1,0:T(8,128)(2,1)}, u32[]{:S(2)}) copy-start(bf16[128,512]{1,0:T(8,128)(2,1)} %state.2) | copy-start | bytes 393220
  5.4 6.2 %copy-start.7 = (bf16[256,512]{1,0:T(8,128)(2,1)S(1)}, bf16[256,512]{1,0:T(8,128)(2,1)}, u32[]{:S(2)}) copy-start(bf16[256,512]{1,0:T(8,128)(2,1)} %up_in.3) | copy-start | bytes 786436
  5.4 6.2 %copy-start.8 = (bf16[512,256]{1,0:T(8,128)(2,1)S(1)}, bf16[512,256]{1,0:T(8,128)(2,1)}, u32[]{:S(2)}) copy-start(bf16[512,256]{1,0:T(8,128)(2,1)} %down_in.3) | copy-start | bytes 786436
  6.3 5.3 %collective-permute-start.1 = (bf16[144,256]{1,0:T(8,128)(2,1)S(1)}, bf16[144,256]{1,0:T(8,128)(2,1)S(1)}, u32[]{:S(2)}, u32[]{:S(2)}) collective-permute-start(bf16[144,256]{1,0:T(8,128)(2,1)S(1)} %get-tuple-element.20), channel_id=1, source_target_pairs={{0,1},{1,0},{2,3},{3,2},{4,5},{5,4},{6,7},{7,6},{8,9},{9,8},{10,11... | collective-permute-start | bytes 221192 | tf_op jit(solution)/shard_map/ppermute | solution.py:269
  6.9 25.0 %collective-permute-start.9 = (bf16[6,128,256]{2,1,0:T(8,128)(2,1)S(1)}, bf16[6,128,256]{2,1,0:T(8,128)(2,1)S(1)}, u32[]{:S(2)}, u32[]{:S(2)}) collective-permute-start(bf16[6,128,256]{2,1,0:T(8,128)(2,1)S(1)} %get-tuple-element.28), channel_id=1, source_target_pairs={{0,1},{1,0},{2,3},{3,2},{4,5},{5,4},{6,7},{7,6},{8,9},{9,8},{10,11... | collective-permute-start | bytes 1179656 | tf_op jit(solution)/shard_map/ppermute | solution.py:269
  8.8 23.1 %collective-permute-start.8 = (bf16[1024,256]{1,0:T(8,128)(2,1)S(1)}, bf16[1024,256]{1,0:T(8,128)(2,1)S(1)}, u32[]{:S(2)}, u32[]{:S(2)}) collective-permute-start(bf16[1024,256]{1,0:T(8,128)(2,1)S(1)} %get-tuple-element.27), channel_id=1, source_target_pairs={{0,17},{1,16},{2,19},{3,18},{4,21},{5,20},{6,23},{7,22},{8,25},{9,... | collective-permute-start | bytes 1572872 | tf_op jit(solution)/shard_map/ppermute | solution.py:269
  12.7 10.1 %collective-permute-start.2 = (bf16[128,512]{1,0:T(8,128)(2,1)S(1)}, bf16[128,512]{1,0:T(8,128)(2,1)S(1)}, u32[]{:S(2)}, u32[]{:S(2)}) collective-permute-start(bf16[128,512]{1,0:T(8,128)(2,1)S(1)} %get-tuple-element.25), channel_id=1, source_target_pairs={{0,1},{1,0},{2,3},{3,2},{4,5},{5,4},{6,7},{7,6},{8,9},{9,8},{10,11... | collective-permute-start | bytes 393224 | tf_op jit(solution)/shard_map/ppermute | solution.py:269
  13.3 18.5 %collective-permute-start.10 = (bf16[2,128,256]{2,1,0:T(8,128)(2,1)S(1)}, bf16[2,128,256]{2,1,0:T(8,128)(2,1)S(1)}, u32[]{:S(2)}, u32[]{:S(2)}) collective-permute-start(bf16[2,128,256]{2,1,0:T(8,128)(2,1)S(1)} %get-tuple-element.29), channel_id=1, source_target_pairs={{1,3},{2,4},{3,1},{4,2},{5,7},{6,8},{7,5},{8,6},{9,11},{10,12},{11... | collective-permute-start | bytes 393224 | tf_op jit(solution)/shard_map/ppermute | solution.py:269
  18.8 13.1 %collective-permute-start.11 = (bf16[2,128,256]{2,1,0:T(8,128)(2,1)S(1)}, bf16[2,128,256]{2,1,0:T(8,128)(2,1)S(1)}, u32[]{:S(2)}, u32[]{:S(2)}) collective-permute-start(bf16[2,128,256]{2,1,0:T(8,128)(2,1)S(1)} %get-tuple-element.30), channel_id=1, source_target_pairs={{0,1},{1,0},{2,3},{3,2},{4,5},{5,4},{6,7},{7,6},{8,9},{9,8},{10,11... | collective-permute-start | bytes 393224 | tf_op jit(solution)/shard_map/ppermute | solution.py:269
  23.5 16.1 %collective-permute-start.4 = (bf16[4,128,128]{2,1,0:T(8,128)(2,1)S(1)}, bf16[4,128,128]{2,1,0:T(8,128)(2,1)S(1)}, u32[]{:S(2)}, u32[]{:S(2)}) collective-permute-start(bf16[4,128,128]{2,1,0:T(8,128)(2,1)S(1)} %get-tuple-element.26.own), channel_id=1, source_target_pairs={{4,8},{5,9},{6,10},{7,11},{8,4},{9,5},{10,6},{11,7},{12,16},{13,17... | collective-permute-start | bytes 393224 | tf_op jit(solution)/shard_map/ppermute | solution.py:269
  31.8 8.3 %collective-permute-start.5 = (bf16[4,128,128]{2,1,0:T(8,128)(2,1)S(1)}, bf16[4,128,128]{2,1,0:T(8,128)(2,1)S(1)}, u32[]{:S(2)}, u32[]{:S(2)}) collective-permute-start(bf16[4,128,128]{2,1,0:T(8,128)(2,1)S(1)} %get-tuple-element.26.own), channel_id=1, source_target_pairs={{0,4},{1,5},{2,6},{3,7},{4,0},{5,1},{6,2},{7,3},{8,12},{9,13},{10,... | collective-permute-start | bytes 393224 | tf_op jit(solution)/shard_map/ppermute | solution.py:269
  34.6 8.7 %copy-start = (bf16[32,2,128,128]{3,2,1,0:T(8,128)(2,1)S(1)}, bf16[32,2,128,128]{3,2,1,0:T(8,128)(2,1)}, u32[]{:S(2)}) copy-start(bf16[32,2,128,128]{3,2,1,0:T(8,128)(2,1)} %w.1) | copy-start | bytes 6291460
  34.6 8.7 %copy-start.6 = (s32[32,2]{0,1:T(2,128)S(1)}, s32[32,2]{0,1:T(2,128)}, u32[]{:S(2)}) copy-start(s32[32,2]{0,1:T(2,128)} %param.15) | copy-start | bytes 772
  34.7 8.6 %collective-permute-start.12 = (bf16[4,128,256]{2,1,0:T(8,128)(2,1)S(1)}, bf16[4,128,256]{2,1,0:T(8,128)(2,1)S(1)}, u32[]{:S(2)}, u32[]{:S(2)}) collective-permute-start(bf16[4,128,256]{2,1,0:T(8,128)(2,1)S(1)} %get-tuple-element.31), channel_id=1, source_target_pairs={{0,1},{1,0},{2,3},{3,2},{4,5},{5,4},{6,7},{7,6},{8,9},{9,8},{10,11... | collective-permute-start | bytes 786440 | tf_op jit(solution)/shard_map/ppermute | solution.py:269
  37.6 8.5 %collective-permute-start.13 = (bf16[4,128,256]{2,1,0:T(8,128)(2,1)S(1)}, bf16[4,128,256]{2,1,0:T(8,128)(2,1)S(1)}, u32[]{:S(2)}, u32[]{:S(2)}) collective-permute-start(bf16[4,128,256]{2,1,0:T(8,128)(2,1)S(1)} %get-tuple-element.34), channel_id=1, source_target_pairs={{0,1},{1,0},{2,3},{3,2},{4,5},{5,4},{6,7},{7,6},{8,9},{9,8},{10,11... | collective-permute-start | bytes 786440 | tf_op jit(solution)/shard_map/ppermute | solution.py:269
  39.6 1.3 %collective-permute-start.3 = (bf16[4,128,128]{2,1,0:T(8,128)(2,1)S(1)}, bf16[4,128,128]{2,1,0:T(8,128)(2,1)S(1)}, u32[]{:S(2)}, u32[]{:S(2)}) collective-permute-start(bf16[4,128,128]{2,1,0:T(8,128)(2,1)S(1)} %get-tuple-element.26.own), channel_id=1, source_target_pairs={{0,2},{1,3},{2,0},{3,1},{4,6},{5,7},{6,4},{7,5},{8,10},{9,11},{10,... | collective-permute-start | bytes 393224 | tf_op jit(solution)/shard_map/ppermute | solution.py:269
  39.6 1.5 %collective-permute-start.6 = (bf16[4,128,128]{2,1,0:T(8,128)(2,1)S(1)}, bf16[4,128,128]{2,1,0:T(8,128)(2,1)S(1)}, u32[]{:S(2)}, u32[]{:S(2)}) collective-permute-start(bf16[4,128,128]{2,1,0:T(8,128)(2,1)S(1)} %collective-permute-done.4.e1), channel_id=1, source_target_pairs={{0,2},{1,3},{2,0},{3,1},{4,6},{5,7},{6,4},{7,5},{8,10},{9,11},{10,... | collective-permute-start | bytes 393224 | tf_op jit(solution)/shard_map/ppermute | solution.py:269
  40.1 1.3 %collective-permute-start.7 = (bf16[4,128,128]{2,1,0:T(8,128)(2,1)S(1)}, bf16[4,128,128]{2,1,0:T(8,128)(2,1)S(1)}, u32[]{:S(2)}, u32[]{:S(2)}) collective-permute-start(bf16[4,128,128]{2,1,0:T(8,128)(2,1)S(1)} %collective-permute-done.5.e2), channel_id=1, source_target_pairs={{0,2},{1,3},{2,0},{3,1},{4,6},{5,7},{6,4},{7,5},{8,10},{9,11},{10,... | collective-permute-start | bytes 393224 | tf_op jit(solution)/shard_map/ppermute | solution.py:269
  43.3 2.8 %copy-start.2 = (bf16[128,16,256]{2,1,0:T(8,128)(2,1)S(1)}, bf16[128,16,256]{2,1,0:T(8,128)(2,1)}, u32[]{:S(2)}) copy-start(bf16[128,16,256]{2,1,0:T(8,128)(2,1)} %state.3) | copy-start | bytes 3145732
